TPU v7x, 128 devices: a whole 4x4x4 slice. The times are simulated.
128 devices in a mesh: tv: 16 (over z, x_hi, core), sv: 8 (over x_lo, y).
Axes of the slice: x: 4 (x_hi: 2, x_lo: 2; x = x_hi * 2 + x_lo), y: 4, z: 4, core: 2. Of those that a mesh axis runs over, the one named last changes fastest.
Arguments:
- teacher_hidden: bfloat16 [1024, 4096], P('tv', 'sv'), may hold values from -250 to 250
- student_hidden: bfloat16 [1024, 5120], P('sv', 'tv'), may hold values from -250 to 250
- teacher_head: bfloat16 [4096, 151936], P('sv', 'tv'), may hold values from -0.09375 to 0.09375
- student_head: bfloat16 [5120, 151936], P('tv', 'sv'), may hold values from -0.078125 to 0.078125
- token_ids: int32 [1024], P('tv'), may hold values from 0 to 151935
Outputs:
- rewards: float32 [1024], P('tv')
- kl_div: float32 [1024], P('tv')
- logit_grad: bfloat16 [1024, 151936], P('tv', 'sv')
All inputs are finite; a program needn't handle non-finite values.
Results may differ from a plain program's by a relative error of at most 0.0042.
Values may be sent and summed in bfloat16 or wider, within the bound.
No kernel may reach another device: no remote copies, remote signals or barrier semaphores. Data moves between devices by JAX's collectives and lax.ppermute only.
A program may use at most 320 MiB of HBM per device.

v0:
```python
import jax
import jax.numpy as jnp
from jax import lax
from jax.sharding import PartitionSpec as P


def joined(array, axis, combine):
    everything = jax.tree.map(lambda part: lax.all_gather(part, axis), array)
    leading = jax.tree.map(lambda part: part[0], everything)

    def turn(k, so_far):
        return combine(so_far, jax.tree.map(lambda part: part[k], everything))

    return lax.fori_loop(1, lax.axis_size(axis), turn, leading)


def join_pair(first, second):
    peak_new = jnp.maximum(first[0], second[0])
    return (
        peak_new,
        first[1] * jnp.exp(first[0] - peak_new) + second[1] * jnp.exp(second[0] - peak_new),
    )


def join_four(first, second):
    return join_pair(first[:2], second[:2]) + join_pair(first[2:], second[2:])


def row_mass(values):
    peak_row = jnp.max(values, axis=1)
    return (peak_row, jnp.sum(jnp.exp(values - peak_row[:, None]), axis=1))


def shards(teacher_hidden, student_hidden, teacher_head, student_head, token_ids):
    tv_count = lax.axis_size("tv")
    sv_count = lax.axis_size("sv")
    teacher_rows = lax.all_gather(teacher_hidden, "tv", axis=0, tiled=True)
    all_tokens = teacher_rows.shape[0]
    inner_rows = all_tokens // (tv_count * sv_count)
    feature_width = teacher_rows.shape[1]
    reordered = teacher_rows.reshape(tv_count, sv_count, inner_rows, feature_width)
    reordered = reordered.transpose(1, 0, 2, 3).reshape(all_tokens, feature_width)
    block_rows = reordered
    teacher_logit = lax.psum_scatter(
        jnp.dot(block_rows, teacher_head, preferred_element_type=jnp.float32),
        "sv",
        scatter_dimension=0,
        tiled=True,
    ).astype(jnp.bfloat16)
    teacher_base = lax.all_to_all(
        lax.all_to_all(teacher_logit, "tv", split_axis=0, concat_axis=1, tiled=True),
        "sv",
        split_axis=1,
        concat_axis=0,
        tiled=True,
    ).astype(jnp.float32)
    student_rows = lax.all_gather(student_hidden, "sv", axis=0, tiled=True)
    block_rows = student_rows
    student_logit = lax.psum_scatter(
        jnp.dot(block_rows, student_head, preferred_element_type=jnp.float32),
        "tv",
        scatter_dimension=0,
        tiled=True,
    )
    col_width = student_logit.shape[1]
    vocab_ids = lax.axis_index("sv") * col_width + lax.broadcasted_iota(
        jnp.int32, student_logit.shape, 1
    )
    logit_gap = student_logit - teacher_base
    picked = jnp.sum(jnp.where(vocab_ids == token_ids[:, None], -logit_gap, 0.0), axis=1)
    peak_student, mass_student = row_mass(student_logit)
    peak_teacher, mass_teacher = row_mass(teacher_base)
    peak_student, mass_student, peak_teacher, mass_teacher = joined(
        (peak_student, mass_student, peak_teacher, mass_teacher), "sv", join_four
    )
    student_norm = peak_student + jnp.log(mass_student)
    teacher_norm = peak_teacher + jnp.log(mass_teacher)
    student_prob = jnp.exp(student_logit - student_norm[:, None])
    kl_part = jnp.sum(student_prob * logit_gap, axis=1)
    kl_total, picked = lax.psum((kl_part, picked), "sv")
    kl_div = kl_total - student_norm + teacher_norm
    rewards = picked + student_norm - teacher_norm
    shift_rows = student_norm - teacher_norm + kl_div
    logit_grad = (student_prob * (logit_gap - shift_rows[:, None])).astype(jnp.bfloat16)
    return (rewards, kl_div, logit_grad)


def solution(mesh):
    in_specs = (P("tv", "sv"), P("sv", "tv"), P("sv", "tv"), P("tv", "sv"), P("tv"))
    out_specs = (P("tv"), P("tv"), P("tv", "sv"))
    return jax.shard_map(shards, mesh=mesh, in_specs=in_specs, out_specs=out_specs, check_vma=False)
```

profile of v0, /device:TPU:6, one launch (start us, length us, event | category | flops | bytes accessed | tf_op | source)
XLA Modules:
  0.0 1099.0 jit_solution(6927053905682309133)
XLA Ops:
  7.2 0.0 all-gather.6.cloned.1.call-start
  7.2 0.7 all-gather.6.cloned.1.call-update
  7.9 0.0 reduce-scatter.5.cloned.1.call-start
  7.9 48.2 %all-gather.6.cloned.1.call-done = bf16[1024,512]{1,0:T(8,128)(2,1)} async-done(((bf16[64,512]{1,0:T(8,128)(2,1)}), bf16[1024,512]{1,0:T(8,128)(2,1)}) %all-gather.6.cloned.1.call-update) | async-done | bytes 1048592 | tf_op jit(solution)/shard_map/all_gather | solution.py:37
  56.2 1.3 copy.17
  57.5 19.7 %fusion.16 = f32[1024,9496]{0,1:T(8,128)} fusion(bf16[1024,512]{1,0:T(8,128)(2,1)S(1)} %bitcast.68, bf16[512,9496]{0,1:T(8,128)(2,1)} %param.9), kind=kOutput, calls=%fused_computation.34 | convolution fusion | flops 9957277696 | bytes 49668096 | tf_op jit(solution)/shard_map/dot_general | solution.py:45
  77.3 0.0 copy-start
  77.3 0.0 reduce-scatter.5.cloned.1.call-update
  77.3 0.0 reduce-scatter.3.cloned.1.call-start
  77.3 0.8 copy-done
  78.1 30.3 %all_gather.28 = bf16[1024,320]{0,1:T(8,128)(2,1)S(1)} all-gather(bf16[128,320]{0,1:T(8,128)(2,1)S(1)} %copy-done), channel_id=1, replica_groups=mesh['tv'=16,'sv'=8] {'sv'}, dimensions={0}, use_global_device_ids=true | all-gather | bytes 737280 | tf_op jit(solution)/shard_map/all_gather | solution.py:57
  108.5 34.6 %fusion.15 = f32[1024,18992]{1,0:T(8,128)} fusion(bf16[1024,320]{0,1:T(8,128)(2,1)S(1)} %all_gather.28, bf16[320,18992]{1,0:T(8,128)(2,1)} %param.10), kind=kOutput, calls=%fused_computation.33 | convolution fusion | flops 12446597120 | bytes 90601472 | tf_op jit(solution)/shard_map/dot_general | solution.py:60
  143.1 0.0 reduce-scatter.3.cloned.1.call-update
  143.1 386.1 %reduce-scatter.5.cloned.1.call-done = f32[128,9496]{0,1:T(8,128)} async-done(((f32[1024,9496]{0,1:T(8,128)}), f32[128,9496]{0,1:T(8,128)}) %reduce-scatter.5.cloned.1.call-update) | async-done | bytes 4861968 | tf_op jit(solution)/shard_map/reduce_scatter | solution.py:44
  529.2 2.6 convert_element_type.15
  531.8 3.6 copy.18
  535.3 44.3 %all_to_all.32 = bf16[16,8,9496]{2,1,0:T(8,128)(2,1)S(1)} all-to-all(bf16[16,8,9496]{2,1,0:T(8,128)(2,1)} %bitcast.65), channel_id=1, replica_groups=mesh['tv'=16,'sv'=8] {'tv'}, dimensions={0} | all-to-all | bytes 4861952 | tf_op jit(solution)/shard_map/all_to_all | solution.py:51
  579.6 1.8 copy.19
  581.4 4.0 all_to_all.27
  585.4 0.0 copy-start.2
  585.4 1.7 copy.20
  587.1 3.6 all-to-all-start.1
  590.7 0.0 copy-done.2
  590.8 0.6 dynamic-slice
  592.0 27.8 %all-to-all-done.1 = bf16[8,8,18992]{2,0,1:T(8,128)(2,1)S(1)} async-done(((bf16[8,8,18992]{2,0,1:T(8,128)(2,1)}), bf16[8,8,18992]{2,0,1:T(8,128)(2,1)S(1)}, u32[]{:S(2)}, u32[]{:S(2)}) %all-to-all-start.1) | async-done | bytes 2431008 | tf_op jit(solution)/shard_map/all_to_all | solution.py:50
  619.9 0.5 bitcast_reduce_fusion
  620.4 0.1 copy.26
  620.4 0.1 copy.22
  620.5 0.1 reshape.67
  620.6 1.0 fusion.12
  621.6 0.1 reshape.69
  621.7 16.9 %all-gather.3 = f32[8,1,64]{2,1,0:T(1,128)S(1)} all-gather(f32[1,1,64]{2,1,0:T(1,128)S(1)} %reshape.69), channel_id=1, replica_groups=mesh['tv'=16,'sv'=8] {'sv'}, dimensions={0}, use_global_device_ids=true | all-gather | bytes 2304 | tf_op jit(solution)/shard_map/all_gather | solution.py:8
  638.5 15.3 %all-gather.2 = f32[8,1,64]{2,1,0:T(1,128)S(1)} all-gather(f32[1,1,64]{2,1,0:T(1,128)S(1)} %reshape.67), channel_id=1, replica_groups=mesh['tv'=16,'sv'=8] {'sv'}, dimensions={0}, use_global_device_ids=true | all-gather | bytes 2304 | tf_op jit(solution)/shard_map/all_gather | solution.py:8
  653.8 0.0 copy-start.1
  653.8 387.0 %reduce-scatter.3.cloned.1.call-done = f32[64,18992]{1,0:T(8,128)} async-done(((f32[1024,18992]{1,0:T(8,128)}), f32[64,18992]{1,0:T(8,128)}) %reduce-scatter.3.cloned.1.call-update) | async-done | bytes 4861968 | tf_op jit(solution)/shard_map/reduce_scatter | solution.py:59
  1040.8 2.7 reduce_max.27
  1043.6 0.2 dynamic-update-slice
  1043.8 3.2 exponential_reduce_fusion
  1047.0 0.2 dynamic-update-slice.1
  1047.2 18.9 %all-reduce.3 = (f32[512]{0:T(512)S(1)}, f32[512]{0:T(512)S(1)}) all-reduce(f32[512]{0:T(512)S(1)} %dynamic-update-slice, f32[512]{0:T(512)S(1)} %dynamic-update-slice.1), channel_id=2, replica_groups=mesh['tv'=16,'sv'=8] {'sv'}, use_global_device_ids=true, to_apply=%add | all-reduce | flops 1024 | bytes 8192
  1066.2 0.1 reshape.55
  1066.2 0.1 reshape.56
  1066.3 0.3 while.21
  1066.7 0.0 copy-done.1
  1066.7 4.3 multiply_reduce_fusion
  1070.9 16.0 %all-reduce.2 = (f32[64]{0:T(128)S(1)}, f32[64]{0:T(128)S(1)}) all-reduce(f32[64]{0:T(128)S(1)} %get-tuple-element.231, f32[64]{0:T(128)S(1)} %get-tuple-element.230), channel_id=1, replica_groups=mesh['tv'=16,'sv'=8] {'sv'}, use_global_device_ids=true, to_apply=%region_3.4 | all-reduce | flops 128 | bytes 1024 | tf_op jit(solution)/shard_map/psum | solution.py:80
  1086.9 0.5 subtract_add_fusion
  1087.4 5.0 multiply_convert_fusion
  (15 shorter events, 0.2 us)
Async XLA Ops:
  7.2 49.0 %all-gather.6.cloned.1.call-start = ((), (), s32[]{:S(2)}) async-start(), calls=%async_computation.5 | async-start | bytes 1114112 | tf_op jit(solution)/shard_map/all_gather | solution.py:37
  7.9 521.3 %reduce-scatter.5.cloned.1.call-start = ((), (), s32[]{:S(2)}) async-start(), calls=%async_computation.6 | async-start | bytes 43757568 | tf_op jit(solution)/shard_map/reduce_scatter | solution.py:44
  77.3 0.9 copy-start
  77.3 963.6 %reduce-scatter.3.cloned.1.call-start = ((), (), s32[]{:S(2)}) async-start(), calls=%async_computation.4 | async-start | bytes 83001344 | tf_op jit(solution)/shard_map/reduce_scatter | solution.py:59
  585.4 5.3 copy-start.2
  587.1 32.8 %all-to-all-start.1 = ((bf16[8,8,18992]{2,0,1:T(8,128)(2,1)}), bf16[8,8,18992]{2,0,1:T(8,128)(2,1)S(1)}, u32[]{:S(2)}, u32[]{:S(2)}) async-start(bf16[8,8,18992]{2,0,1:T(8,128)(2,1)} %copy.20), calls=%async_computation.3 | async-start | bytes 4882432 | tf_op jit(solution)/shard_map/all_to_all | solution.py:50
  653.8 412.8 %copy-start.1 = (s32[64]{0:T(128)S(1)}, s32[64]{0:T(128)}, u32[]{:S(2)}) copy-start(s32[64]{0:T(128)} %param.11) | copy-start | bytes 772
Sparse Core Ops, SparseCore 0:
  10.5 45.6 all-gather.5
  77.4 451.7 reduce-scatter.4
  533.7 507.0 reduce-scatter.2
where the time goes:
time: 1100 us
  waiting for transfers between devices  850 us (77%)
  blocking collectives  142 us (13%)
  matrix products  54.4 us (5%)
  other arithmetic  20 us (2%)
  local copies, waits for them, and re-layouts  14.8 us (1%)
  between operations  14.5 us (1%)
    reduce_scatter x1, waiting for transfers between devices, shards(): lax.psum_scatter(jnp.dot(block_rows, student_head, preferred_element_type...  387 us
    reduce_scatter x1, waiting for transfers between devices, shards(): lax.psum_scatter(jnp.dot(block_rows, teacher_head, preferred_element_type...  386 us
    all_gather x1, waiting for transfers between devices, shards(): teacher_rows = lax.all_gather(teacher_hidden, 'tv', axis=0, tiled=True)  48.2 us
    all_to_all x1, blocking collectives, shards(): lax.all_to_all(teacher_logit, 'tv', split_axis=0, concat_axis=1, tiled=True)  44.3 us
    dot_general x1, matrix products, shards(): jnp.dot(block_rows, student_head, preferred_element_type=jnp.float32)  34.6 us
    all_gather x2, blocking collectives, joined(): everything = jax.tree.map(lambda part: lax.all_gather(part, axis), array)  32.1 us
    all_gather x1, blocking collectives, shards(): student_rows = lax.all_gather(student_hidden, 'sv', axis=0, tiled=True)  30.3 us
    all_to_all x1, waiting for transfers between devices, shards(): lax.all_to_all(lax.all_to_all(teacher_logit, 'tv', split_axis=0, concat_a...  27.8 us
  transfers between devices with their start and end apart: 4, of which 4 were waited for; matrix products, arithmetic and copies ran while one was open for 4% of the time, Pallas kernels for 0%

commit v1 on v0

v1 whole, which is shorter than its diff:
```python
import functools

import jax
import jax.numpy as jnp
from jax import lax
from jax.experimental import pallas as pl
from jax.experimental.pallas import tpu as pltpu
from jax.sharding import PartitionSpec as P

AXES = ("tv", "sv")
GROUPS = 2
SHIFTS = (0, 1, 3, 2)
TILE = 512
F32 = jnp.float32
BF16 = jnp.bfloat16


def place(t, s):
    return t // 4, (t // 2) % 2, t % 2, s // 4, s % 4


def moved(x, step):
    pairs = []
    for source in range(128):
        z, xh, c, xl, y = step(*place(source // 8, source % 8))
        target = ((z % 4) * 4 + (xh % 2) * 2 + c % 2) * 8 + (xl % 2) * 4 + y % 4
        pairs.append((source, target))
    return lax.ppermute(x, AXES, pairs)


def along_z(d):
    return lambda z, xh, c, xl, y: (z + d, xh, c, xl, y)


def along_y(d):
    return lambda z, xh, c, xl, y: (z, xh, c, xl, y + d)


def other_core(z, xh, c, xl, y):
    return z, xh, c + 1, xl, y


def other_xh(z, xh, c, xl, y):
    return z, xh + 1, c, xl, y


def other_xl(z, xh, c, xl, y):
    return z, xh, c, xl + 1, y


def ring(x, along):
    return [x if d == 0 else moved(x, along(d)) for d in SHIFTS]


def ordered(parts, here):
    back = jnp.stack([parts[SHIFTS.index(d)] for d in (3, 2, 1, 0)] * 2)
    return lax.dynamic_slice_in_dim(back, 3 - here, 4, axis=0)


def paired(x, step, here):
    other = moved(x, step)
    return jnp.where(here == 0, jnp.stack([x, other]), jnp.stack([other, x]))


def coded(x):
    top = jnp.maximum(jnp.max(jnp.abs(x), axis=1, keepdims=True), 1e-30)
    power = jnp.ceil(jnp.log2(top) + 1e-4)
    code = jnp.clip(jnp.round(x * jnp.exp2(15.0 - power)), -32767.0, 32767.0)
    return jnp.concatenate([code, power], axis=1).astype(jnp.int16)


def decoded(code):
    power = code[:, -1:].astype(F32)
    return code[:, :-1].astype(F32) * jnp.exp2(power - 15.0)


def student_kernel(hidden, w0, w1, w2, w3, theirs, ours, joint):
    depth = w0.shape[0]
    for k, w in enumerate((w0, w1, w2, w3)):
        joint[k * depth:(k + 1) * depth, :] = w[...]
    theirs[...] = jnp.dot(hidden[1], joint[...], preferred_element_type=F32)
    ours[...] = jnp.dot(hidden[0], joint[...], preferred_element_type=F32)


def student_partial(hidden, weights):
    _, rows, width = hidden.shape
    depth, words = weights[0].shape
    block = pl.BlockSpec((rows, TILE), lambda j: (0, j))
    return pl.pallas_call(
        student_kernel,
        grid=(pl.cdiv(words, TILE),),
        in_specs=[pl.BlockSpec((2, rows, width), lambda j: (0, 0, 0))]
        + [pl.BlockSpec((depth, TILE), lambda j: (0, j))] * 4,
        out_specs=[block, block],
        out_shape=[jax.ShapeDtypeStruct((rows, words), F32)] * 2,
        scratch_shapes=[pltpu.VMEM((4 * depth, TILE), BF16)],
        compiler_params=pltpu.CompilerParams(vmem_limit_bytes=40 << 20),
        cost_estimate=pl.CostEstimate(
            flops=4 * rows * width * words,
            bytes_accessed=2 * width * words + 8 * rows * words,
            transcendentals=0,
        ),
    )(hidden, *weights)


def teacher_kernel(hidden, weights, logits, total):
    k = pl.program_id(0)

    @pl.when(k == 0)
    def _():
        total[...] = jnp.zeros_like(total)

    total[...] += lax.dot_general(
        hidden[0], weights[0], (((1,), (1,)), ((), ())), preferred_element_type=F32
    )

    @pl.when(k == pl.num_programs(0) - 1)
    def _():
        logits[...] = total[...].astype(BF16)


def teacher_product(hidden, weights):
    steps, rows, depth = hidden.shape
    words = weights.shape[1]
    return pl.pallas_call(
        teacher_kernel,
        grid=(steps,),
        in_specs=[
            pl.BlockSpec((1, rows, depth), lambda k: (k, 0, 0)),
            pl.BlockSpec((1, words, depth), lambda k: (k, 0, 0)),
        ],
        out_specs=pl.BlockSpec((rows, words), lambda k: (0, 0)),
        out_shape=jax.ShapeDtypeStruct((rows, words), BF16),
        scratch_shapes=[pltpu.VMEM((rows, words), F32)],
        compiler_params=pltpu.CompilerParams(vmem_limit_bytes=40 << 20),
        cost_estimate=pl.CostEstimate(
            flops=2 * steps * rows * depth * words,
            bytes_accessed=2 * steps * depth * (rows + words) + 2 * rows * words,
            transcendentals=0,
        ),
    )(hidden, weights)


def student_rows(student_hidden, z, xh, c, xl, y):
    hidden = jnp.concatenate(ring(student_hidden, along_z), axis=1)
    hidden = ordered(ring(paired(hidden, other_xl, xl), along_y), y)
    rows = hidden.shape[2] // 2
    hidden = hidden.reshape(2, 2, 2, 2, rows, -1).transpose(3, 1, 2, 0, 4, 5)
    hidden = hidden.reshape(2, 2, 4, rows, -1)
    hidden = jnp.where(c == 0, hidden, hidden[::-1])
    hidden = jnp.where(xh == 0, hidden, hidden[:, ::-1])
    twice = jnp.concatenate([hidden, hidden], axis=2)
    hidden = lax.dynamic_slice_in_dim(twice, z, 4, axis=2)
    return hidden.reshape(2, 8 * rows, -1)


def student_weights(student_head, z):
    quarter = student_head.shape[1] // 4
    part = quarter // GROUPS
    groups = []
    for g in range(GROUPS):
        pieces = []
        for d in SHIFTS:
            start = ((z + d) % 4) * quarter + g * part
            pieces.append(lax.dynamic_slice_in_dim(student_head, start, part, axis=1))
        student_head, pieces = lax.optimization_barrier((student_head, pieces))
        groups.append([p if d == 0 else moved(p, along_z(d)) for d, p in zip(SHIFTS, pieces)])
    return groups


def student_logits(hidden, weights):
    theirs, ours = student_partial(hidden, weights)
    ours = ours + moved(theirs, other_core)
    half = ours.shape[0] // 2
    rows = half // 4
    full = ours[:half] + decoded(moved(coded(ours[half:]), other_xh))
    parts = []
    for d in SHIFTS:
        part = full[d * rows:(d + 1) * rows]
        parts.append(part if d == 0 else decoded(moved(coded(part), along_z(d))))
    return parts


def teacher_rows(teacher_hidden, z, xh, c, xl, y):
    hidden = paired(teacher_hidden, other_xh, xh)
    hidden = ordered(ring(hidden, along_z), z)
    hidden = paired(hidden, other_xl, xl)
    hidden = ordered(ring(hidden, along_y), y)
    hidden = paired(hidden, other_core, c)
    rows, depth = hidden.shape[5:]
    return hidden.transpose(2, 1, 3, 4, 0, 5, 6).reshape(8, 16 * rows, depth)


def teacher_logits(hidden, weights, z):
    logits = teacher_product(hidden, weights)
    rows, part = logits.shape[0] // 16, logits.shape[1]
    logits = lax.all_to_all(logits.reshape(16, rows, part), "tv", 0, 0, tiled=True)
    logits = lax.all_to_all(logits.reshape(8, 2, rows, part), "sv", 0, 0, tiled=True)
    logits = logits.reshape(2, GROUPS, 2, 2, rows, part).transpose(3, 0, 1, 4, 2, 5)
    logits = logits.reshape(4, GROUPS, rows, 2 * part)
    back = jnp.concatenate([logits[::-1]] * 2)
    return lax.dynamic_slice_in_dim(back, 3 - z, 4, axis=0)


def shards(teacher_hidden, student_hidden, teacher_head, student_head, token_ids):
    t, s = lax.axis_index("tv"), lax.axis_index("sv")
    here = place(t, s)
    z = here[0]
    width = student_head.shape[1]
    quarter = width // 4
    part = quarter // GROUPS
    words8 = teacher_head.shape[1] // 8
    s_hidden = student_rows(student_hidden, *here)
    s_weights = student_weights(student_head, z)
    pieces = jnp.stack([teacher_head[:, k * words8:(k + 1) * words8].T for k in range(8)])
    t_weights = lax.all_to_all(pieces, "sv", 0, 0, tiled=True)
    t_hidden = teacher_rows(teacher_hidden, *here)
    teacher = teacher_logits(t_hidden, t_weights, z).astype(F32)
    groups = [student_logits(s_hidden, weights) for weights in s_weights]
    student = jnp.stack(
        [jnp.stack([parts[SHIFTS.index(d)] for parts in groups]) for d in range(4)]
    )
    quarters = (z - jnp.arange(4)) % 4
    starts = s * width + quarters[:, None] * quarter + jnp.arange(GROUPS)[None, :] * part
    words = starts[:, :, None, None] + lax.broadcasted_iota(jnp.int32, student.shape, 3)
    gap = student - teacher
    picked = jnp.sum(jnp.where(words == token_ids[:, None], gap, 0.0), axis=(0, 1, 3))
    peak_s = jnp.max(student, axis=(0, 1, 3))
    peak_t = jnp.max(teacher, axis=(0, 1, 3))
    raw = jnp.exp(student - peak_s[:, None])
    mass_s = jnp.sum(raw, axis=(0, 1, 3))
    mass_t = jnp.sum(jnp.exp(teacher - peak_t[:, None]), axis=(0, 1, 3))
    cross = jnp.sum(raw * gap, axis=(0, 1, 3))
    stats = jnp.stack([peak_s, mass_s, cross, peak_t, mass_t, picked])
    stats = lax.all_gather(stats, "sv", axis=0)
    top_s = jnp.max(stats[:, 0], axis=0)
    top_t = jnp.max(stats[:, 3], axis=0)
    scale_s = jnp.exp(stats[:, 0] - top_s)
    scale_t = jnp.exp(stats[:, 3] - top_t)
    total_s = jnp.sum(stats[:, 1] * scale_s, axis=0)
    total_t = jnp.sum(stats[:, 4] * scale_t, axis=0)
    norm_s = top_s + jnp.log(total_s)
    norm_t = top_t + jnp.log(total_t)
    mean_gap = jnp.sum(stats[:, 2] * scale_s, axis=0) / total_s
    kl_div = mean_gap - norm_s + norm_t
    rewards = norm_s - norm_t - jnp.sum(stats[:, 5], axis=0)
    prob = jnp.exp(student - norm_s[:, None])
    grad = (prob * (gap - mean_gap[:, None])).astype(BF16)
    back = jnp.concatenate([grad[::-1]] * 2)
    grad = lax.dynamic_slice_in_dim(back, 3 - z, 4, axis=0)
    logit_grad = grad.transpose(2, 0, 1, 3).reshape(grad.shape[2], width)
    return rewards, kl_div, logit_grad


def solution(mesh):
    in_specs = (P("tv", "sv"), P("sv", "tv"), P("sv", "tv"), P("tv", "sv"), P("tv"))
    out_specs = (P("tv"), P("tv"), P("tv", "sv"))
    return jax.shard_map(shards, mesh=mesh, in_specs=in_specs, out_specs=out_specs, check_vma=False)
```

time: 1100 us -> 626 us (0.57)
  waiting for transfers between devices: 850 us -> 290 us
  blocking collectives: 142 us -> 28.3 us
  local copies, waits for them, and re-layouts: 14.8 us -> 122 us
  starting transfers between devices: 3.74 us -> 69.5 us
  matrix products: 54.4 us -> 0 us
  other arithmetic: 20 us -> 67.1 us
  Pallas kernels: 0 us -> 37.6 us
  between operations: 14.5 us -> 1.82 us
    reduce_scatter x2 -> x0, waiting for transfers between devices: 773 us -> none  [the longest x1 387 us: shards(): lax.psum_scatter(jnp.dot(block_rows, student_head, preferred_element_type...]
    ppermute x0 -> x32, waiting for transfers between devices: none -> 268 us  [moved(): return lax.ppermute(x, AXES, pairs)]
    dot_general x2 -> x0, matrix products: 54.4 us -> none  [the longest x1 34.6 us: shards(): jnp.dot(block_rows, student_head, preferred_element_type=jnp.float32)]
    ppermute x0 -> x32, starting transfers between devices: none -> 49.1 us  [moved(): return lax.ppermute(x, AXES, pairs)]
    all_gather x1 -> x0, waiting for transfers between devices: 48.2 us -> none  [shards(): teacher_rows = lax.all_gather(teacher_hidden, 'tv', axis=0, tiled=True)]
    all_to_all x1 -> x0, blocking collectives: 44.3 us -> none  [shards(): lax.all_to_all(teacher_logit, 'tv', split_axis=0, concat_axis=1, tiled=True)]
    pallas_call x0 -> x3, Pallas kernels: none -> 37.6 us  [the longest x2 21.7 us: student_partial(): pl.pallas_call(student_kernel, grid=(pl.cdiv(words, TILE),), in_specs=[pl...]
    unnamed x14 -> x80, local copies, waits for them, and re-layouts: 2.15 us -> 39.2 us
  transfers between devices with their start and end apart: 4 -> 35, of which waited for: 4 -> 13; matrix products, arithmetic and copies ran while one was open for 4% -> 23% of each run, Pallas kernels for 0% -> 6%
where the time goes in v1:
time: 626 us; the launch traced here: 616 us
  waiting for transfers between devices  290 us (46%)
  local copies, waits for them, and re-layouts  122 us (19%)
  starting transfers between devices  69.5 us (11%)
  other arithmetic  67.1 us (11%)
  Pallas kernels  37.6 us (6%)
  blocking collectives  28.3 us (5%)
    ppermute x32, waiting for transfers between devices, moved(): return lax.ppermute(x, AXES, pairs)  268 us
    ppermute x32, starting transfers between devices, moved(): return lax.ppermute(x, AXES, pairs)  49.1 us
    unnamed x80, local copies, waits for them, and re-layouts  39.2 us
    all_gather x1, blocking collectives, shards(): stats = lax.all_gather(stats, 'sv', axis=0)  28.3 us
    all_to_all x1, waiting for transfers between devices, teacher_logits(): lax.all_to_all(logits.reshape(8, 2, rows, part), 'sv', 0, 0, tiled=True)  22.5 us
    pallas_call x2, Pallas kernels, student_partial(): pl.pallas_call(student_kernel, grid=(pl.cdiv(words, TILE),), in_specs=[pl...  21.7 us
    dynamic_slice x2, local copies, waits for them, and re-layouts, student_weights(): pieces.append(lax.dynamic_slice_in_dim(student_head, start, part, axis=1))  18.2 us
    pallas_call x1, Pallas kernels, teacher_product(): pl.pallas_call(teacher_kernel, grid=(steps,), in_specs=[pl.BlockSpec((1,...  15.9 us
  transfers between devices with their start and end apart: 35, of which 13 were waited for; matrix products, arithmetic and copies ran while one was open for 23% of the time, Pallas kernels for 6%

profile of v1, /device:TPU:6, one launch (start us, length us, event | category | flops | bytes accessed | tf_op | source)
XLA Modules:
  0.0 616.1 jit_solution(17715938622690793349)
XLA Ops:
  1.6 2.0 collective-permute-start
  3.6 2.2 collective-permute-start.1
  9.0 9.1 %constant_dynamic-slice_fusion.6 = (bf16[320,2374]{1,0:T(8,128)(2,1)}, bf16[320,2374]{1,0:T(8,128)(2,1)}, bf16[320,2374]{1,0:T(8,128)(2,1)}, bf16[320,2374]{1,0:T(8,128)(2,1)}) fusion(bf16[320,18992]{1,0:T(8,128)(2,1)} %param.8, s32[]{:T(128)S(6)} %select_n.201, s32[]{:T(128)S(6)} %select_n.199, s32[]{:T(128)S(6)} %select_n.197, s32[]{:T(128)S(6)} %select_n.195), kind=kLoop, calls=%fused_computation.127 | loop fusion | bytes 12154896 | tf_op jit(solution)/shard_map/dynamic_slice | solution.py:165
  18.2 9.1 %constant_dynamic-slice_fusion.2 = (bf16[320,2374]{1,0:T(8,128)(2,1)}, bf16[320,2374]{1,0:T(8,128)(2,1)}, bf16[320,2374]{1,0:T(8,128)(2,1)}, bf16[320,2374]{1,0:T(8,128)(2,1)}) fusion(bf16[320,18992]{1,0:T(8,128)(2,1)} %param.8, s32[]{:T(128)S(6)} %select_n.205, s32[]{:T(128)S(6)} %select_n.204, s32[]{:T(128)S(6)} %select_n.203, s32[]{:T(128)S(6)} %select_n.202), kind=kLoop, calls=%fused_computation.123 | loop fusion | bytes 12154896 | tf_op jit(solution)/shard_map/dynamic_slice | solution.py:165
  28.3 2.4 bitcast_dynamic-update-slice_fusion.7
  30.7 2.3 collective-permute-start.24
  33.0 2.6 bitcast_dynamic-update-slice_fusion.6
  38.0 28.7 %collective-permute-done.25 = bf16[2,64,512]{2,1,0:T(8,128)(2,1)S(1)} collective-permute-done((bf16[2,64,512]{2,1,0:T(8,128)(2,1)S(1)}, bf16[2,64,512]{2,1,0:T(8,128)(2,1)S(1)}, u32[]{:S(2)}, u32[]{:S(2)}) %collective-permute-start.25) | collective-permute-done | bytes 131104 | tf_op jit(solution)/shard_map/ppermute | solution.py:28
  66.8 2.2 collective-permute-done.26
  70.9 3.5 collective-permute-start.4
  74.4 2.7 bitcast_dynamic-update-slice_fusion.5
  77.8 3.3 collective-permute-done.27
  82.8 18.0 %collective-permute-done.4 = bf16[2,128,1280]{2,1,0:T(8,128)(2,1)S(1)} collective-permute-done((bf16[2,128,1280]{2,1,0:T(8,128)(2,1)}, bf16[2,128,1280]{2,1,0:T(8,128)(2,1)S(1)}, u32[]{:S(2)}, u32[]{:S(2)}) %collective-permute-start.4) | collective-permute-done | bytes 655392 | tf_op jit(solution)/shard_map/ppermute | solution.py:28
  100.9 4.1 collective-permute-start.28
  105.2 5.4 collective-permute-done.6
  113.5 31.3 %collective-permute-done.28 = bf16[2,4,2,64,512]{4,3,2,1,0:T(8,128)(2,1)S(1)} collective-permute-done((bf16[2,4,2,64,512]{4,3,2,1,0:T(8,128)(2,1)S(1)}, bf16[2,4,2,64,512]{4,3,2,1,0:T(8,128)(2,1)S(1)}, u32[]{:S(2)}, u32[]{:S(2)}) %collective-permute-start.28) | collective-permute-done | bytes 1048608 | tf_op jit(solution)/shard_map/ppermute | solution.py:28
  145.4 6.8 %collective-permute-start.7 = (bf16[320,2374]{1,0:T(8,128)(2,1)}, bf16[320,2374]{1,0:T(8,128)(2,1)}, u32[]{:S(2)}, u32[]{:S(2)}) collective-permute-start(bf16[320,2374]{1,0:T(8,128)(2,1)} %get-tuple-element.17), channel_id=1, source_target_pairs={{0,32},{1,33},{2,34},{3,35},{4,36},{5,37},{6,38},{7,39},{8,40},{9,... | collective-permute-start | bytes 4558088 | tf_op jit(solution)/shard_map/ppermute | solution.py:28
  152.2 5.4 collective-permute-start.8
  158.6 2.5 constant_dynamic-slice_fusion
  161.1 2.1 copy-done.11
  163.2 16.6 %collective-permute-done.14.w3 = bf16[320,2374]{1,0:T(8,128)(2,1)S(1)} collective-permute-done((bf16[320,2374]{1,0:T(8,128)(2,1)S(1)}, bf16[320,2374]{1,0:T(8,128)(2,1)S(1)}, u32[]{:S(2)}, u32[]{:S(2)}) %collective-permute-start.14) | collective-permute-done | bytes 1519392 | tf_op jit(solution)/shard_map/ppermute | solution.py:28
  179.9 10.9 %shard_map.77 = (f32[512,2374]{1,0:T(8,128)S(1)}, f32[512,2374]{1,0:T(8,128)}) custom-call(bf16[2,512,1280]{2,1,0:T(8,128)(2,1)S(1)} %bitcast.151, bf16[320,2374]{1,0:T(8,128)(2,1)S(1)} %copy-done.4, bf16[320,2374]{1,0:T(8,128)(2,1)} %collective-permute-done.12.w1, bf16[320,2374]{1,0:T(8,128)(2,1)} %collective-permute-done.13.w2, ...), custom_call_target="tpu_custom_call" | custom-call | flops 6223298560 | bytes 15801344 | tf_op jit(solution)/shard_map/pallas_call | solution.py:89
  190.7 2.3 copy-done.2
  193.0 5.8 copy.92
  198.8 2.6 bitcast_dynamic-update-slice_fusion.4
  201.4 3.1 collective-permute-done.7.w1
  204.5 32.8 %collective-permute-done.8.w2 = bf16[320,2374]{1,0:T(8,128)(2,1)} collective-permute-done((bf16[320,2374]{1,0:T(8,128)(2,1)}, bf16[320,2374]{1,0:T(8,128)(2,1)}, u32[]{:S(2)}, u32[]{:S(2)}) %collective-permute-start.8) | collective-permute-done | bytes 1519392 | tf_op jit(solution)/shard_map/ppermute | solution.py:28
  238.6 10.8 %shard_map.76 = (f32[512,2374]{1,0:T(8,128)S(1)}, f32[512,2374]{1,0:T(8,128)}) custom-call(bf16[2,512,1280]{2,1,0:T(8,128)(2,1)S(1)} %bitcast.152, bf16[320,2374]{1,0:T(8,128)(2,1)S(1)} %copy-done.3, bf16[320,2374]{1,0:T(8,128)(2,1)} %collective-permute-done.7.w1, bf16[320,2374]{1,0:T(8,128)(2,1)} %collective-permute-done.8.w2, ...), custom_call_target="tpu_custom_call" | custom-call | flops 6223298560 | bytes 15801344 | tf_op jit(solution)/shard_map/pallas_call | solution.py:89
  249.4 2.3 copy-done.1
  251.7 5.8 copy.87
  257.6 2.6 bitcast_dynamic-update-slice_fusion.3
  260.2 2.6 bitcast_dynamic-update-slice_fusion.2
  262.9 2.6 bitcast_dynamic-update-slice_fusion.1
  265.5 2.6 bitcast_dynamic-update-slice_fusion
  268.1 6.7 %all-to-all-start = ((bf16[8,1187,512]{2,1,0:T(8,128)(2,1)}), bf16[8,1187,512]{2,1,0:T(8,128)(2,1)}, u32[]{:S(2)}, u32[]{:S(2)}) async-start(bf16[8,1187,512]{2,1,0:T(8,128)(2,1)} %bitcast_dynamic-update-slice_fusion), calls=%async_computation | async-start | bytes 19529728 | tf_op jit(solution)/shard_map/all_to_all | solution.py:216
  275.4 2.7 fusion.38
  278.1 8.1 %fusion = bf16[2,4,4,2,2,64,512]{6,5,3,2,0,1,4:T(8,128)(2,1)} fusion(bf16[1,4,2,4,2,64,512]{6,5,4,3,2,1,0:T(8,128)(2,1)} %bitcast.48, bf16[1,4,2,4,2,64,512]{6,5,4,3,2,1,0:T(8,128)(2,1)S(1)} %fusion.38, pred[]{:T(512)S(6)} %eq.35), kind=kLoop, calls=%fused_computation.1 | loop fusion | flops 12582912 | bytes 16777216 | tf_op jit(solution)/shard_map/transpose | solution.py:191
  286.2 7.9 %copy.103 = bf16[2,4,4,2,2,64,512]{6,5,4,3,2,1,0:T(8,128)(2,1)} copy(bf16[2,4,4,2,2,64,512]{6,5,3,2,0,1,4:T(8,128)(2,1)} %fusion) | data formatting | bytes 16777216 | tf_op jit(solution)/shard_map/transpose | solution.py:191
  294.1 5.7 copy.93
  299.9 4.4 add.342
  308.5 2.5 collective-permute-start.16
  311.0 5.7 copy.88
  316.7 4.4 add.330
  326.4 83.3 %collective-permute-done.16 = s16[256,2375]{0,1:T(8,128)(2,1)S(1)} collective-permute-done((s16[256,2375]{0,1:T(8,128)(2,1)}, s16[256,2375]{0,1:T(8,128)(2,1)S(1)}, u32[]{:S(2)}, u32[]{:S(2)}) %collective-permute-start.16) | collective-permute-done | bytes 1216032 | tf_op jit(solution)/shard_map/ppermute | solution.py:28
  411.6 2.5 slice_add_fusion
  417.8 17.4 %collective-permute-done.11 = s16[256,2375]{0,1:T(8,128)(2,1)} collective-permute-done((s16[256,2375]{0,1:T(8,128)(2,1)}, s16[256,2375]{0,1:T(8,128)(2,1)}, u32[]{:S(2)}, u32[]{:S(2)}) %collective-permute-start.11) | collective-permute-done | bytes 1216032 | tf_op jit(solution)/shard_map/ppermute | solution.py:28
  435.2 2.7 copy.109
  438.6 2.5 slice_add_fusion.1
  446.6 4.3 collective-permute-start.20
  452.4 3.4 copy-done
  455.8 15.9 %shard_map.78 = bf16[1024,1187]{1,0:T(8,128)(2,1)} custom-call(bf16[8,1024,512]{2,1,0:T(8,128)(2,1)S(1)} %bitcast.150, bf16[8,1187,512]{2,1,0:T(8,128)(2,1)} %all-to-all-done.weights), custom_call_target="tpu_custom_call" | custom-call | flops 9957277696 | bytes 20543488 | tf_op jit(solution)/shard_map/pallas_call | solution.py:125
  471.7 7.9 %all-to-all-start.1 = ((bf16[16,64,1187]{2,1,0:T(8,128)(2,1)}), bf16[16,64,1187]{2,1,0:T(8,128)(2,1)}, u32[]{:S(2)}, u32[]{:S(2)}) async-start(bf16[16,64,1187]{2,1,0:T(8,128)(2,1)} %bitcast.67), calls=%async_computation.1 | async-start | bytes 5242880 | tf_op jit(solution)/shard_map/all_to_all | solution.py:197
  480.5 2.7 collective-permute-start.22
  492.1 25.6 %collective-permute-done.22 = s16[64,2375]{1,0:T(8,128)(2,1)S(1)} collective-permute-done((s16[64,2375]{1,0:T(8,128)(2,1)}, s16[64,2375]{1,0:T(8,128)(2,1)S(1)}, u32[]{:S(2)}, u32[]{:S(2)}) %collective-permute-start.22) | collective-permute-done | bytes 304032 | tf_op jit(solution)/shard_map/ppermute | solution.py:28
  520.0 5.7 all-to-all-start.2
  533.6 22.5 %all-to-all-done.2 = bf16[8,2,64,1187]{3,2,1,0:T(8,128)(2,1)S(1)} async-done(((bf16[8,2,64,1187]{3,2,1,0:T(8,128)(2,1)}), bf16[8,2,64,1187]{3,2,1,0:T(8,128)(2,1)S(1)}, u32[]{:S(2)}, u32[]{:S(2)}) %all-to-all-start.2) | async-done | bytes 2431008 | tf_op jit(solution)/shard_map/all_to_all | solution.py:198
  556.2 4.2 copy.104
  560.4 5.4 reshape.673
  567.4 3.0 fusion.35
  570.6 2.8 select_reduce_fusion
  573.4 28.3 %all-gather.1 = f32[8,6,64]{2,1,0:T(8,128)S(1)} all-gather(f32[1,6,64]{2,1,0:T(8,128)S(1)} %bitcast.178), channel_id=2, replica_groups=mesh['tv'=16,'sv'=8] {'sv'}, dimensions={0}, use_global_device_ids=true | all-gather | bytes 13824 | tf_op jit(solution)/shard_map/all_gather | solution.py:235
  602.4 4.1 multiply_convert_fusion
  609.5 2.6 copy.108
  612.0 3.1 reshape.674
  (196 shorter events, 67.1 us)
Async XLA Ops:
  1.6 34.0 %collective-permute-start = (bf16[128,320]{1,0:T(8,128)(2,1)S(1)}, bf16[128,320]{1,0:T(8,128)(2,1)S(1)}, u32[]{:S(2)}, u32[]{:S(2)}) collective-permute-start(bf16[128,320]{1,0:T(8,128)(2,1)S(1)} %copy.85), channel_id=1, source_target_pairs={{0,32},{1,33},{2,34},{3,35},{4,36},{5,37},{6,38},{7,39},{8,40},{9,... | collective-permute-start | bytes 245768 | tf_op jit(solution)/shard_map/ppermute | solution.py:28
  3.6 32.0 %collective-permute-start.1 = (bf16[128,320]{1,0:T(8,128)(2,1)S(1)}, bf16[128,320]{1,0:T(8,128)(2,1)S(1)}, u32[]{:S(2)}, u32[]{:S(2)}) collective-permute-start(bf16[128,320]{1,0:T(8,128)(2,1)S(1)} %copy.85), channel_id=1, source_target_pairs={{0,96},{1,97},{2,98},{3,99},{4,100},{5,101},{6,102},{7,103},{8,104... | collective-permute-start | bytes 245768 | tf_op jit(solution)/shard_map/ppermute | solution.py:28
  5.8 31.7 %collective-permute-start.2 = (bf16[128,320]{1,0:T(8,128)(2,1)S(1)}, bf16[128,320]{1,0:T(8,128)(2,1)S(1)}, u32[]{:S(2)}, u32[]{:S(2)}) collective-permute-start(bf16[128,320]{1,0:T(8,128)(2,1)S(1)} %copy.85), channel_id=1, source_target_pairs={{0,64},{1,65},{2,66},{3,67},{4,68},{5,69},{6,70},{7,71},{8,72},{9,... | collective-permute-start | bytes 245768 | tf_op jit(solution)/shard_map/ppermute | solution.py:28
  7.6 23.1 %collective-permute-start.23 = (bf16[64,512]{1,0:T(8,128)(2,1)}, bf16[64,512]{1,0:T(8,128)(2,1)S(1)}, u32[]{:S(2)}, u32[]{:S(2)}) collective-permute-start(bf16[64,512]{1,0:T(8,128)(2,1)} %param.5), channel_id=1, source_target_pairs={{0,16},{1,17},{2,18},{3,19},{4,20},{5,21},{6,22},{7,23},{8,24},{9,... | collective-permute-start | bytes 196616 | tf_op jit(solution)/shard_map/ppermute | solution.py:28
  18.2 12.5 %copy-start.17 = (bf16[64,512]{1,0:T(8,128)(2,1)S(1)}, bf16[64,512]{1,0:T(8,128)(2,1)}, u32[]{:S(2)}) copy-start(bf16[64,512]{1,0:T(8,128)(2,1)} %param.5) | copy-start | bytes 196612
  27.2 130.9 %collective-permute-start.12 = (bf16[320,2374]{1,0:T(8,128)(2,1)}, bf16[320,2374]{1,0:T(8,128)(2,1)}, u32[]{:S(2)}, u32[]{:S(2)}) collective-permute-start(bf16[320,2374]{1,0:T(8,128)(2,1)} %get-tuple-element.24), channel_id=1, source_target_pairs={{0,32},{1,33},{2,34},{3,35},{4,36},{5,37},{6,38},{7,39},{8,40},{9,... | collective-permute-start | bytes 4558088 | tf_op jit(solution)/shard_map/ppermute | solution.py:28
  30.7 7.2 %collective-permute-start.24 = (bf16[2,64,512]{2,1,0:T(8,128)(2,1)S(1)}, bf16[2,64,512]{2,1,0:T(8,128)(2,1)S(1)}, u32[]{:S(2)}, u32[]{:S(2)}) collective-permute-start(bf16[2,64,512]{2,1,0:T(8,128)(2,1)S(1)} %maximum_select_fusion.5), channel_id=1, source_target_pairs={{0,96},{1,97},{2,98},{3,99},{4,100},{5,101},{6,102},{7,103},{8,104... | collective-permute-start | bytes 393224 | tf_op jit(solution)/shard_map/ppermute | solution.py:28
  35.6 127.6 %collective-permute-start.13 = (bf16[320,2374]{1,0:T(8,128)(2,1)}, bf16[320,2374]{1,0:T(8,128)(2,1)}, u32[]{:S(2)}, u32[]{:S(2)}) collective-permute-start(bf16[320,2374]{1,0:T(8,128)(2,1)} %get-tuple-element.25), channel_id=1, source_target_pairs={{0,96},{1,97},{2,98},{3,99},{4,100},{5,101},{6,102},{7,103},{8,104... | collective-permute-start | bytes 4558088 | tf_op jit(solution)/shard_map/ppermute | solution.py:28
  35.6 31.1 %collective-permute-start.25 = (bf16[2,64,512]{2,1,0:T(8,128)(2,1)S(1)}, bf16[2,64,512]{2,1,0:T(8,128)(2,1)S(1)}, u32[]{:S(2)}, u32[]{:S(2)}) collective-permute-start(bf16[2,64,512]{2,1,0:T(8,128)(2,1)S(1)} %maximum_select_fusion.5), channel_id=1, source_target_pairs={{0,64},{1,65},{2,66},{3,67},{4,68},{5,69},{6,70},{7,71},{8,72},{9,... | collective-permute-start | bytes 393224 | tf_op jit(solution)/shard_map/ppermute | solution.py:28
  37.5 31.5 %collective-permute-start.26 = (bf16[2,64,512]{2,1,0:T(8,128)(2,1)S(1)}, bf16[2,64,512]{2,1,0:T(8,128)(2,1)S(1)}, u32[]{:S(2)}, u32[]{:S(2)}) collective-permute-start(bf16[2,64,512]{2,1,0:T(8,128)(2,1)S(1)} %maximum_select_fusion.5), channel_id=1, source_target_pairs={{0,32},{1,33},{2,34},{3,35},{4,36},{5,37},{6,38},{7,39},{8,40},{9,... | collective-permute-start | bytes 393224 | tf_op jit(solution)/shard_map/ppermute | solution.py:28
  37.9 32.0 %collective-permute-start.3 = (bf16[128,1280]{1,0:T(8,128)(2,1)S(1)}, bf16[128,1280]{1,0:T(8,128)(2,1)S(1)}, u32[]{:S(2)}, u32[]{:S(2)}) collective-permute-start(bf16[128,1280]{1,0:T(8,128)(2,1)S(1)} %concatenate.86), channel_id=1, source_target_pairs={{0,4},{1,5},{2,6},{3,7},{4,0},{5,1},{6,2},{7,3},{8,12},{9,13},{10,... | collective-permute-start | bytes 983048 | tf_op jit(solution)/shard_map/ppermute | solution.py:28
  69.9 11.1 %collective-permute-start.27 = (bf16[4,2,64,512]{3,2,1,0:T(8,128)(2,1)}, bf16[4,2,64,512]{3,2,1,0:T(8,128)(2,1)S(1)}, u32[]{:S(2)}, u32[]{:S(2)}) collective-permute-start(bf16[4,2,64,512]{3,2,1,0:T(8,128)(2,1)} %constant_dynamic-slice_fusion.1), channel_id=1, source_target_pairs={{0,4},{1,5},{2,6},{3,7},{4,0},{5,1},{6,2},{7,3},{8,12},{9,13},{10,... | collective-permute-start | bytes 1572872 | tf_op jit(solution)/shard_map/ppermute | solution.py:28
  70.9 30.0 %collective-permute-start.4 = (bf16[2,128,1280]{2,1,0:T(8,128)(2,1)}, bf16[2,128,1280]{2,1,0:T(8,128)(2,1)S(1)}, u32[]{:S(2)}, u32[]{:S(2)}) collective-permute-start(bf16[2,128,1280]{2,1,0:T(8,128)(2,1)} %maximum_select_fusion.3), channel_id=1, source_target_pairs={{0,3},{1,0},{2,1},{3,2},{4,7},{5,4},{6,5},{7,6},{8,11},{9,8},{10,9... | collective-permute-start | bytes 1966088 | tf_op jit(solution)/shard_map/ppermute | solution.py:28
  77.1 27.9 %collective-permute-start.5 = (bf16[2,128,1280]{2,1,0:T(8,128)(2,1)}, bf16[2,128,1280]{2,1,0:T(8,128)(2,1)S(1)}, u32[]{:S(2)}, u32[]{:S(2)}) collective-permute-start(bf16[2,128,1280]{2,1,0:T(8,128)(2,1)} %maximum_select_fusion.3), channel_id=1, source_target_pairs={{0,2},{1,3},{2,0},{3,1},{4,6},{5,7},{6,4},{7,5},{8,10},{9,11},{10,... | collective-permute-start | bytes 1966088 | tf_op jit(solution)/shard_map/ppermute | solution.py:28
  81.1 29.4 %collective-permute-start.6 = (bf16[2,128,1280]{2,1,0:T(8,128)(2,1)}, bf16[2,128,1280]{2,1,0:T(8,128)(2,1)S(1)}, u32[]{:S(2)}, u32[]{:S(2)}) collective-permute-start(bf16[2,128,1280]{2,1,0:T(8,128)(2,1)} %maximum_select_fusion.3), channel_id=1, source_target_pairs={{0,1},{1,2},{2,3},{3,0},{4,5},{5,6},{6,7},{7,4},{8,9},{9,10},{10,1... | collective-permute-start | bytes 1966088 | tf_op jit(solution)/shard_map/ppermute | solution.py:28
  100.9 43.9 %collective-permute-start.28 = (bf16[2,4,2,64,512]{4,3,2,1,0:T(8,128)(2,1)S(1)}, bf16[2,4,2,64,512]{4,3,2,1,0:T(8,128)(2,1)S(1)}, u32[]{:S(2)}, u32[]{:S(2)}) collective-permute-start(bf16[2,4,2,64,512]{4,3,2,1,0:T(8,128)(2,1)S(1)} %maximum_select_fusion.1), channel_id=1, source_target_pairs={{0,3},{1,0},{2,1},{3,2},{4,7},{5,4},{6,5},{7,6},{8,11},{9,8},{10,9... | collective-permute-start | bytes 3145736 | tf_op jit(solution)/shard_map/ppermute | solution.py:28
  105.0 40.4 %collective-permute-start.29 = (bf16[2,4,2,64,512]{4,3,2,1,0:T(8,128)(2,1)S(1)}, bf16[2,4,2,64,512]{4,3,2,1,0:T(8,128)(2,1)S(1)}, u32[]{:S(2)}, u32[]{:S(2)}) collective-permute-start(bf16[2,4,2,64,512]{4,3,2,1,0:T(8,128)(2,1)S(1)} %maximum_select_fusion.1), channel_id=1, source_target_pairs={{0,2},{1,3},{2,0},{3,1},{4,6},{5,7},{6,4},{7,5},{8,10},{9,11},{10,... | collective-permute-start | bytes 3145736 | tf_op jit(solution)/shard_map/ppermute | solution.py:28
  110.5 41.7 %collective-permute-start.30 = (bf16[2,4,2,64,512]{4,3,2,1,0:T(8,128)(2,1)S(1)}, bf16[2,4,2,64,512]{4,3,2,1,0:T(8,128)(2,1)S(1)}, u32[]{:S(2)}, u32[]{:S(2)}) collective-permute-start(bf16[2,4,2,64,512]{4,3,2,1,0:T(8,128)(2,1)S(1)} %maximum_select_fusion.1), channel_id=1, source_target_pairs={{0,1},{1,2},{2,3},{3,0},{4,5},{5,6},{6,7},{7,4},{8,9},{9,10},{10,1... | collective-permute-start | bytes 3145736 | tf_op jit(solution)/shard_map/ppermute | solution.py:28
  112.5 32.3 %copy-start.15 = (bf16[320,2374]{1,0:T(8,128)(2,1)S(1)}, bf16[320,2374]{1,0:T(8,128)(2,1)}, u32[]{:S(2)}) copy-start(bf16[320,2374]{1,0:T(8,128)(2,1)} %get-tuple-element.26) | copy-start | bytes 4558084
  144.8 35.1 %collective-permute-start.14 = (bf16[320,2374]{1,0:T(8,128)(2,1)S(1)}, bf16[320,2374]{1,0:T(8,128)(2,1)S(1)}, u32[]{:S(2)}, u32[]{:S(2)}) collective-permute-start(bf16[320,2374]{1,0:T(8,128)(2,1)S(1)} %copy-done.15), channel_id=1, source_target_pairs={{0,64},{1,65},{2,66},{3,67},{4,68},{5,69},{6,70},{7,71},{8,72},{9,... | collective-permute-start | bytes 4558088 | tf_op jit(solution)/shard_map/ppermute | solution.py:28
  145.4 59.1 %collective-permute-start.7 = (bf16[320,2374]{1,0:T(8,128)(2,1)}, bf16[320,2374]{1,0:T(8,128)(2,1)}, u32[]{:S(2)}, u32[]{:S(2)}) collective-permute-start(bf16[320,2374]{1,0:T(8,128)(2,1)} %get-tuple-element.17), channel_id=1, source_target_pairs={{0,32},{1,33},{2,34},{3,35},{4,36},{5,37},{6,38},{7,39},{8,40},{9,... | collective-permute-start | bytes 4558088 | tf_op jit(solution)/shard_map/ppermute | solution.py:28
  152.2 85.0 %collective-permute-start.8 = (bf16[320,2374]{1,0:T(8,128)(2,1)}, bf16[320,2374]{1,0:T(8,128)(2,1)}, u32[]{:S(2)}, u32[]{:S(2)}) collective-permute-start(bf16[320,2374]{1,0:T(8,128)(2,1)} %get-tuple-element.18), channel_id=1, source_target_pairs={{0,96},{1,97},{2,98},{3,99},{4,100},{5,101},{6,102},{7,103},{8,104... | collective-permute-start | bytes 4558088 | tf_op jit(solution)/shard_map/ppermute | solution.py:28
  158.2 79.1 %collective-permute-start.9 = (bf16[320,2374]{1,0:T(8,128)(2,1)}, bf16[320,2374]{1,0:T(8,128)(2,1)}, u32[]{:S(2)}, u32[]{:S(2)}) collective-permute-start(bf16[320,2374]{1,0:T(8,128)(2,1)} %get-tuple-element.19), channel_id=1, source_target_pairs={{0,64},{1,65},{2,66},{3,67},{4,68},{5,69},{6,70},{7,71},{8,72},{9,... | collective-permute-start | bytes 4558088 | tf_op jit(solution)/shard_map/ppermute | solution.py:28
  158.6 4.7 copy-start.11
  158.6 21.3 %copy-start.4 = (bf16[320,2374]{1,0:T(8,128)(2,1)S(1)}, bf16[320,2374]{1,0:T(8,128)(2,1)}, u32[]{:S(2)}) copy-start(bf16[320,2374]{1,0:T(8,128)(2,1)} %get-tuple-element.23.w0) | copy-start | bytes 4558084
  163.2 114.9 %collective-permute-start.31 = (bf16[4,2,4,2,64,512]{5,4,3,2,1,0:T(8,128)(2,1)}, bf16[4,2,4,2,64,512]{5,4,3,2,1,0:T(8,128)(2,1)}, u32[]{:S(2)}, u32[]{:S(2)}) collective-permute-start(bf16[4,2,4,2,64,512]{5,4,3,2,1,0:T(8,128)(2,1)} %constant_dynamic-slice_fusion), channel_id=1, source_target_pairs={{0,8},{1,9},{2,10},{3,11},{4,12},{5,13},{6,14},{7,15},{8,0},{9,1},... | collective-permute-start | bytes 12582920 | tf_op jit(solution)/shard_map/ppermute | solution.py:28
  190.7 2.3 copy-start.2
  198.8 95.3 %collective-permute-start.15 = (f32[512,2374]{0,1:T(8,128)}, f32[512,2374]{0,1:T(8,128)}, u32[]{:S(2)}, u32[]{:S(2)}) collective-permute-start(f32[512,2374]{0,1:T(8,128)} %copy.92), channel_id=1, source_target_pairs={{0,8},{1,9},{2,10},{3,11},{4,12},{5,13},{6,14},{7,15},{8,0},{9,1},... | collective-permute-start | bytes 14585864 | tf_op jit(solution)/shard_map/ppermute | solution.py:28
  237.2 1.4 copy-start.3
  249.4 2.3 copy-start.1
  257.5 53.5 %collective-permute-start.10 = (f32[512,2374]{0,1:T(8,128)}, f32[512,2374]{0,1:T(8,128)}, u32[]{:S(2)}, u32[]{:S(2)}) collective-permute-start(f32[512,2374]{0,1:T(8,128)} %copy.87), channel_id=1, source_target_pairs={{0,8},{1,9},{2,10},{3,11},{4,12},{5,13},{6,14},{7,15},{8,0},{9,1},... | collective-permute-start | bytes 14585864 | tf_op jit(solution)/shard_map/ppermute | solution.py:28
  268.1 184.3 %all-to-all-start = ((bf16[8,1187,512]{2,1,0:T(8,128)(2,1)}), bf16[8,1187,512]{2,1,0:T(8,128)(2,1)}, u32[]{:S(2)}, u32[]{:S(2)}) async-start(bf16[8,1187,512]{2,1,0:T(8,128)(2,1)} %bitcast_dynamic-update-slice_fusion), calls=%async_computation | async-start | bytes 19529728 | tf_op jit(solution)/shard_map/all_to_all | solution.py:216
  304.3 2.3 copy-start.6
  308.5 101.2 %collective-permute-start.16 = (s16[256,2375]{0,1:T(8,128)(2,1)}, s16[256,2375]{0,1:T(8,128)(2,1)S(1)}, u32[]{:S(2)}, u32[]{:S(2)}) collective-permute-start(s16[256,2375]{0,1:T(8,128)(2,1)} %copy.95), channel_id=1, source_target_pairs={{0,16},{1,17},{2,18},{3,19},{4,20},{5,21},{6,22},{7,23},{8,24},{9,... | collective-permute-start | bytes 3648008 | tf_op jit(solution)/shard_map/ppermute | solution.py:28
  321.2 2.3 copy-start.5
  325.3 109.8 %collective-permute-start.11 = (s16[256,2375]{0,1:T(8,128)(2,1)}, s16[256,2375]{0,1:T(8,128)(2,1)}, u32[]{:S(2)}, u32[]{:S(2)}) collective-permute-start(s16[256,2375]{0,1:T(8,128)(2,1)} %copy.90), channel_id=1, source_target_pairs={{0,16},{1,17},{2,18},{3,19},{4,20},{5,21},{6,22},{7,23},{8,24},{9,... | collective-permute-start | bytes 3648008 | tf_op jit(solution)/shard_map/ppermute | solution.py:28
  416.9 69.0 %collective-permute-start.18 = (s16[64,2375]{1,0:T(8,128)(2,1)}, s16[64,2375]{1,0:T(8,128)(2,1)}, u32[]{:S(2)}, u32[]{:S(2)}) collective-permute-start(s16[64,2375]{1,0:T(8,128)(2,1)} %pad_add_fusion.3), channel_id=1, source_target_pairs={{0,32},{1,33},{2,34},{3,35},{4,36},{5,37},{6,38},{7,39},{8,40},{9,... | collective-permute-start | bytes 912008 | tf_op jit(solution)/shard_map/ppermute | solution.py:28
  443.8 43.8 %collective-permute-start.17 = (s16[64,2375]{1,0:T(8,128)(2,1)S(1)}, s16[64,2375]{1,0:T(8,128)(2,1)S(1)}, u32[]{:S(2)}, u32[]{:S(2)}) collective-permute-start(s16[64,2375]{1,0:T(8,128)(2,1)S(1)} %pad_add_fusion.2), channel_id=1, source_target_pairs={{0,32},{1,33},{2,34},{3,35},{4,36},{5,37},{6,38},{7,39},{8,40},{9,... | collective-permute-start | bytes 912008 | tf_op jit(solution)/shard_map/ppermute | solution.py:28
  446.6 41.2 %collective-permute-start.20 = (s16[64,2375]{1,0:T(8,128)(2,1)}, s16[64,2375]{1,0:T(8,128)(2,1)S(1)}, u32[]{:S(2)}, u32[]{:S(2)}) collective-permute-start(s16[64,2375]{1,0:T(8,128)(2,1)} %pad_add_fusion.5), channel_id=1, source_target_pairs={{0,64},{1,65},{2,66},{3,67},{4,68},{5,69},{6,70},{7,71},{8,72},{9,... | collective-permute-start | bytes 912008 | tf_op jit(solution)/shard_map/ppermute | solution.py:28
  452.0 37.7 %collective-permute-start.19 = (s16[64,2375]{1,0:T(8,128)(2,1)S(1)}, s16[64,2375]{1,0:T(8,128)(2,1)S(1)}, u32[]{:S(2)}, u32[]{:S(2)}) collective-permute-start(s16[64,2375]{1,0:T(8,128)(2,1)S(1)} %pad_add_fusion.4), channel_id=1, source_target_pairs={{0,64},{1,65},{2,66},{3,67},{4,68},{5,69},{6,70},{7,71},{8,72},{9,... | collective-permute-start | bytes 912008 | tf_op jit(solution)/shard_map/ppermute | solution.py:28
  452.4 3.4 copy-start
  471.7 12.2 %copy-start.12 = (f32[1,64,2374]{2,1,0:T(8,128)S(1)}, f32[1,64,2374]{2,1,0:T(8,128)}, u32[]{:S(2)}) copy-start(f32[1,64,2374]{2,1,0:T(8,128)} %get-tuple-element.56) | copy-start | bytes 1823236
  471.7 48.3 %all-to-all-start.1 = ((bf16[16,64,1187]{2,1,0:T(8,128)(2,1)}), bf16[16,64,1187]{2,1,0:T(8,128)(2,1)}, u32[]{:S(2)}, u32[]{:S(2)}) async-start(bf16[16,64,1187]{2,1,0:T(8,128)(2,1)} %bitcast.67), calls=%async_computation.1 | async-start | bytes 5242880 | tf_op jit(solution)/shard_map/all_to_all | solution.py:197
  479.6 5.4 copy-start.16
  480.5 37.2 %collective-permute-start.22 = (s16[64,2375]{1,0:T(8,128)(2,1)}, s16[64,2375]{1,0:T(8,128)(2,1)S(1)}, u32[]{:S(2)}, u32[]{:S(2)}) collective-permute-start(s16[64,2375]{1,0:T(8,128)(2,1)} %pad_add_fusion.7), channel_id=1, source_target_pairs={{0,96},{1,97},{2,98},{3,99},{4,100},{5,101},{6,102},{7,103},{8,104... | collective-permute-start | bytes 912008 | tf_op jit(solution)/shard_map/ppermute | solution.py:28
  485.9 39.9 %collective-permute-start.21 = (s16[64,2375]{1,0:T(8,128)(2,1)}, s16[64,2375]{1,0:T(8,128)(2,1)}, u32[]{:S(2)}, u32[]{:S(2)}) collective-permute-start(s16[64,2375]{1,0:T(8,128)(2,1)} %pad_add_fusion.6), channel_id=1, source_target_pairs={{0,96},{1,97},{2,98},{3,99},{4,100},{5,101},{6,102},{7,103},{8,104... | collective-permute-start | bytes 912008 | tf_op jit(solution)/shard_map/ppermute | solution.py:28
  489.7 30.3 %copy-start.18 = (s16[64,2375]{1,0:T(8,128)(2,1)}, s16[64,2375]{1,0:T(8,128)(2,1)S(1)}, u32[]{:S(2)}) copy-start(s16[64,2375]{1,0:T(8,128)(2,1)S(1)} %collective-permute-done.19) | copy-start | bytes 912004
  520.0 36.2 %all-to-all-start.2 = ((bf16[8,2,64,1187]{3,2,1,0:T(8,128)(2,1)}), bf16[8,2,64,1187]{3,2,1,0:T(8,128)(2,1)S(1)}, u32[]{:S(2)}, u32[]{:S(2)}) async-start(bf16[8,2,64,1187]{3,2,1,0:T(8,128)(2,1)} %bitcast.68), calls=%async_computation.2 | async-start | bytes 5242880 | tf_op jit(solution)/shard_map/all_to_all | solution.py:198
  525.7 4.4 copy-start.20
  525.7 4.4 copy-start.21
  525.8 4.4 copy-start.22
  525.8 4.4 copy-start.23
  525.8 4.4 copy-start.24
  525.8 4.5 copy-start.13
  526.8 4.6 copy-start.14
  567.4 3.1 copy-start.7
  567.4 3.1 copy-start.8
  567.4 3.1 copy-start.9
  567.4 3.2 copy-start.10
  567.4 3.2 copy-start.19
  567.4 3.2 copy-start.25

commit v2 on v1

v2 whole, which is shorter than its diff:
```python
import functools

import jax
import jax.numpy as jnp
from jax import lax
from jax.experimental import pallas as pl
from jax.experimental.pallas import tpu as pltpu
from jax.sharding import PartitionSpec as P

AXES = ("tv", "sv")
GROUPS = 2
SHIFTS = (0, 1, 3, 2)
TILE = 512
F32 = jnp.float32
BF16 = jnp.bfloat16


def place(t, s):
    return t // 4, (t // 2) % 2, t % 2, s // 4, s % 4


def moved(x, step):
    pairs = []
    for source in range(128):
        z, xh, c, xl, y = step(*place(source // 8, source % 8))
        target = ((z % 4) * 4 + (xh % 2) * 2 + c % 2) * 8 + (xl % 2) * 4 + y % 4
        pairs.append((source, target))
    return lax.ppermute(x, AXES, pairs)


def along_z(d):
    return lambda z, xh, c, xl, y: (z + d, xh, c, xl, y)


def along_y(d):
    return lambda z, xh, c, xl, y: (z, xh, c, xl, y + d)


def other_core(z, xh, c, xl, y):
    return z, xh, c + 1, xl, y


def other_xh(z, xh, c, xl, y):
    return z, xh + 1, c, xl, y


def other_xl(z, xh, c, xl, y):
    return z, xh, c, xl + 1, y


def ring(x, along):
    return [x if d == 0 else moved(x, along(d)) for d in SHIFTS]


def ordered(parts, here):
    back = jnp.stack([parts[SHIFTS.index(d)] for d in (3, 2, 1, 0)] * 2)
    return lax.dynamic_slice_in_dim(back, 3 - here, 4, axis=0)


def paired(x, step, here, axis=0):
    other = moved(x, step)
    return jnp.where(
        here == 0, jnp.stack([x, other], axis=axis), jnp.stack([other, x], axis=axis)
    )


def coded(x):
    top = jnp.maximum(jnp.max(jnp.abs(x), axis=1, keepdims=True), 1e-30)
    power = jnp.ceil(jnp.log2(top) + 1e-4)
    code = jnp.clip(jnp.round(x * jnp.exp2(15.0 - power)), -32767.0, 32767.0)
    column = lax.broadcasted_iota(jnp.int32, x.shape, 1)
    return jnp.where(column == x.shape[1] - 1, power, code).astype(jnp.int16)


def decoded(code):
    power = code[:, -1:].astype(F32)
    return code.astype(F32) * jnp.exp2(power - 15.0)


def student_kernel(words, hidden, w0, w1, w2, w3, theirs, ours, joint):
    depth = w0.shape[0]
    for k, w in enumerate((w0, w1, w2, w3)):
        joint[k * depth:(k + 1) * depth, :] = w[...]
    column = pl.program_id(0) * TILE + lax.broadcasted_iota(jnp.int32, ours.shape, 1)
    for part, out in ((1, theirs), (0, ours)):
        logits = jnp.dot(hidden[part], joint[...], preferred_element_type=F32)
        out[...] = jnp.where(column < words, logits, 0.0)


def student_partial(hidden, weights, padded):
    _, rows, width = hidden.shape
    depth, words = weights[0].shape
    block = pl.BlockSpec((rows, TILE), lambda j: (0, j))
    return pl.pallas_call(
        functools.partial(student_kernel, words),
        grid=(pl.cdiv(padded, TILE),),
        in_specs=[pl.BlockSpec((2, rows, width), lambda j: (0, 0, 0))]
        + [pl.BlockSpec((depth, TILE), lambda j: (0, j))] * 4,
        out_specs=[block, block],
        out_shape=[jax.ShapeDtypeStruct((rows, padded), F32)] * 2,
        scratch_shapes=[pltpu.VMEM((4 * depth, TILE), BF16)],
        compiler_params=pltpu.CompilerParams(vmem_limit_bytes=40 << 20),
        cost_estimate=pl.CostEstimate(
            flops=4 * rows * width * words,
            bytes_accessed=2 * width * words + 8 * rows * words,
            transcendentals=0,
        ),
    )(hidden, *weights)


def teacher_kernel(hidden, weights, logits, total):
    k = pl.program_id(0)

    @pl.when(k == 0)
    def _():
        total[...] = jnp.zeros_like(total)

    total[...] += lax.dot_general(
        hidden[0], weights[0], (((1,), (1,)), ((), ())), preferred_element_type=F32
    )

    @pl.when(k == pl.num_programs(0) - 1)
    def _():
        logits[...] = total[...].astype(BF16)


def teacher_product(hidden, weights):
    steps, rows, depth = hidden.shape
    words = weights.shape[1]
    return pl.pallas_call(
        teacher_kernel,
        grid=(steps,),
        in_specs=[
            pl.BlockSpec((1, rows, depth), lambda k: (k, 0, 0)),
            pl.BlockSpec((1, words, depth), lambda k: (k, 0, 0)),
        ],
        out_specs=pl.BlockSpec((rows, words), lambda k: (0, 0)),
        out_shape=jax.ShapeDtypeStruct((rows, words), BF16),
        scratch_shapes=[pltpu.VMEM((rows, words), F32)],
        compiler_params=pltpu.CompilerParams(vmem_limit_bytes=40 << 20),
        cost_estimate=pl.CostEstimate(
            flops=2 * steps * rows * depth * words,
            bytes_accessed=2 * steps * depth * (rows + words) + 2 * rows * words,
            transcendentals=0,
        ),
    )(hidden, weights)


def student_rows(hidden, z, xh, c):
    rows = hidden.shape[2] // 2
    hidden = hidden.reshape(2, 2, 2, 2, rows, -1).transpose(3, 1, 2, 0, 4, 5)
    hidden = hidden.reshape(2, 2, 4, rows, -1)
    hidden = jnp.where(c == 0, hidden, hidden[::-1])
    hidden = jnp.where(xh == 0, hidden, hidden[:, ::-1])
    twice = jnp.concatenate([hidden, hidden], axis=2)
    hidden = lax.dynamic_slice_in_dim(twice, z, 4, axis=2)
    return hidden.reshape(2, 8 * rows, -1)


def first_stage(teacher_hidden, student_hidden):
    width = teacher_hidden.shape[1]
    pack = jnp.concatenate([teacher_hidden, student_hidden.reshape(-1, width)])
    return ring(pack, along_z)


def all_rows(stage, teacher_shape, student_shape, z, xh, c, xl, y):
    rows, width = teacher_shape
    s_rows, s_depth = student_shape
    teacher = ordered([part[:rows] for part in stage], z)
    teacher = paired(teacher, other_xh, xh, axis=1)
    student = jnp.concatenate([part[rows:].reshape(s_rows, s_depth) for part in stage], axis=1)
    pack = jnp.concatenate([teacher.reshape(-1, width), student.reshape(-1, width)])
    pack = ordered(ring(paired(pack, other_xl, xl), along_y), y)
    student = pack[:, :, 8 * rows:].reshape(4, 2, s_rows, 4 * s_depth)
    teacher = pack[:, :, :8 * rows].transpose(1, 0, 2, 3).reshape(8, 8, rows, width)
    teacher = paired(teacher, other_core, c, axis=2)
    return teacher.reshape(8, 16 * rows, width), student_rows(student, z, xh, c)


def student_pieces(student_head, z, start, words):
    quarter = student_head.shape[1] // 4
    return [
        lax.dynamic_slice_in_dim(student_head, ((z + d) % 4) * quarter + start, words, axis=1)
        for d in SHIFTS
    ]


def sent(pieces):
    return [p if d == 0 else moved(p, along_z(d)) for d, p in zip(SHIFTS, pieces)]


def student_logits(hidden, weights, padded):
    theirs, ours = student_partial(hidden, weights, padded)
    ours = ours + moved(theirs, other_core)
    half = ours.shape[0] // 2
    rows = half // 4
    full = ours[:half] + decoded(moved(coded(ours[half:]), other_xh))
    parts = []
    for d in SHIFTS:
        part = full[d * rows:(d + 1) * rows]
        parts.append(part if d == 0 else decoded(moved(coded(part), along_z(d))))
    return parts


def teacher_logits(hidden, weights, padded):
    logits = teacher_product(hidden, weights)
    rows, part = logits.shape[0] // 16, logits.shape[1]
    logits = lax.all_to_all(logits.reshape(16, rows, part), "tv", 0, 0, tiled=True)
    logits = lax.all_to_all(logits.reshape(8, 2, rows, part), "sv", 0, 0, tiled=True)
    logits = logits.reshape(GROUPS, 4, 2, rows, part).transpose(2, 0, 3, 1, 4)
    logits = logits.reshape(2, GROUPS, rows, 4 * part)
    return jnp.pad(logits, ((0, 0), (0, 0), (0, 0), (0, padded - 4 * part)))


def pooled(a, b):
    top_s = jnp.maximum(a[0], b[0])
    top_t = jnp.maximum(a[3], b[3])
    a_s, b_s = jnp.exp(a[0] - top_s), jnp.exp(b[0] - top_s)
    a_t, b_t = jnp.exp(a[3] - top_t), jnp.exp(b[3] - top_t)
    return jnp.stack([
        top_s,
        a[1] * a_s + b[1] * b_s,
        a[2] * a_s + b[2] * b_s,
        top_t,
        a[4] * a_t + b[4] * b_t,
        a[5] + b[5],
    ])


def shards(teacher_hidden, student_hidden, teacher_head, student_head, token_ids):
    t, s = lax.axis_index("tv"), lax.axis_index("sv")
    here = place(t, s)
    z, c = here[0], here[2]
    width = student_head.shape[1]
    quarter = width // 4
    chunk = -(-quarter // 64) * 8
    sizes = (4 * chunk, quarter - 4 * chunk)
    padded = (4 * chunk // 128 + 1) * 128
    stage = first_stage(teacher_hidden, student_hidden)
    tall = teacher_head.T
    t_first = tall[:8 * chunk].reshape(8, chunk, -1)
    t_second = jnp.pad(tall[quarter:], ((0, 8 * chunk - quarter), (0, 0))).reshape(8, chunk, -1)
    student_head, stage, t_first = lax.optimization_barrier((student_head, stage, t_first))
    s_first = student_pieces(student_head, z, 0, sizes[0])
    t_first = lax.all_to_all(t_first, "sv", 0, 0, tiled=True)
    s_first = sent(s_first)
    t_hidden, s_hidden = all_rows(stage, teacher_hidden.shape, student_hidden.shape, *here)
    s_second = student_pieces(student_head, z, sizes[0], sizes[1])
    s_second, t_second, t_first = lax.optimization_barrier((s_second, t_second, t_first))
    t_second = lax.all_to_all(t_second, "sv", 0, 0, tiled=True)
    s_second = sent(s_second)
    s_second, t_second = lax.optimization_barrier((s_second, t_second))
    teacher = [teacher_logits(t_hidden, w, padded) for w in (t_first, t_second)]
    teacher = jnp.stack(teacher, axis=1).reshape(4, GROUPS, -1, padded).astype(F32)
    groups = [student_logits(s_hidden, w, padded) for w in (s_first, s_second)]
    student = jnp.zeros(teacher.shape, F32)
    for g, parts in enumerate(groups):
        for d, part in zip(SHIFTS, parts):
            student = lax.dynamic_update_slice(student, part[None, None], ((z - d) % 4, g, 0, 0))
    column = lax.broadcasted_iota(jnp.int32, student.shape, 3)
    group = lax.broadcasted_iota(jnp.int32, student.shape, 1)
    index = lax.broadcasted_iota(jnp.int32, student.shape, 0) * quarter + group * sizes[0] + column
    real = column < jnp.where(group == 0, sizes[0], sizes[1])
    student = jnp.where(real, student, -1e30)
    teacher = jnp.where(real, teacher, -1e30)
    gap = student - teacher
    chosen = real & (s * width + index == token_ids[:, None])
    picked = jnp.sum(jnp.where(chosen, gap, 0.0), axis=(0, 1, 3))
    peak_s = jnp.max(student, axis=(0, 1, 3))
    peak_t = jnp.max(teacher, axis=(0, 1, 3))
    raw = jnp.exp(student - peak_s[:, None])
    mass_s = jnp.sum(raw, axis=(0, 1, 3))
    mass_t = jnp.sum(jnp.exp(teacher - peak_t[:, None]), axis=(0, 1, 3))
    cross = jnp.sum(raw * gap, axis=(0, 1, 3))
    stats = jnp.stack([peak_s, mass_s, cross, peak_t, mass_t, picked])
    stats = pooled(stats, moved(stats, other_xl))
    stats = functools.reduce(pooled, ring(stats, along_y))
    norm_s = stats[0] + jnp.log(stats[1])
    norm_t = stats[3] + jnp.log(stats[4])
    mean_gap = stats[2] / stats[1]
    kl_div = mean_gap - norm_s + norm_t
    rewards = norm_s - norm_t - stats[5]
    prob = jnp.exp(student - norm_s[:, None])
    grad = (prob * (gap - mean_gap[:, None])).astype(BF16)
    pieces = [grad[q, g, :, :sizes[g]] for q in range(4) for g in range(GROUPS)]
    return rewards, kl_div, jnp.concatenate(pieces, axis=1)


def solution(mesh):
    in_specs = (P("tv", "sv"), P("sv", "tv"), P("sv", "tv"), P("tv", "sv"), P("tv"))
    out_specs = (P("tv"), P("tv"), P("tv", "sv"))
    return jax.shard_map(shards, mesh=mesh, in_specs=in_specs, out_specs=out_specs, check_vma=False)
```

time: 626 us -> 575 us (0.919)
  waiting for transfers between devices: 290 us -> 247 us
  other arithmetic: 67.1 us -> 51.8 us
  blocking collectives: 28.3 us -> 42.8 us
    all_to_all x0 -> x1, blocking collectives: none -> 42.8 us  [teacher_logits(): lax.all_to_all(logits.reshape(16, rows, part), 'tv', 0, 0, tiled=True)]
    ppermute x32 -> x29, waiting for transfers between devices: 268 us -> 233 us  [moved(): return lax.ppermute(x, AXES, pairs)]
    all_gather x1 -> x0, blocking collectives: 28.3 us -> none  [shards(): stats = lax.all_gather(stats, 'sv', axis=0)]
    all_to_all x1 -> x2, waiting for transfers between devices: 22.5 us -> 6.55 us  [teacher_logits(): lax.all_to_all(logits.reshape(8, 2, rows, part), 'sv', 0, 0, tiled=True)]
    another operation x14 -> x1, other arithmetic: 15.8 us -> 1.12 us  [paired(): jnp.stack([x, other], axis=axis)]
    slice x0 -> x7, local copies, waits for them, and re-layouts: none -> 14.2 us  [the longest x1 5.72 us: shards(): tall[quarter:]]
    ppermute x32 -> x29, starting transfers between devices: 49.1 us -> 35.3 us  [moved(): return lax.ppermute(x, AXES, pairs)]
    pallas_call x2 -> x0, local copies, waits for them, and re-layouts: 11.6 us -> none  [student_partial(): pl.pallas_call(student_kernel, grid=(pl.cdiv(words, TILE),), in_specs=[pl...]
  transfers between devices with their start and end apart: 35 -> 34, of which waited for: 13 -> 15; matrix products, arithmetic and copies ran while one was open for 23% -> 23% of each run, Pallas kernels for 6% -> 7%
where the time goes in v2:
time: 575 us; the launch traced here: 564 us
  waiting for transfers between devices  247 us (43%)
  local copies, waits for them, and re-layouts  117 us (20%)
  starting transfers between devices  63.8 us (11%)
  other arithmetic  51.8 us (9%)
  blocking collectives  42.8 us (7%)
  Pallas kernels  40.9 us (7%)
    ppermute x29, waiting for transfers between devices, moved(): return lax.ppermute(x, AXES, pairs)  233 us
    all_to_all x1, blocking collectives, teacher_logits(): lax.all_to_all(logits.reshape(16, rows, part), 'tv', 0, 0, tiled=True)  42.8 us
    unnamed x77, local copies, waits for them, and re-layouts  40 us
    ppermute x29, starting transfers between devices, moved(): return lax.ppermute(x, AXES, pairs)  35.3 us
    pallas_call x2, Pallas kernels, teacher_product(): pl.pallas_call(teacher_kernel, grid=(steps,), in_specs=[pl.BlockSpec((1,...  20.5 us
    pallas_call x2, Pallas kernels, student_partial(): pl.pallas_call(functools.partial(student_kernel, words), grid=(pl.cdiv(pa...  20.5 us
    dynamic_slice x2, local copies, waits for them, and re-layouts, student_pieces(): lax.dynamic_slice_in_dim(student_head, (z + d) % 4 * quarter + start, wor...  18.1 us
    select_n x3, other arithmetic, paired(): jnp.where(here == 0, jnp.stack([x, other], axis=axis), jnp.stack([other,...  12 us
  transfers between devices with their start and end apart: 34, of which 15 were waited for; matrix products, arithmetic and copies ran while one was open for 23% of the time, Pallas kernels for 7%

profile of v2, /device:TPU:6, one launch (start us, length us, event | category | flops | bytes accessed | tf_op | source)
XLA Modules:
  0.0 564.5 jit_solution(5420128396683080821)
XLA Ops:
  2.7 2.0 collective-permute-start
  4.6 2.2 collective-permute-start.1
  8.6 5.0 slice.264
  15.1 5.9 %all-to-all-start = ((bf16[8,600,512]{2,1,0:T(8,128)(2,1)}), bf16[8,600,512]{2,1,0:T(8,128)(2,1)}, u32[]{:S(2)}, u32[]{:S(2)}) async-start(bf16[8,600,512]{2,1,0:T(8,128)(2,1)} %bitcast.388), calls=%async_computation | async-start | bytes 9830400 | tf_op jit(solution)/shard_map/all_to_all | solution.py:245
  23.6 56.6 %collective-permute-done.3 = bf16[4,64,512]{2,1,0:T(8,128)(2,1)S(1)} collective-permute-done((bf16[4,64,512]{2,1,0:T(8,128)(2,1)S(1)}, bf16[4,64,512]{2,1,0:T(8,128)(2,1)S(1)}, u32[]{:S(2)}, u32[]{:S(2)}) %collective-permute-start.3) | collective-permute-done | bytes 262176 | tf_op jit(solution)/shard_map/ppermute | solution.py:28
  81.5 18.7 %collective-permute-done.4 = bf16[832,512]{1,0:T(8,128)(2,1)S(1)} collective-permute-done((bf16[832,512]{1,0:T(8,128)(2,1)S(1)}, bf16[832,512]{1,0:T(8,128)(2,1)S(1)}, u32[]{:S(2)}, u32[]{:S(2)}) %collective-permute-start.4) | collective-permute-done | bytes 852000 | tf_op jit(solution)/shard_map/ppermute | solution.py:28
  101.6 3.0 collective-permute-start.5
  106.0 5.7 %slice.275 = bf16[4748,512]{1,0:T(8,128)(2,1)} slice(bf16[9496,512]{1,0:T(8,128)(2,1)} %bitcast.393), slice={[4748:9496], [0:512]} | slice | bytes 9723904 | tf_op jit(solution)/shard_map/slice | solution.py:242
  111.7 4.9 pad.11
  116.7 9.1 %constant_dynamic-slice_fusion.5 = (bf16[320,2400]{1,0:T(8,128)(2,1)}, bf16[320,2400]{1,0:T(8,128)(2,1)}, bf16[320,2400]{1,0:T(8,128)(2,1)}, bf16[320,2400]{1,0:T(8,128)(2,1)}) fusion(bf16[320,18992]{1,0:T(8,128)(2,1)} %param.8, s32[]{:T(128)S(6)} %select_n.260, s32[]{:T(128)S(6)} %select_n.258, s32[]{:T(128)S(6)} %select_n.256, s32[]{:T(128)S(6)} %select_n.254), kind=kLoop, calls=%fused_computation.100 | loop fusion | bytes 12288016 | tf_op jit(solution)/shard_map/dynamic_slice | solution.py:183
  127.2 9.1 %constant_dynamic-slice_fusion.1 = (bf16[320,2348]{1,0:T(8,128)(2,1)}, bf16[320,2348]{1,0:T(8,128)(2,1)}, bf16[320,2348]{1,0:T(8,128)(2,1)}, bf16[320,2348]{1,0:T(8,128)(2,1)}) fusion(bf16[320,18992]{1,0:T(8,128)(2,1)} %param.8, s32[]{:T(128)S(6)} %select_n.275, s32[]{:T(128)S(6)} %select_n.274, s32[]{:T(128)S(6)} %select_n.273, s32[]{:T(128)S(6)} %select_n.272), kind=kLoop, calls=%fused_computation.96 | loop fusion | bytes 12021776 | tf_op jit(solution)/shard_map/dynamic_slice | solution.py:183
  136.3 38.7 %collective-permute-done.5 = bf16[2,832,512]{2,1,0:T(8,128)(2,1)} collective-permute-done((bf16[2,832,512]{2,1,0:T(8,128)(2,1)}, bf16[2,832,512]{2,1,0:T(8,128)(2,1)}, u32[]{:S(2)}, u32[]{:S(2)}) %collective-permute-start.5) | collective-permute-done | bytes 1703968 | tf_op jit(solution)/shard_map/ppermute | solution.py:28
  175.0 2.8 bitcast_dynamic-update-slice_fusion.4
  177.8 2.7 bitcast_dynamic-update-slice_fusion.2
  180.5 2.8 bitcast_dynamic-update-slice_fusion
  183.3 6.4 %all-to-all-start.1 = ((bf16[8,600,512]{2,1,0:T(8,128)(2,1)}), bf16[8,600,512]{2,1,0:T(8,128)(2,1)}, u32[]{:S(2)}, u32[]{:S(2)}) async-start(bf16[8,600,512]{2,1,0:T(8,128)(2,1)} %bitcast.389), calls=%async_computation.1 | async-start | bytes 9830400 | tf_op jit(solution)/shard_map/all_to_all | solution.py:250
  189.7 3.7 fusion.10
  193.4 2.7 bitcast_dynamic-update-slice_fusion.5
  196.1 2.9 bitcast_dynamic-update-slice_fusion.3
  199.0 2.8 bitcast_dynamic-update-slice_fusion.1
  203.4 2.6 dynamic-slice_bitcast_fusion
  206.0 2.5 copy.43
  208.5 3.4 constant_dynamic-slice_fusion
  212.0 5.6 reshape_reshape.3
  220.9 2.0 collective-permute-start.16
  229.1 16.6 %collective-permute-done.9.w2 = bf16[320,2400]{1,0:T(8,128)(2,1)} collective-permute-done((bf16[320,2400]{1,0:T(8,128)(2,1)}, bf16[320,2400]{1,0:T(8,128)(2,1)}, u32[]{:S(2)}, u32[]{:S(2)}) %collective-permute-start.9) | collective-permute-done | bytes 1536032 | tf_op jit(solution)/shard_map/ppermute | solution.py:28
  245.7 10.5 %shard_map.76 = (f32[512,2432]{1,0:T(8,128)}, f32[512,2432]{1,0:T(8,128)}) custom-call(bf16[2,512,1280]{2,1,0:T(8,128)(2,1)S(1)} %bitcast.381, bf16[320,2400]{1,0:T(8,128)(2,1)S(1)} %copy-done.3, bf16[320,2400]{1,0:T(8,128)(2,1)S(1)} %copy-done.7, bf16[320,2400]{1,0:T(8,128)(2,1)} %collective-permute-done.9.w2, bf16[320,2400]{1,0:T(8,128)(2,1)S(1)} %copy-done.5), custom_call_target="tpu_custom_call" | custom-call | flops 6291456000 | bytes 15974400 | tf_op jit(solution)/shard_map/pallas_call | solution.py:94
  256.4 35.6 %collective-permute-done.16.w1 = bf16[320,2348]{1,0:T(8,128)(2,1)S(1)} collective-permute-done((bf16[320,2348]{1,0:T(8,128)(2,1)S(1)}, bf16[320,2348]{1,0:T(8,128)(2,1)S(1)}, u32[]{:S(2)}, u32[]{:S(2)}) %collective-permute-start.16) | collective-permute-done | bytes 1502752 | tf_op jit(solution)/shard_map/ppermute | solution.py:28
  301.0 9.9 %shard_map.77 = (f32[512,2432]{1,0:T(8,128)}, f32[512,2432]{1,0:T(8,128)}) custom-call(bf16[2,512,1280]{2,1,0:T(8,128)(2,1)S(1)} %bitcast.382, bf16[320,2348]{1,0:T(8,128)(2,1)S(1)} %copy-done.2, bf16[320,2348]{1,0:T(8,128)(2,1)S(1)} %copy-done.9, bf16[320,2348]{1,0:T(8,128)(2,1)S(1)} %copy-done.11, bf16[320,2348]{1,0:T(8,128)(2,1)S(1)} %copy-done.13), custom_call_target="tpu_custom_call" | custom-call | flops 6155141120 | bytes 15628288 | tf_op jit(solution)/shard_map/pallas_call | solution.py:94
  310.9 10.5 %maximum_select_fusion = bf16[8,8,2,64,512]{4,3,1,0,2:T(8,128)(2,1)} fusion(bf16[8,8,1,64,512]{4,3,1,0,2:T(8,128)(2,1)} %bitcast.33, bf16[8,8,1,64,512]{4,3,1,0,2:T(8,128)(2,1)} %bitcast.31, pred[]{:T(512)S(6)} %eq.81), kind=kLoop, calls=%fused_computation | loop fusion | flops 12582912 | bytes 16777216 | tf_op jit(solution)/shard_map/jit(_where)/select_n | solution.py:62
  321.4 7.7 %copy.45 = bf16[8,8,2,64,512]{4,3,2,1,0:T(8,128)(2,1)} copy(bf16[8,8,2,64,512]{4,3,1,0,2:T(8,128)(2,1)} %maximum_select_fusion) | data formatting | bytes 16777216 | tf_op jit(solution)/shard_map/jit(_where)/select_n | solution.py:62
  329.1 3.4 copy-done
  332.5 9.7 %shard_map.78 = bf16[1024,600]{1,0:T(8,128)(2,1)S(1)} custom-call(bf16[8,1024,512]{2,1,0:T(8,128)(2,1)S(1)} %bitcast.379, bf16[8,600,512]{2,1,0:T(8,128)(2,1)} %all-to-all-done.weights), custom_call_target="tpu_custom_call" | custom-call | flops 5033164800 | bytes 14532608 | tf_op jit(solution)/shard_map/pallas_call | solution.py:130
  342.2 42.8 %all_to_all.30 = bf16[16,64,600]{2,1,0:T(8,128)(2,1)} all-to-all(bf16[16,64,600]{2,1,0:T(8,128)(2,1)S(1)} %bitcast.383), channel_id=1, replica_groups=mesh['tv'=16,'sv'=8] {'tv'}, dimensions={0} | all-to-all | bytes 2457600 | tf_op jit(solution)/shard_map/all_to_all | solution.py:208
  385.0 5.7 %all-to-all-start.3 = ((bf16[8,2,64,600]{3,2,1,0:T(8,128)(2,1)}), bf16[8,2,64,600]{3,2,1,0:T(8,128)(2,1)S(1)}, u32[]{:S(2)}, u32[]{:S(2)}) async-start(bf16[8,2,64,600]{3,2,1,0:T(8,128)(2,1)} %bitcast.36), calls=%async_computation.3 | async-start | bytes 2621440 | tf_op jit(solution)/shard_map/all_to_all | solution.py:209
  390.7 3.4 copy-done.1
  394.1 10.8 %shard_map.79 = bf16[1024,600]{1,0:T(8,128)(2,1)} custom-call(bf16[8,1024,512]{2,1,0:T(8,128)(2,1)S(1)} %bitcast.380, bf16[8,600,512]{2,1,0:T(8,128)(2,1)} %all-to-all-done.1.weights), custom_call_target="tpu_custom_call" | custom-call | flops 5033164800 | bytes 14532608 | tf_op jit(solution)/shard_map/pallas_call | solution.py:130
  404.9 3.2 all-to-all-done.3
  408.1 6.3 %all-to-all-start.4 = ((bf16[16,64,600]{2,1,0:T(8,128)(2,1)}), bf16[16,64,600]{2,1,0:T(8,128)(2,1)}, u32[]{:S(2)}, u32[]{:S(2)}) async-start(bf16[16,64,600]{2,1,0:T(8,128)(2,1)} %bitcast.40), calls=%async_computation.4 | async-start | bytes 2621440 | tf_op jit(solution)/shard_map/all_to_all | solution.py:208
  414.4 4.6 add.389
  419.7 3.9 add.410
  423.9 2.0 copy-done.16
  425.9 6.8 %all-to-all-done.4 = bf16[16,64,600]{2,1,0:T(8,128)(2,1)} async-done(((bf16[16,64,600]{2,1,0:T(8,128)(2,1)}), bf16[16,64,600]{2,1,0:T(8,128)(2,1)}, u32[]{:S(2)}, u32[]{:S(2)}) %all-to-all-start.4) | async-done | bytes 1228832 | tf_op jit(solution)/shard_map/all_to_all | solution.py:208
  432.7 4.2 all-to-all-start.5
  436.9 5.4 select_convert_fusion
  442.3 3.0 collective-permute-start.12
  445.3 2.1 copy.51
  447.3 3.5 reshape.472
  450.9 3.4 all-to-all-done.5
  454.2 2.1 copy.50
  456.3 3.6 reshape.476
  459.9 2.0 pad_bitcast_fusion
  462.7 2.5 collective-permute-start.20
  466.4 16.0 %collective-permute-done.12 = s16[256,2432]{1,0:T(8,128)(2,1)} collective-permute-done((s16[256,2432]{1,0:T(8,128)(2,1)}, s16[256,2432]{1,0:T(8,128)(2,1)}, u32[]{:S(2)}, u32[]{:S(2)}) %collective-permute-start.12) | collective-permute-done | bytes 1245216 | tf_op jit(solution)/shard_map/ppermute | solution.py:28
  485.6 21.9 %collective-permute-done.20 = s16[256,2432]{1,0:T(8,128)(2,1)S(1)} collective-permute-done((s16[256,2432]{1,0:T(8,128)(2,1)S(1)}, s16[256,2432]{1,0:T(8,128)(2,1)S(1)}, u32[]{:S(2)}, u32[]{:S(2)}) %collective-permute-start.20) | collective-permute-done | bytes 1245216 | tf_op jit(solution)/shard_map/ppermute | solution.py:28
  509.7 3.2 collective-permute-start.14
  513.8 2.4 collective-permute-start.22
  516.6 11.3 %collective-permute-done.13 = s16[64,2432]{1,0:T(8,128)(2,1)S(1)} collective-permute-done((s16[64,2432]{1,0:T(8,128)(2,1)S(1)}, s16[64,2432]{1,0:T(8,128)(2,1)S(1)}, u32[]{:S(2)}, u32[]{:S(2)}) %collective-permute-start.13) | collective-permute-done | bytes 311328 | tf_op jit(solution)/shard_map/ppermute | solution.py:28
  529.1 9.6 %collective-permute-done.21 = s16[64,2432]{1,0:T(8,128)(2,1)S(1)} collective-permute-done((s16[64,2432]{1,0:T(8,128)(2,1)S(1)}, s16[64,2432]{1,0:T(8,128)(2,1)S(1)}, u32[]{:S(2)}, u32[]{:S(2)}) %collective-permute-start.21) | collective-permute-done | bytes 311328 | tf_op jit(solution)/shard_map/ppermute | solution.py:28
  540.4 2.7 multiply_reduce_fusion
  543.2 3.6 collective-permute-done.25
  551.9 3.3 collective-permute-done.28
  555.8 3.4 multiply_convert_fusion
  559.5 4.1 concatenate.33
  (180 shorter events, 52.4 us)
Async XLA Ops:
  2.7 11.0 %collective-permute-start = (bf16[144,512]{1,0:T(8,128)(2,1)S(1)}, bf16[144,512]{1,0:T(8,128)(2,1)S(1)}, u32[]{:S(2)}, u32[]{:S(2)}) collective-permute-start(bf16[144,512]{1,0:T(8,128)(2,1)S(1)} %constant_dynamic-update-slice_fusion), channel_id=1, source_target_pairs={{0,32},{1,33},{2,34},{3,35},{4,36},{5,37},{6,38},{7,39},{8,40},{9,... | collective-permute-start | bytes 442376 | tf_op jit(solution)/shard_map/ppermute | solution.py:28
  4.6 9.0 %collective-permute-start.1 = (bf16[144,512]{1,0:T(8,128)(2,1)S(1)}, bf16[144,512]{1,0:T(8,128)(2,1)S(1)}, u32[]{:S(2)}, u32[]{:S(2)}) collective-permute-start(bf16[144,512]{1,0:T(8,128)(2,1)S(1)} %constant_dynamic-update-slice_fusion), channel_id=1, source_target_pairs={{0,96},{1,97},{2,98},{3,99},{4,100},{5,101},{6,102},{7,103},{8,104... | collective-permute-start | bytes 442376 | tf_op jit(solution)/shard_map/ppermute | solution.py:28
  6.8 8.1 %collective-permute-start.2 = (bf16[144,512]{1,0:T(8,128)(2,1)S(1)}, bf16[144,512]{1,0:T(8,128)(2,1)S(1)}, u32[]{:S(2)}, u32[]{:S(2)}) collective-permute-start(bf16[144,512]{1,0:T(8,128)(2,1)S(1)} %constant_dynamic-update-slice_fusion), channel_id=1, source_target_pairs={{0,64},{1,65},{2,66},{3,67},{4,68},{5,69},{6,70},{7,71},{8,72},{9,... | collective-permute-start | bytes 442376 | tf_op jit(solution)/shard_map/ppermute | solution.py:28
  15.1 168.2 %all-to-all-start = ((bf16[8,600,512]{2,1,0:T(8,128)(2,1)}), bf16[8,600,512]{2,1,0:T(8,128)(2,1)}, u32[]{:S(2)}, u32[]{:S(2)}) async-start(bf16[8,600,512]{2,1,0:T(8,128)(2,1)} %bitcast.388), calls=%async_computation | async-start | bytes 9830400 | tf_op jit(solution)/shard_map/all_to_all | solution.py:245
  21.0 59.2 %collective-permute-start.3 = (bf16[4,64,512]{2,1,0:T(8,128)(2,1)S(1)}, bf16[4,64,512]{2,1,0:T(8,128)(2,1)S(1)}, u32[]{:S(2)}, u32[]{:S(2)}) collective-permute-start(bf16[4,64,512]{2,1,0:T(8,128)(2,1)S(1)} %constant_dynamic-slice_fusion.9), channel_id=1, source_target_pairs={{0,16},{1,17},{2,18},{3,19},{4,20},{5,21},{6,22},{7,23},{8,24},{9,... | collective-permute-start | bytes 786440 | tf_op jit(solution)/shard_map/ppermute | solution.py:28
  81.5 18.7 %collective-permute-start.4 = (bf16[832,512]{1,0:T(8,128)(2,1)S(1)}, bf16[832,512]{1,0:T(8,128)(2,1)S(1)}, u32[]{:S(2)}, u32[]{:S(2)}) collective-permute-start(bf16[832,512]{1,0:T(8,128)(2,1)S(1)} %get-tuple-element.96), channel_id=1, source_target_pairs={{0,4},{1,5},{2,6},{3,7},{4,0},{5,1},{6,2},{7,3},{8,12},{9,13},{10,... | collective-permute-start | bytes 2555912 | tf_op jit(solution)/shard_map/ppermute | solution.py:28
  100.1 11.6 %copy-start.17 = (bf16[832,512]{1,0:T(8,128)(2,1)}, bf16[832,512]{1,0:T(8,128)(2,1)S(1)}, u32[]{:S(2)}) copy-start(bf16[832,512]{1,0:T(8,128)(2,1)S(1)} %collective-permute-done.4) | copy-start | bytes 2555908
  101.6 73.4 %collective-permute-start.5 = (bf16[2,832,512]{2,1,0:T(8,128)(2,1)}, bf16[2,832,512]{2,1,0:T(8,128)(2,1)}, u32[]{:S(2)}, u32[]{:S(2)}) collective-permute-start(bf16[2,832,512]{2,1,0:T(8,128)(2,1)} %maximum_select_fusion.1), channel_id=1, source_target_pairs={{0,3},{1,0},{2,1},{3,2},{4,7},{5,4},{6,5},{7,6},{8,11},{9,8},{10,9... | collective-permute-start | bytes 5111816 | tf_op jit(solution)/shard_map/ppermute | solution.py:28
  104.6 73.2 %collective-permute-start.6 = (bf16[2,832,512]{2,1,0:T(8,128)(2,1)}, bf16[2,832,512]{2,1,0:T(8,128)(2,1)}, u32[]{:S(2)}, u32[]{:S(2)}) collective-permute-start(bf16[2,832,512]{2,1,0:T(8,128)(2,1)} %maximum_select_fusion.1), channel_id=1, source_target_pairs={{0,2},{1,3},{2,0},{3,1},{4,6},{5,7},{6,4},{7,5},{8,10},{9,11},{10,... | collective-permute-start | bytes 5111816 | tf_op jit(solution)/shard_map/ppermute | solution.py:28
  105.2 75.3 %collective-permute-start.7 = (bf16[2,832,512]{2,1,0:T(8,128)(2,1)}, bf16[2,832,512]{2,1,0:T(8,128)(2,1)}, u32[]{:S(2)}, u32[]{:S(2)}) collective-permute-start(bf16[2,832,512]{2,1,0:T(8,128)(2,1)} %maximum_select_fusion.1), channel_id=1, source_target_pairs={{0,1},{1,2},{2,3},{3,0},{4,5},{5,6},{6,7},{7,4},{8,9},{9,10},{10,1... | collective-permute-start | bytes 5111816 | tf_op jit(solution)/shard_map/ppermute | solution.py:28
  125.7 97.2 %collective-permute-start.10 = (bf16[320,2400]{1,0:T(8,128)(2,1)}, bf16[320,2400]{1,0:T(8,128)(2,1)S(1)}, u32[]{:S(2)}, u32[]{:S(2)}) collective-permute-start(bf16[320,2400]{1,0:T(8,128)(2,1)} %get-tuple-element.76), channel_id=1, source_target_pairs={{0,64},{1,65},{2,66},{3,67},{4,68},{5,69},{6,70},{7,71},{8,72},{9,... | collective-permute-start | bytes 4608008 | tf_op jit(solution)/shard_map/ppermute | solution.py:28
  126.8 98.6 %collective-permute-start.8 = (bf16[320,2400]{1,0:T(8,128)(2,1)}, bf16[320,2400]{1,0:T(8,128)(2,1)S(1)}, u32[]{:S(2)}, u32[]{:S(2)}) collective-permute-start(bf16[320,2400]{1,0:T(8,128)(2,1)} %get-tuple-element.78), channel_id=1, source_target_pairs={{0,32},{1,33},{2,34},{3,35},{4,36},{5,37},{6,38},{7,39},{8,40},{9,... | collective-permute-start | bytes 4608008 | tf_op jit(solution)/shard_map/ppermute | solution.py:28
  183.3 112.1 %all-to-all-start.1 = ((bf16[8,600,512]{2,1,0:T(8,128)(2,1)}), bf16[8,600,512]{2,1,0:T(8,128)(2,1)}, u32[]{:S(2)}, u32[]{:S(2)}) async-start(bf16[8,600,512]{2,1,0:T(8,128)(2,1)} %bitcast.389), calls=%async_computation.1 | async-start | bytes 9830400 | tf_op jit(solution)/shard_map/all_to_all | solution.py:250
  196.1 5.7 %copy-start.18 = (bf16[832,512]{1,0:T(8,128)(2,1)S(1)}, bf16[832,512]{1,0:T(8,128)(2,1)}, u32[]{:S(2)}) copy-start(bf16[832,512]{1,0:T(8,128)(2,1)} %copy-done.17) | copy-start | bytes 2555908
  196.1 5.7 %copy-start.19 = (bf16[1,1,832,512]{3,2,1,0:T(8,128)(2,1)S(1)}, bf16[1,1,832,512]{3,2,1,0:T(8,128)(2,1)}, u32[]{:S(2)}) copy-start(bf16[1,1,832,512]{3,2,1,0:T(8,128)(2,1)} %get-tuple-element.94) | copy-start | bytes 2555908
  208.5 102.4 %collective-permute-start.24 = (bf16[8,8,64,512]{3,2,1,0:T(8,128)(2,1)}, bf16[8,8,64,512]{3,2,1,0:T(8,128)(2,1)}, u32[]{:S(2)}, u32[]{:S(2)}) collective-permute-start(bf16[8,8,64,512]{3,2,1,0:T(8,128)(2,1)} %bitcast.32), channel_id=1, source_target_pairs={{0,8},{1,9},{2,10},{3,11},{4,12},{5,13},{6,14},{7,15},{8,0},{9,1},... | collective-permute-start | bytes 12582920 | tf_op jit(solution)/shard_map/ppermute | solution.py:28
  208.5 37.2 %collective-permute-start.9 = (bf16[320,2400]{1,0:T(8,128)(2,1)}, bf16[320,2400]{1,0:T(8,128)(2,1)}, u32[]{:S(2)}, u32[]{:S(2)}) collective-permute-start(bf16[320,2400]{1,0:T(8,128)(2,1)} %get-tuple-element.77), channel_id=1, source_target_pairs={{0,96},{1,97},{2,98},{3,99},{4,100},{5,101},{6,102},{7,103},{8,104... | collective-permute-start | bytes 4608008 | tf_op jit(solution)/shard_map/ppermute | solution.py:28
  219.5 1.4 copy-start.22
  219.5 4.6 copy-start.21
  219.5 6.9 %copy-start.20 = (bf16[320,2348]{1,0:T(8,128)(2,1)S(1)}, bf16[320,2348]{1,0:T(8,128)(2,1)}, u32[]{:S(2)}) copy-start(bf16[320,2348]{1,0:T(8,128)(2,1)} %get-tuple-element.35) | copy-start | bytes 4508164
  220.9 71.0 %collective-permute-start.16 = (bf16[320,2348]{1,0:T(8,128)(2,1)S(1)}, bf16[320,2348]{1,0:T(8,128)(2,1)S(1)}, u32[]{:S(2)}, u32[]{:S(2)}) collective-permute-start(bf16[320,2348]{1,0:T(8,128)(2,1)S(1)} %copy-done.22), channel_id=1, source_target_pairs={{0,32},{1,33},{2,34},{3,35},{4,36},{5,37},{6,38},{7,39},{8,40},{9,... | collective-permute-start | bytes 4508168 | tf_op jit(solution)/shard_map/ppermute | solution.py:28
  222.9 1.2 copy-start.4
  224.1 69.0 %collective-permute-start.17 = (bf16[320,2348]{1,0:T(8,128)(2,1)S(1)}, bf16[320,2348]{1,0:T(8,128)(2,1)S(1)}, u32[]{:S(2)}, u32[]{:S(2)}) collective-permute-start(bf16[320,2348]{1,0:T(8,128)(2,1)S(1)} %copy-done.21), channel_id=1, source_target_pairs={{0,96},{1,97},{2,98},{3,99},{4,100},{5,101},{6,102},{7,103},{8,104... | collective-permute-start | bytes 4508168 | tf_op jit(solution)/shard_map/ppermute | solution.py:28
  225.3 1.1 copy-start.6
  226.5 67.8 %collective-permute-start.18 = (bf16[320,2348]{1,0:T(8,128)(2,1)S(1)}, bf16[320,2348]{1,0:T(8,128)(2,1)S(1)}, u32[]{:S(2)}, u32[]{:S(2)}) collective-permute-start(bf16[320,2348]{1,0:T(8,128)(2,1)S(1)} %copy-done.20), channel_id=1, source_target_pairs={{0,64},{1,65},{2,66},{3,67},{4,68},{5,69},{6,70},{7,71},{8,72},{9,... | collective-permute-start | bytes 4508168 | tf_op jit(solution)/shard_map/ppermute | solution.py:28
  228.1 17.6 %copy-start.3 = (bf16[320,2400]{1,0:T(8,128)(2,1)S(1)}, bf16[320,2400]{1,0:T(8,128)(2,1)}, u32[]{:S(2)}) copy-start(bf16[320,2400]{1,0:T(8,128)(2,1)} %get-tuple-element.79.w0) | copy-start | bytes 4608004
  228.1 17.6 %copy-start.5 = (bf16[320,2400]{1,0:T(8,128)(2,1)S(1)}, bf16[320,2400]{1,0:T(8,128)(2,1)}, u32[]{:S(2)}) copy-start(bf16[320,2400]{1,0:T(8,128)(2,1)} %copy-done.4) | copy-start | bytes 4608004
  228.1 17.6 %copy-start.7 = (bf16[320,2400]{1,0:T(8,128)(2,1)S(1)}, bf16[320,2400]{1,0:T(8,128)(2,1)}, u32[]{:S(2)}) copy-start(bf16[320,2400]{1,0:T(8,128)(2,1)} %copy-done.6) | copy-start | bytes 4608004
  256.2 158.1 %collective-permute-start.11 = (f32[512,2432]{1,0:T(8,128)}, f32[512,2432]{1,0:T(8,128)}, u32[]{:S(2)}, u32[]{:S(2)}) collective-permute-start(f32[512,2432]{1,0:T(8,128)} %get-tuple-element.30), channel_id=1, source_target_pairs={{0,8},{1,9},{2,10},{3,11},{4,12},{5,13},{6,14},{7,15},{8,0},{9,1},... | collective-permute-start | bytes 14942216 | tf_op jit(solution)/shard_map/ppermute | solution.py:28
  291.9 1.1 copy-start.8
  293.1 1.1 copy-start.10
  294.2 1.1 copy-start.12
  295.4 1.4 copy-start.2
  296.8 1.4 copy-start.9
  298.2 1.4 copy-start.11
  299.6 1.4 copy-start.13
  310.9 108.3 %collective-permute-start.19 = (f32[512,2432]{1,0:T(8,128)}, f32[512,2432]{1,0:T(8,128)}, u32[]{:S(2)}, u32[]{:S(2)}) collective-permute-start(f32[512,2432]{1,0:T(8,128)} %get-tuple-element.42), channel_id=1, source_target_pairs={{0,8},{1,9},{2,10},{3,11},{4,12},{5,13},{6,14},{7,15},{8,0},{9,1},... | collective-permute-start | bytes 14942216 | tf_op jit(solution)/shard_map/ppermute | solution.py:28
  329.1 3.4 copy-start
  385.0 23.0 %all-to-all-start.3 = ((bf16[8,2,64,600]{3,2,1,0:T(8,128)(2,1)}), bf16[8,2,64,600]{3,2,1,0:T(8,128)(2,1)S(1)}, u32[]{:S(2)}, u32[]{:S(2)}) async-start(bf16[8,2,64,600]{3,2,1,0:T(8,128)(2,1)} %bitcast.36), calls=%async_computation.3 | async-start | bytes 2621440 | tf_op jit(solution)/shard_map/all_to_all | solution.py:209
  390.7 3.4 copy-start.1
  408.1 24.6 %all-to-all-start.4 = ((bf16[16,64,600]{2,1,0:T(8,128)(2,1)}), bf16[16,64,600]{2,1,0:T(8,128)(2,1)}, u32[]{:S(2)}, u32[]{:S(2)}) async-start(bf16[16,64,600]{2,1,0:T(8,128)(2,1)} %bitcast.40), calls=%async_computation.4 | async-start | bytes 2621440 | tf_op jit(solution)/shard_map/all_to_all | solution.py:208
  414.4 5.1 slice-start.4
  414.4 5.3 slice-start.5
  418.9 4.7 copy-start.15
  423.6 2.3 copy-start.16
  432.7 21.5 %all-to-all-start.5 = ((bf16[8,2,64,600]{3,2,1,0:T(8,128)(2,1)}), bf16[8,2,64,600]{3,2,1,0:T(8,128)(2,1)S(1)}, u32[]{:S(2)}, u32[]{:S(2)}) async-start(bf16[8,2,64,600]{3,2,1,0:T(8,128)(2,1)} %bitcast.41), calls=%async_computation.5 | async-start | bytes 2621440 | tf_op jit(solution)/shard_map/all_to_all | solution.py:209
  442.3 40.1 %collective-permute-start.12 = (s16[256,2432]{1,0:T(8,128)(2,1)}, s16[256,2432]{1,0:T(8,128)(2,1)}, u32[]{:S(2)}, u32[]{:S(2)}) collective-permute-start(s16[256,2432]{1,0:T(8,128)(2,1)} %get-tuple-element.110), channel_id=1, source_target_pairs={{0,16},{1,17},{2,18},{3,19},{4,20},{5,21},{6,22},{7,23},{8,24},{9,... | collective-permute-start | bytes 3735560 | tf_op jit(solution)/shard_map/ppermute | solution.py:28
  456.3 27.1 %slice-start = ((s8[4980736]{0:T(1024)(128)(4,1)}), s8[786432]{0:T(1024)(128)(4,1)S(1)}, s32[]{:S(2)}) async-start(s8[4980736]{0:T(1024)(128)(4,1)} %bitcast.384), calls=%async_computation.6 | async-start | bytes 1572864
  459.9 2.8 copy-start.23
  459.9 23.6 %slice-start.1 = ((s8[4980736]{0:T(1024)(128)(4,1)}), s8[4194304]{0:T(1024)(128)(4,1)S(1)}, s32[]{:S(2)}) async-start(s8[4980736]{0:T(1024)(128)(4,1)} %bitcast.384), calls=%async_computation.7 | async-start | bytes 8388608
  462.7 44.7 %collective-permute-start.20 = (s16[256,2432]{1,0:T(8,128)(2,1)S(1)}, s16[256,2432]{1,0:T(8,128)(2,1)S(1)}, u32[]{:S(2)}, u32[]{:S(2)}) collective-permute-start(s16[256,2432]{1,0:T(8,128)(2,1)S(1)} %copy-done.23), channel_id=1, source_target_pairs={{0,16},{1,17},{2,18},{3,19},{4,20},{5,21},{6,22},{7,23},{8,24},{9,... | collective-permute-start | bytes 3735560 | tf_op jit(solution)/shard_map/ppermute | solution.py:28
  465.2 42.4 %slice-start.2 = ((s8[4980736]{0:T(1024)(128)(4,1)}), s8[4194304]{0:T(1024)(128)(4,1)S(1)}, s32[]{:S(2)}) async-start(s8[4980736]{0:T(1024)(128)(4,1)} %bitcast.386), calls=%async_computation.8 | async-start | bytes 8388608
  483.4 24.2 %slice-start.3 = ((s8[4980736]{0:T(1024)(128)(4,1)}), s8[786432]{0:T(1024)(128)(4,1)S(1)}, s32[]{:S(2)}) async-start(s8[4980736]{0:T(1024)(128)(4,1)} %bitcast.386), calls=%async_computation.9 | async-start | bytes 1572864
  509.6 18.2 %collective-permute-start.13 = (s16[64,2432]{1,0:T(8,128)(2,1)S(1)}, s16[64,2432]{1,0:T(8,128)(2,1)S(1)}, u32[]{:S(2)}, u32[]{:S(2)}) collective-permute-start(s16[64,2432]{1,0:T(8,128)(2,1)S(1)} %get-tuple-element.107), channel_id=1, source_target_pairs={{0,32},{1,33},{2,34},{3,35},{4,36},{5,37},{6,38},{7,39},{8,40},{9,... | collective-permute-start | bytes 933896 | tf_op jit(solution)/shard_map/ppermute | solution.py:28
  509.7 18.6 %collective-permute-start.14 = (s16[64,2432]{1,0:T(8,128)(2,1)S(1)}, s16[64,2432]{1,0:T(8,128)(2,1)S(1)}, u32[]{:S(2)}, u32[]{:S(2)}) collective-permute-start(s16[64,2432]{1,0:T(8,128)(2,1)S(1)} %get-tuple-element.106), channel_id=1, source_target_pairs={{0,96},{1,97},{2,98},{3,99},{4,100},{5,101},{6,102},{7,103},{8,104... | collective-permute-start | bytes 933896 | tf_op jit(solution)/shard_map/ppermute | solution.py:28
  512.9 15.6 %collective-permute-start.15 = (s16[64,2432]{1,0:T(8,128)(2,1)S(1)}, s16[64,2432]{1,0:T(8,128)(2,1)S(1)}, u32[]{:S(2)}, u32[]{:S(2)}) collective-permute-start(s16[64,2432]{1,0:T(8,128)(2,1)S(1)} %get-tuple-element.108), channel_id=1, source_target_pairs={{0,64},{1,65},{2,66},{3,67},{4,68},{5,69},{6,70},{7,71},{8,72},{9,... | collective-permute-start | bytes 933896 | tf_op jit(solution)/shard_map/ppermute | solution.py:28
  512.9 25.8 %collective-permute-start.21 = (s16[64,2432]{1,0:T(8,128)(2,1)S(1)}, s16[64,2432]{1,0:T(8,128)(2,1)S(1)}, u32[]{:S(2)}, u32[]{:S(2)}) collective-permute-start(s16[64,2432]{1,0:T(8,128)(2,1)S(1)} %get-tuple-element.81), channel_id=1, source_target_pairs={{0,32},{1,33},{2,34},{3,35},{4,36},{5,37},{6,38},{7,39},{8,40},{9,... | collective-permute-start | bytes 933896 | tf_op jit(solution)/shard_map/ppermute | solution.py:28
  513.8 25.1 %collective-permute-start.22 = (s16[64,2432]{1,0:T(8,128)(2,1)S(1)}, s16[64,2432]{1,0:T(8,128)(2,1)S(1)}, u32[]{:S(2)}, u32[]{:S(2)}) collective-permute-start(s16[64,2432]{1,0:T(8,128)(2,1)S(1)} %get-tuple-element.82), channel_id=1, source_target_pairs={{0,96},{1,97},{2,98},{3,99},{4,100},{5,101},{6,102},{7,103},{8,104... | collective-permute-start | bytes 933896 | tf_op jit(solution)/shard_map/ppermute | solution.py:28
  527.9 11.3 %collective-permute-start.23 = (s16[64,2432]{1,0:T(8,128)(2,1)S(1)}, s16[64,2432]{1,0:T(8,128)(2,1)S(1)}, u32[]{:S(2)}, u32[]{:S(2)}) collective-permute-start(s16[64,2432]{1,0:T(8,128)(2,1)S(1)} %get-tuple-element.80), channel_id=1, source_target_pairs={{0,64},{1,65},{2,66},{3,67},{4,68},{5,69},{6,70},{7,71},{8,72},{9,... | collective-permute-start | bytes 933896 | tf_op jit(solution)/shard_map/ppermute | solution.py:28
  539.7 3.4 copy-start.14
  543.1 3.7 collective-permute-start.25
  546.8 5.1 collective-permute-start.26
  548.3 3.6 collective-permute-start.27
  550.1 5.1 collective-permute-start.28
  (1 other events, 0.9 us)

commit v3 on v2

--- a/solution.py
+++ b/solution.py
@@ -108,42 +108,50 @@
     )(hidden, *weights)
 
 
-def teacher_kernel(hidden, weights, logits, total):
-    k = pl.program_id(0)
+def teacher_kernel(words, here, hidden, weights, theirs, ours, total):
+    half, k = pl.program_id(0), pl.program_id(1)
 
     @pl.when(k == 0)
     def _():
         total[...] = jnp.zeros_like(total)
 
-    total[...] += lax.dot_general(
+    total[:, :words] += lax.dot_general(
         hidden[0], weights[0], (((1,), (1,)), ((), ())), preferred_element_type=F32
     )
 
-    @pl.when(k == pl.num_programs(0) - 1)
+    @pl.when((k == pl.num_programs(1) - 1) & (half == 0))
     def _():
-        logits[...] = total[...].astype(BF16)
-
-
-def teacher_product(hidden, weights):
+        theirs[...] = total[...]
+
+    @pl.when((k == pl.num_programs(1) - 1) & (half == 1))
+    def _():
+        ours[...] = total[...]
+
+
+def teacher_partial(hidden, weights, xl, padded):
     steps, rows, depth = hidden.shape
-    words = weights.shape[1]
+    words = weights.shape[1] // 2
+    block = pl.BlockSpec((rows, padded), lambda h, k, here: (0, 0))
     return pl.pallas_call(
-        teacher_kernel,
-        grid=(steps,),
-        in_specs=[
-            pl.BlockSpec((1, rows, depth), lambda k: (k, 0, 0)),
-            pl.BlockSpec((1, words, depth), lambda k: (k, 0, 0)),
-        ],
-        out_specs=pl.BlockSpec((rows, words), lambda k: (0, 0)),
-        out_shape=jax.ShapeDtypeStruct((rows, words), BF16),
-        scratch_shapes=[pltpu.VMEM((rows, words), F32)],
+        functools.partial(teacher_kernel, words),
+        grid_spec=pltpu.PrefetchScalarGridSpec(
+            num_scalar_prefetch=1,
+            grid=(2, steps),
+            in_specs=[
+                pl.BlockSpec((1, rows, depth), lambda h, k, here: (k, 0, 0)),
+                pl.BlockSpec((1, words, depth), lambda h, k, here: (k, (h + here[0] + 1) % 2, 0)),
+            ],
+            out_specs=[block, block],
+            scratch_shapes=[pltpu.VMEM((rows, padded), F32)],
+        ),
+        out_shape=[jax.ShapeDtypeStruct((rows, padded), F32)] * 2,
         compiler_params=pltpu.CompilerParams(vmem_limit_bytes=40 << 20),
         cost_estimate=pl.CostEstimate(
-            flops=2 * steps * rows * depth * words,
-            bytes_accessed=2 * steps * depth * (rows + words) + 2 * rows * words,
+            flops=4 * steps * rows * depth * words,
+            bytes_accessed=2 * steps * depth * 2 * (rows + words) + 8 * rows * padded,
             transcendentals=0,
         ),
-    )(hidden, weights)
+    )(xl.reshape(1).astype(jnp.int32), hidden, weights)
 
 
 def student_rows(hidden, z, xh, c):
@@ -166,15 +174,13 @@
 def all_rows(stage, teacher_shape, student_shape, z, xh, c, xl, y):
     rows, width = teacher_shape
     s_rows, s_depth = student_shape
-    teacher = ordered([part[:rows] for part in stage], z)
-    teacher = paired(teacher, other_xh, xh, axis=1)
     student = jnp.concatenate([part[rows:].reshape(s_rows, s_depth) for part in stage], axis=1)
-    pack = jnp.concatenate([teacher.reshape(-1, width), student.reshape(-1, width)])
-    pack = ordered(ring(paired(pack, other_xl, xl), along_y), y)
-    student = pack[:, :, 8 * rows:].reshape(4, 2, s_rows, 4 * s_depth)
-    teacher = pack[:, :, :8 * rows].transpose(1, 0, 2, 3).reshape(8, 8, rows, width)
-    teacher = paired(teacher, other_core, c, axis=2)
-    return teacher.reshape(8, 16 * rows, width), student_rows(student, z, xh, c)
+    student = paired(student, other_xl, xl)
+    teacher = ordered(ring(ordered([part[:rows] for part in stage], z), along_y), y)
+    student = ordered(ring(student, along_y), y)
+    teacher = paired(teacher.reshape(16, rows, width), other_xh, xh, axis=1)
+    teacher = paired(teacher.reshape(32, rows, width), other_core, c, axis=1)
+    return teacher.reshape(4, 16 * rows, width), student_rows(student, z, xh, c)
 
 
 def student_pieces(student_head, z, start, words):
@@ -189,27 +195,42 @@
     return [p if d == 0 else moved(p, along_z(d)) for d, p in zip(SHIFTS, pieces)]
 
 
-def student_logits(hidden, weights, padded):
+def student_halves(hidden, weights, padded):
     theirs, ours = student_partial(hidden, weights, padded)
     ours = ours + moved(theirs, other_core)
     half = ours.shape[0] // 2
-    rows = half // 4
-    full = ours[:half] + decoded(moved(coded(ours[half:]), other_xh))
-    parts = []
-    for d in SHIFTS:
-        part = full[d * rows:(d + 1) * rows]
-        parts.append(part if d == 0 else decoded(moved(coded(part), along_z(d))))
-    return parts
-
-
-def teacher_logits(hidden, weights, padded):
-    logits = teacher_product(hidden, weights)
+    return ours[:half], moved(coded(ours[half:]), other_xh)
+
+
+def student_logits(ours, theirs):
+    full = ours + decoded(theirs)
+    rows = full.shape[0] // 4
+    parts = [full[k * rows:(k + 1) * rows] for k in range(4)]
+    return [parts[0]] + [moved(coded(parts[d]), along_z(d)) for d in SHIFTS[1:]]
+
+
+def teacher_logits(ours, theirs):
+    return (ours + decoded(theirs)).astype(BF16)
+
+
+def teacher_place(logits, chunk, padded):
     rows, part = logits.shape[0] // 16, logits.shape[1]
     logits = lax.all_to_all(logits.reshape(16, rows, part), "tv", 0, 0, tiled=True)
     logits = lax.all_to_all(logits.reshape(8, 2, rows, part), "sv", 0, 0, tiled=True)
-    logits = logits.reshape(GROUPS, 4, 2, rows, part).transpose(2, 0, 3, 1, 4)
-    logits = logits.reshape(2, GROUPS, rows, 4 * part)
-    return jnp.pad(logits, ((0, 0), (0, 0), (0, 0), (0, padded - 4 * part)))
+    logits = logits.reshape(2, GROUPS, 2, 2, rows, part)[..., :chunk].transpose(3, 1, 4, 2, 0, 5)
+    logits = logits.reshape(2, GROUPS, rows, 4 * chunk)
+    return jnp.pad(logits, ((0, 0), (0, 0), (0, 0), (0, padded - 4 * chunk)))
+
+
+def tiled_rows(rows, chunk):
+    rows = rows.reshape(4, 2, chunk, -1)
+    rows = jnp.pad(rows, ((0, 0), (0, 0), (0, -chunk % 16), (0, 0)))
+    return rows.reshape(4, 2 * rows.shape[2], -1)
+
+
+def over_y(pieces):
+    groups = [[0, 1, 2, 3], [4, 5, 6, 7]]
+    return lax.all_to_all(pieces, "sv", 0, 0, axis_index_groups=groups, tiled=True)
 
 
 def pooled(a, b):
@@ -236,26 +257,47 @@
     chunk = -(-quarter // 64) * 8
     sizes = (4 * chunk, quarter - 4 * chunk)
     padded = (4 * chunk // 128 + 1) * 128
+    t_padded = (chunk // 128 + 1) * 128
+    barrier = lax.optimization_barrier
+    xl = here[3]
+
     stage = first_stage(teacher_hidden, student_hidden)
     tall = teacher_head.T
-    t_first = tall[:8 * chunk].reshape(8, chunk, -1)
-    t_second = jnp.pad(tall[quarter:], ((0, 8 * chunk - quarter), (0, 0))).reshape(8, chunk, -1)
-    student_head, stage, t_first = lax.optimization_barrier((student_head, stage, t_first))
+    t_first = tiled_rows(tall[:8 * chunk], chunk)
     s_first = student_pieces(student_head, z, 0, sizes[0])
-    t_first = lax.all_to_all(t_first, "sv", 0, 0, tiled=True)
+    stage, t_first, s_first = barrier((stage, t_first, s_first))
     s_first = sent(s_first)
+    t_first = over_y(t_first)
     t_hidden, s_hidden = all_rows(stage, teacher_hidden.shape, student_hidden.shape, *here)
+
+    t_second = jnp.pad(tall[quarter:], ((0, 8 * chunk - quarter), (0, 0)))
+    t_second = tiled_rows(t_second, chunk)
     s_second = student_pieces(student_head, z, sizes[0], sizes[1])
-    s_second, t_second, t_first = lax.optimization_barrier((s_second, t_second, t_first))
-    t_second = lax.all_to_all(t_second, "sv", 0, 0, tiled=True)
+    s_second, t_second, s_first, t_first, t_hidden, s_hidden = barrier(
+        (s_second, t_second, s_first, t_first, t_hidden, s_hidden)
+    )
     s_second = sent(s_second)
-    s_second, t_second = lax.optimization_barrier((s_second, t_second))
-    teacher = [teacher_logits(t_hidden, w, padded) for w in (t_first, t_second)]
-    teacher = jnp.stack(teacher, axis=1).reshape(4, GROUPS, -1, padded).astype(F32)
-    groups = [student_logits(s_hidden, w, padded) for w in (s_first, s_second)]
+    t_second = over_y(t_second)
+    t_theirs, t_ours = teacher_partial(t_hidden, t_first, xl, t_padded)
+    t_first = t_ours, moved(coded(t_theirs), other_xl)
+    s_first = student_halves(s_hidden, s_first, padded)
+
+    s_second, t_second, t_first, s_first = barrier((s_second, t_second, t_first, s_first))
+    t_theirs, t_ours = teacher_partial(t_hidden, t_second, xl, t_padded)
+    t_theirs, t_ours, s_second = barrier((t_theirs, t_ours, s_second))
+    t_second = t_ours, moved(coded(t_theirs), other_xl)
+    t_first = teacher_place(teacher_logits(*t_first), chunk, padded)
+    s_first = student_logits(*s_first)
+    s_second = student_halves(s_hidden, s_second, padded)
+    t_second, t_first, s_first, s_second = barrier((t_second, t_first, s_first, s_second))
+    t_second = teacher_place(teacher_logits(*t_second), chunk, padded)
+    s_second = student_logits(*s_second)
+
+    teacher = jnp.stack([t_first, t_second], axis=1).reshape(4, GROUPS, -1, padded).astype(F32)
     student = jnp.zeros(teacher.shape, F32)
-    for g, parts in enumerate(groups):
+    for g, parts in enumerate((s_first, s_second)):
         for d, part in zip(SHIFTS, parts):
+            part = part if d == 0 else decoded(part)
             student = lax.dynamic_update_slice(student, part[None, None], ((z - d) % 4, g, 0, 0))
     column = lax.broadcasted_iota(jnp.int32, student.shape, 3)
     group = lax.broadcasted_iota(jnp.int32, student.shape, 1)

time: 575 us -> 509 us (0.89)
  blocking collectives: 42.8 us -> 0 us
  starting transfers between devices: 63.8 us -> 97.8 us
  waiting for transfers between devices: 247 us -> 214 us
  local copies, waits for them, and re-layouts: 117 us -> 85.6 us
  other arithmetic: 51.8 us -> 58.4 us
    ppermute x29 -> x34, waiting for transfers between devices: 233 us -> 170 us  [moved(): return lax.ppermute(x, AXES, pairs)]
    all_to_all x1 -> x0, blocking collectives: 42.8 us -> none  [teacher_logits(): lax.all_to_all(logits.reshape(16, rows, part), 'tv', 0, 0, tiled=True)]
    all_to_all x5 -> x6, waiting for transfers between devices: 13.4 us -> 44.4 us  [the longest x2 30.4 us: teacher_place(): lax.all_to_all(logits.reshape(8, 2, rows, part), 'sv', 0, 0, tiled=True)]
    all_to_all x5 -> x6, starting transfers between devices: 28.5 us -> 51.7 us  [the longest x2 22.1 us: over_y(): lax.all_to_all(pieces, 'sv', 0, 0, axis_index_groups=groups, tiled=True)]
    unnamed x77 -> x100, local copies, waits for them, and re-layouts: 40 us -> 26.2 us
    ppermute x29 -> x34, starting transfers between devices: 35.3 us -> 46.1 us  [moved(): return lax.ppermute(x, AXES, pairs)]
    select_n x3, other arithmetic: 12 us -> 2.44 us  [paired(): jnp.where(here == 0, jnp.stack([x, other], axis=axis), jnp.stack([other,...]
    pad x1 -> x4, local copies, waits for them, and re-layouts: 4.92 us -> 13 us  [the longest x2 7.88 us: tiled_rows(): rows = jnp.pad(rows, ((0, 0), (0, 0), (0, -chunk % 16), (0, 0)))]
  transfers between devices with their start and end apart: 34 -> 40, of which waited for: 15 -> 16; matrix products, arithmetic and copies ran while one was open for 23% -> 20% of each run, Pallas kernels for 7% -> 2%
where the time goes in v3:
time: 509 us; the launch traced here: 499 us
  waiting for transfers between devices  214 us (42%)
  starting transfers between devices  97.8 us (19%)
  local copies, waits for them, and re-layouts  85.6 us (17%)
  other arithmetic  58.4 us (11%)
  Pallas kernels  41.2 us (8%)
    ppermute x34, waiting for transfers between devices, moved(): return lax.ppermute(x, AXES, pairs)  170 us
    ppermute x34, starting transfers between devices, moved(): return lax.ppermute(x, AXES, pairs)  46.1 us
    all_to_all x2, waiting for transfers between devices, teacher_place(): lax.all_to_all(logits.reshape(8, 2, rows, part), 'sv', 0, 0, tiled=True)  30.4 us
    unnamed x100, local copies, waits for them, and re-layouts  26.2 us
    all_to_all x2, starting transfers between devices, over_y(): lax.all_to_all(pieces, 'sv', 0, 0, axis_index_groups=groups, tiled=True)  22.1 us
    pallas_call x2, Pallas kernels, teacher_partial(): pl.pallas_call(functools.partial(teacher_kernel, words), grid_spec=pltpu....  20.7 us
    pallas_call x2, Pallas kernels, student_partial(): pl.pallas_call(functools.partial(student_kernel, words), grid=(pl.cdiv(pa...  20.5 us
    dynamic_slice x2, local copies, waits for them, and re-layouts, student_pieces(): lax.dynamic_slice_in_dim(student_head, (z + d) % 4 * quarter + start, wor...  18.2 us
  transfers between devices with their start and end apart: 40, of which 16 were waited for; matrix products, arithmetic and copies ran while one was open for 20% of the time, Pallas kernels for 2%

profile of v3, /device:TPU:6, one launch (start us, length us, event | category | flops | bytes accessed | tf_op | source)
XLA Modules:
  0.0 498.8 jit_solution(8423353800189257363)
XLA Ops:
  2.7 2.0 collective-permute-start
  4.6 2.2 collective-permute-start.1
  6.8 1.8 collective-permute-start.2
  8.6 9.1 %constant_dynamic-slice_fusion.3 = (bf16[320,2400]{1,0:T(8,128)(2,1)}, bf16[320,2400]{1,0:T(8,128)(2,1)}, bf16[320,2400]{1,0:T(8,128)(2,1)}, bf16[320,2400]{1,0:T(8,128)(2,1)}) fusion(bf16[320,18992]{1,0:T(8,128)(2,1)} %param.8, s32[]{:T(128)S(6)} %select_n.264, s32[]{:T(128)S(6)} %select_n.262, s32[]{:T(128)S(6)} %select_n.261, s32[]{:T(128)S(6)} %select_n.263), kind=kLoop, calls=%fused_computation.110 | loop fusion | bytes 12288016 | tf_op jit(solution)/shard_map/dynamic_slice | solution.py:189
  17.8 4.9 slice.273
  22.7 5.1 %pad.20 = bf16[4,2,608,512]{3,2,1,0:T(8,128)(2,1)} pad(bf16[4,2,600,512]{3,2,1,0:T(8,128)(2,1)} %bitcast.398, bf16[]{:T(256)} %constant.168.clone.1), padding=0_0x0_0x0_8x0_0 | pad | bytes 9895938 | tf_op jit(solution)/shard_map/jit(_pad)/pad | solution.py:227
  28.0 3.1 collective-permute-start.6
  31.7 9.0 %constant_dynamic-slice_fusion.7 = (bf16[320,2348]{1,0:T(8,128)(2,1)}, bf16[320,2348]{1,0:T(8,128)(2,1)}, bf16[320,2348]{1,0:T(8,128)(2,1)}, bf16[320,2348]{1,0:T(8,128)(2,1)}) fusion(bf16[320,18992]{1,0:T(8,128)(2,1)} %param.8, s32[]{:T(128)S(6)} %select_n.260, s32[]{:T(128)S(6)} %select_n.258, s32[]{:T(128)S(6)} %select_n.256, s32[]{:T(128)S(6)} %select_n.254), kind=kLoop, calls=%fused_computation.114 | loop fusion | bytes 12021776 | tf_op jit(solution)/shard_map/dynamic_slice | solution.py:189
  40.7 5.8 %slice.272 = bf16[4748,512]{1,0:T(8,128)(2,1)} slice(bf16[9496,512]{1,0:T(8,128)(2,1)} %bitcast.403), slice={[4748:9496], [0:512]} | slice | bytes 9723904 | tf_op jit(solution)/shard_map/slice | solution.py:273
  46.5 2.7 pad.18
  49.2 2.7 pad.19
  56.1 5.0 %all-to-all-start = ((bf16[4,1216,512]{2,1,0:T(8,128)(2,1)}), bf16[4,1216,512]{2,1,0:T(8,128)(2,1)}, u32[]{:S(2)}, u32[]{:S(2)}) async-start(bf16[4,1216,512]{2,1,0:T(8,128)(2,1)} %bitcast.396), calls=%async_computation | async-start | bytes 9961472 | tf_op jit(solution)/shard_map/all_to_all | solution.py:233
  61.1 2.3 collective-permute-start.4
  64.3 3.2 collective-permute-start.12
  68.6 63.8 %collective-permute-done.12 = bf16[2,128,1280]{2,1,0:T(8,128)(2,1)S(1)} collective-permute-done((bf16[2,128,1280]{2,1,0:T(8,128)(2,1)S(1)}, bf16[2,128,1280]{2,1,0:T(8,128)(2,1)S(1)}, u32[]{:S(2)}, u32[]{:S(2)}) %collective-permute-start.12) | collective-permute-done | bytes 655392 | tf_op jit(solution)/shard_map/ppermute | solution.py:28
  134.4 10.2 %collective-permute-done.14 = bf16[2,128,1280]{2,1,0:T(8,128)(2,1)S(1)} collective-permute-done((bf16[2,128,1280]{2,1,0:T(8,128)(2,1)S(1)}, bf16[2,128,1280]{2,1,0:T(8,128)(2,1)S(1)}, u32[]{:S(2)}, u32[]{:S(2)}) %collective-permute-start.14) | collective-permute-done | bytes 655392 | tf_op jit(solution)/shard_map/ppermute | solution.py:28
  144.9 8.7 %collective-permute-done.9 = bf16[16,64,512]{2,1,0:T(8,128)(2,1)S(1)} collective-permute-done((bf16[16,64,512]{2,1,0:T(8,128)(2,1)S(1)}, bf16[16,64,512]{2,1,0:T(8,128)(2,1)S(1)}, u32[]{:S(2)}, u32[]{:S(2)}) %collective-permute-start.9) | collective-permute-done | bytes 1048608 | tf_op jit(solution)/shard_map/ppermute | solution.py:28
  158.1 2.1 maximum_select_fusion
  166.7 10.4 %shard_map.77 = (f32[512,2432]{1,0:T(8,128)}, f32[512,2432]{1,0:T(8,128)}) custom-call(bf16[2,512,1280]{2,1,0:T(8,128)(2,1)S(1)} %bitcast.390, bf16[320,2400]{1,0:T(8,128)(2,1)S(1)} %copy-done.9, bf16[320,2400]{1,0:T(8,128)(2,1)} %collective-permute-done.3.w1, bf16[320,2400]{1,0:T(8,128)(2,1)S(1)} %copy-done.11, bf16[320,2400]{1,0:T(8,128)(2,1)S(1)} %copy-done.13), custom_call_target="tpu_custom_call" | custom-call | flops 6291456000 | bytes 15974400 | tf_op jit(solution)/shard_map/pallas_call | solution.py:94
  177.3 17.1 %all-to-all-start.1 = ((bf16[4,1216,512]{2,1,0:T(8,128)(2,1)}), bf16[4,1216,512]{2,1,0:T(8,128)(2,1)}, u32[]{:S(2)}, u32[]{:S(2)}) async-start(bf16[4,1216,512]{2,1,0:T(8,128)(2,1)} %bitcast.397), calls=%async_computation.1 | async-start | bytes 9961472 | tf_op jit(solution)/shard_map/all_to_all | solution.py:233
  194.4 2.2 copy-done
  196.6 10.3 %shard_map.76 = (f32[1024,640]{1,0:T(8,128)S(1)}, f32[1024,640]{1,0:T(8,128)S(1)}) custom-call(s32[1]{0:T(128)} %bitcast.here, bf16[4,1024,512]{2,1,0:T(8,128)(2,1)S(1)} %bitcast.388, bf16[4,1216,512]{2,1,0:T(8,128)(2,1)} %all-to-all-done.weights), custom_call_target="tpu_custom_call" | custom-call | flops 5100273664 | bytes 18612224 | tf_op jit(solution)/shard_map/pallas_call | solution.py:135
  211.0 2.0 collective-permute-start.16
  213.6 2.9 add.433
  216.8 2.3 select_convert_fusion.3
  220.5 19.5 %collective-permute-done.18 = s16[1024,640]{1,0:T(8,128)(2,1)S(1)} collective-permute-done((s16[1024,640]{1,0:T(8,128)(2,1)S(1)}, s16[1024,640]{1,0:T(8,128)(2,1)S(1)}, u32[]{:S(2)}, u32[]{:S(2)}) %collective-permute-start.18) | collective-permute-done | bytes 1310752 | tf_op jit(solution)/shard_map/ppermute | solution.py:28
  240.0 7.4 %collective-permute-done.15.w1 = bf16[320,2348]{1,0:T(8,128)(2,1)S(1)} collective-permute-done((bf16[320,2348]{1,0:T(8,128)(2,1)S(1)}, bf16[320,2348]{1,0:T(8,128)(2,1)S(1)}, u32[]{:S(2)}, u32[]{:S(2)}) %collective-permute-start.15) | collective-permute-done | bytes 1502752 | tf_op jit(solution)/shard_map/ppermute | solution.py:28
  248.5 30.8 %collective-permute-done.16.w2 = bf16[320,2348]{1,0:T(8,128)(2,1)S(1)} collective-permute-done((bf16[320,2348]{1,0:T(8,128)(2,1)S(1)}, bf16[320,2348]{1,0:T(8,128)(2,1)S(1)}, u32[]{:S(2)}, u32[]{:S(2)}) %collective-permute-start.16) | collective-permute-done | bytes 1502752 | tf_op jit(solution)/shard_map/ppermute | solution.py:28
  282.9 2.2 copy-done.1
  285.1 10.4 %shard_map.78 = (f32[1024,640]{1,0:T(8,128)S(1)}, f32[1024,640]{1,0:T(8,128)S(1)}) custom-call(s32[1]{0:T(128)} %bitcast.here, bf16[4,1024,512]{2,1,0:T(8,128)(2,1)S(1)} %bitcast.389, bf16[4,1216,512]{2,1,0:T(8,128)(2,1)} %all-to-all-done.1.weights), custom_call_target="tpu_custom_call" | custom-call | flops 5100273664 | bytes 18612224 | tf_op jit(solution)/shard_map/pallas_call | solution.py:135
  298.4 10.0 %shard_map.79 = (f32[512,2432]{1,0:T(8,128)}, f32[512,2432]{1,0:T(8,128)}) custom-call(bf16[2,512,1280]{2,1,0:T(8,128)(2,1)S(1)} %bitcast.391, bf16[320,2348]{1,0:T(8,128)(2,1)S(1)} %copy-done.8, bf16[320,2348]{1,0:T(8,128)(2,1)S(1)} %copy-done.15, bf16[320,2348]{1,0:T(8,128)(2,1)S(1)} %copy-done.17, bf16[320,2348]{1,0:T(8,128)(2,1)S(1)} %copy-done.19), custom_call_target="tpu_custom_call" | custom-call | flops 6155141120 | bytes 15628288 | tf_op jit(solution)/shard_map/pallas_call | solution.py:94
  308.8 1.6 add_convert_fusion.1
  310.4 8.0 %all-to-all-start.2 = ((bf16[16,64,640]{2,1,0:T(8,128)(2,1)}), bf16[16,64,640]{2,1,0:T(8,128)(2,1)}, u32[]{:S(2)}, u32[]{:S(2)}) async-start(bf16[16,64,640]{2,1,0:T(8,128)(2,1)} %bitcast.410), calls=%async_computation.2 | async-start | bytes 2621440 | tf_op jit(solution)/shard_map/all_to_all | solution.py:218
  318.7 1.9 select_convert_fusion
  322.8 14.0 %all-to-all-done.2 = bf16[16,64,640]{2,1,0:T(8,128)(2,1)} async-done(((bf16[16,64,640]{2,1,0:T(8,128)(2,1)}), bf16[16,64,640]{2,1,0:T(8,128)(2,1)}, u32[]{:S(2)}, u32[]{:S(2)}) %all-to-all-start.2) | async-done | bytes 1310752 | tf_op jit(solution)/shard_map/all_to_all | solution.py:218
  336.7 6.7 %all-to-all-start.3 = ((bf16[8,2,64,640]{3,2,1,0:T(8,128)(2,1)}), bf16[8,2,64,640]{3,2,1,0:T(8,128)(2,1)}, u32[]{:S(2)}, u32[]{:S(2)}) async-start(bf16[8,2,64,640]{3,2,1,0:T(8,128)(2,1)} %bitcast.33), calls=%async_computation.3 | async-start | bytes 2621440 | tf_op jit(solution)/shard_map/all_to_all | solution.py:219
  343.5 4.4 add.441
  348.1 2.7 select_convert_fusion.2
  350.9 3.7 collective-permute-start.26
  356.0 3.2 collective-permute-start.23
  360.4 17.2 %all-to-all-done.3 = bf16[8,2,64,640]{3,2,1,0:T(8,128)(2,1)} async-done(((bf16[8,2,64,640]{3,2,1,0:T(8,128)(2,1)}), bf16[8,2,64,640]{3,2,1,0:T(8,128)(2,1)}, u32[]{:S(2)}, u32[]{:S(2)}) %all-to-all-start.3) | async-done | bytes 1310752 | tf_op jit(solution)/shard_map/all_to_all | solution.py:219
  377.6 3.7 copy.26
  381.3 4.2 reshape.544
  385.5 2.4 pad.21
  388.0 15.0 %collective-permute-done.26 = s16[256,2432]{1,0:T(8,128)(2,1)} collective-permute-done((s16[256,2432]{1,0:T(8,128)(2,1)}, s16[256,2432]{1,0:T(8,128)(2,1)}, u32[]{:S(2)}, u32[]{:S(2)}) %collective-permute-start.26) | collective-permute-done | bytes 1245216 | tf_op jit(solution)/shard_map/ppermute | solution.py:28
  404.3 2.9 add_convert_fusion
  407.3 8.0 %all-to-all-start.4 = ((bf16[16,64,640]{2,1,0:T(8,128)(2,1)}), bf16[16,64,640]{2,1,0:T(8,128)(2,1)}, u32[]{:S(2)}, u32[]{:S(2)}) async-start(bf16[16,64,640]{2,1,0:T(8,128)(2,1)} %bitcast.409), calls=%async_computation.4 | async-start | bytes 2621440 | tf_op jit(solution)/shard_map/all_to_all | solution.py:218
  416.3 1.8 multiply_add_fusion
  422.6 1.8 collective-permute-start.28
  424.4 2.7 broadcast_in_dim.114
  428.9 1.9 bitcast_dynamic-update-slice_fusion.10
  430.8 1.9 bitcast_dynamic-update-slice_fusion.9
  433.6 1.8 collective-permute-start.29
  435.4 4.5 collective-permute-done.27
  442.2 7.0 %all-to-all-start.5 = ((bf16[8,2,64,640]{3,2,1,0:T(8,128)(2,1)}), bf16[8,2,64,640]{3,2,1,0:T(8,128)(2,1)S(1)}, u32[]{:S(2)}, u32[]{:S(2)}) async-start(bf16[8,2,64,640]{3,2,1,0:T(8,128)(2,1)} %bitcast.48), calls=%async_computation.5 | async-start | bytes 2621440 | tf_op jit(solution)/shard_map/all_to_all | solution.py:219
  450.3 2.9 fusion.6
  453.3 13.2 %all-to-all-done.5 = bf16[8,2,64,640]{3,2,1,0:T(8,128)(2,1)S(1)} async-done(((bf16[8,2,64,640]{3,2,1,0:T(8,128)(2,1)}), bf16[8,2,64,640]{3,2,1,0:T(8,128)(2,1)S(1)}, u32[]{:S(2)}, u32[]{:S(2)}) %all-to-all-start.5) | async-done | bytes 1310752 | tf_op jit(solution)/shard_map/all_to_all | solution.py:219
  467.8 1.8 reshape.548
  473.0 4.4 multiply_reduce_fusion
  478.1 3.0 collective-permute-done.30
  482.0 2.4 collective-permute-start.32
  486.0 3.5 collective-permute-done.33
  490.1 3.4 multiply_convert_fusion
  493.8 4.1 concatenate.29
  (221 shorter events, 63.9 us)
Async XLA Ops:
  2.7 25.2 %collective-permute-start = (bf16[144,512]{1,0:T(8,128)(2,1)S(1)}, bf16[144,512]{1,0:T(8,128)(2,1)S(1)}, u32[]{:S(2)}, u32[]{:S(2)}) collective-permute-start(bf16[144,512]{1,0:T(8,128)(2,1)S(1)} %constant_dynamic-update-slice_fusion), channel_id=1, source_target_pairs={{0,32},{1,33},{2,34},{3,35},{4,36},{5,37},{6,38},{7,39},{8,40},{9,... | collective-permute-start | bytes 442376 | tf_op jit(solution)/shard_map/ppermute | solution.py:28
  4.6 23.2 %collective-permute-start.1 = (bf16[144,512]{1,0:T(8,128)(2,1)S(1)}, bf16[144,512]{1,0:T(8,128)(2,1)S(1)}, u32[]{:S(2)}, u32[]{:S(2)}) collective-permute-start(bf16[144,512]{1,0:T(8,128)(2,1)S(1)} %constant_dynamic-update-slice_fusion), channel_id=1, source_target_pairs={{0,96},{1,97},{2,98},{3,99},{4,100},{5,101},{6,102},{7,103},{8,104... | collective-permute-start | bytes 442376 | tf_op jit(solution)/shard_map/ppermute | solution.py:28
  6.8 21.0 %collective-permute-start.2 = (bf16[144,512]{1,0:T(8,128)(2,1)S(1)}, bf16[144,512]{1,0:T(8,128)(2,1)S(1)}, u32[]{:S(2)}, u32[]{:S(2)}) collective-permute-start(bf16[144,512]{1,0:T(8,128)(2,1)S(1)} %constant_dynamic-update-slice_fusion), channel_id=1, source_target_pairs={{0,64},{1,65},{2,66},{3,67},{4,68},{5,69},{6,70},{7,71},{8,72},{9,... | collective-permute-start | bytes 442376 | tf_op jit(solution)/shard_map/ppermute | solution.py:28
  28.0 33.1 %collective-permute-start.6 = (bf16[4,64,512]{2,1,0:T(8,128)(2,1)S(1)}, bf16[4,64,512]{2,1,0:T(8,128)(2,1)S(1)}, u32[]{:S(2)}, u32[]{:S(2)}) collective-permute-start(bf16[4,64,512]{2,1,0:T(8,128)(2,1)S(1)} %constant_dynamic-slice_fusion.2), channel_id=1, source_target_pairs={{0,3},{1,0},{2,1},{3,2},{4,7},{5,4},{6,5},{7,6},{8,11},{9,8},{10,9... | collective-permute-start | bytes 786440 | tf_op jit(solution)/shard_map/ppermute | solution.py:28
  31.1 32.4 %collective-permute-start.7 = (bf16[4,64,512]{2,1,0:T(8,128)(2,1)S(1)}, bf16[4,64,512]{2,1,0:T(8,128)(2,1)S(1)}, u32[]{:S(2)}, u32[]{:S(2)}) collective-permute-start(bf16[4,64,512]{2,1,0:T(8,128)(2,1)S(1)} %constant_dynamic-slice_fusion.2), channel_id=1, source_target_pairs={{0,2},{1,3},{2,0},{3,1},{4,6},{5,7},{6,4},{7,5},{8,10},{9,11},{10,... | collective-permute-start | bytes 786440 | tf_op jit(solution)/shard_map/ppermute | solution.py:28
  52.0 12.1 %collective-permute-start.8 = (bf16[4,64,512]{2,1,0:T(8,128)(2,1)S(1)}, bf16[4,64,512]{2,1,0:T(8,128)(2,1)S(1)}, u32[]{:S(2)}, u32[]{:S(2)}) collective-permute-start(bf16[4,64,512]{2,1,0:T(8,128)(2,1)S(1)} %constant_dynamic-slice_fusion.2), channel_id=1, source_target_pairs={{0,1},{1,2},{2,3},{3,0},{4,5},{5,6},{6,7},{7,4},{8,9},{9,10},{10,1... | collective-permute-start | bytes 786440 | tf_op jit(solution)/shard_map/ppermute | solution.py:28
  54.2 10.0 %collective-permute-start.11 = (bf16[128,1280]{1,0:T(8,128)(2,1)S(1)}, bf16[128,1280]{1,0:T(8,128)(2,1)S(1)}, u32[]{:S(2)}, u32[]{:S(2)}) collective-permute-start(bf16[128,1280]{1,0:T(8,128)(2,1)S(1)} %concatenate.27), channel_id=1, source_target_pairs={{0,4},{1,5},{2,6},{3,7},{4,0},{5,1},{6,2},{7,3},{8,12},{9,13},{10,... | collective-permute-start | bytes 983048 | tf_op jit(solution)/shard_map/ppermute | solution.py:28
  55.1 105.1 %collective-permute-start.3 = (bf16[320,2400]{1,0:T(8,128)(2,1)}, bf16[320,2400]{1,0:T(8,128)(2,1)}, u32[]{:S(2)}, u32[]{:S(2)}) collective-permute-start(bf16[320,2400]{1,0:T(8,128)(2,1)} %get-tuple-element.57), channel_id=1, source_target_pairs={{0,32},{1,33},{2,34},{3,35},{4,36},{5,37},{6,38},{7,39},{8,40},{9,... | collective-permute-start | bytes 4608008 | tf_op jit(solution)/shard_map/ppermute | solution.py:28
  56.1 106.4 %all-to-all-start = ((bf16[4,1216,512]{2,1,0:T(8,128)(2,1)}), bf16[4,1216,512]{2,1,0:T(8,128)(2,1)}, u32[]{:S(2)}, u32[]{:S(2)}) async-start(bf16[4,1216,512]{2,1,0:T(8,128)(2,1)} %bitcast.396), calls=%async_computation | async-start | bytes 9961472 | tf_op jit(solution)/shard_map/all_to_all | solution.py:233
  61.1 99.1 %collective-permute-start.4 = (bf16[320,2400]{1,0:T(8,128)(2,1)}, bf16[320,2400]{1,0:T(8,128)(2,1)S(1)}, u32[]{:S(2)}, u32[]{:S(2)}) collective-permute-start(bf16[320,2400]{1,0:T(8,128)(2,1)} %get-tuple-element.58), channel_id=1, source_target_pairs={{0,96},{1,97},{2,98},{3,99},{4,100},{5,101},{6,102},{7,103},{8,104... | collective-permute-start | bytes 4608008 | tf_op jit(solution)/shard_map/ppermute | solution.py:28
  63.5 97.9 %collective-permute-start.5 = (bf16[320,2400]{1,0:T(8,128)(2,1)}, bf16[320,2400]{1,0:T(8,128)(2,1)S(1)}, u32[]{:S(2)}, u32[]{:S(2)}) collective-permute-start(bf16[320,2400]{1,0:T(8,128)(2,1)} %get-tuple-element.59), channel_id=1, source_target_pairs={{0,64},{1,65},{2,66},{3,67},{4,68},{5,69},{6,70},{7,71},{8,72},{9,... | collective-permute-start | bytes 4608008 | tf_op jit(solution)/shard_map/ppermute | solution.py:28
  64.3 68.1 %collective-permute-start.12 = (bf16[2,128,1280]{2,1,0:T(8,128)(2,1)S(1)}, bf16[2,128,1280]{2,1,0:T(8,128)(2,1)S(1)}, u32[]{:S(2)}, u32[]{:S(2)}) collective-permute-start(bf16[2,128,1280]{2,1,0:T(8,128)(2,1)S(1)} %maximum_select_fusion.2), channel_id=1, source_target_pairs={{0,3},{1,0},{2,1},{3,2},{4,7},{5,4},{6,5},{7,6},{8,11},{9,8},{10,9... | collective-permute-start | bytes 1966088 | tf_op jit(solution)/shard_map/ppermute | solution.py:28
  67.5 65.6 %collective-permute-start.13 = (bf16[2,128,1280]{2,1,0:T(8,128)(2,1)S(1)}, bf16[2,128,1280]{2,1,0:T(8,128)(2,1)S(1)}, u32[]{:S(2)}, u32[]{:S(2)}) collective-permute-start(bf16[2,128,1280]{2,1,0:T(8,128)(2,1)S(1)} %maximum_select_fusion.2), channel_id=1, source_target_pairs={{0,2},{1,3},{2,0},{3,1},{4,6},{5,7},{6,4},{7,5},{8,10},{9,11},{10,... | collective-permute-start | bytes 1966088 | tf_op jit(solution)/shard_map/ppermute | solution.py:28
  132.4 12.2 %collective-permute-start.14 = (bf16[2,128,1280]{2,1,0:T(8,128)(2,1)S(1)}, bf16[2,128,1280]{2,1,0:T(8,128)(2,1)S(1)}, u32[]{:S(2)}, u32[]{:S(2)}) collective-permute-start(bf16[2,128,1280]{2,1,0:T(8,128)(2,1)S(1)} %maximum_select_fusion.2), channel_id=1, source_target_pairs={{0,1},{1,2},{2,3},{3,0},{4,5},{5,6},{6,7},{7,4},{8,9},{9,10},{10,1... | collective-permute-start | bytes 1966088 | tf_op jit(solution)/shard_map/ppermute | solution.py:28
  133.2 20.4 %collective-permute-start.9 = (bf16[16,64,512]{2,1,0:T(8,128)(2,1)S(1)}, bf16[16,64,512]{2,1,0:T(8,128)(2,1)S(1)}, u32[]{:S(2)}, u32[]{:S(2)}) collective-permute-start(bf16[16,64,512]{2,1,0:T(8,128)(2,1)S(1)} %bitcast.416), channel_id=1, source_target_pairs={{0,16},{1,17},{2,18},{3,19},{4,20},{5,21},{6,22},{7,23},{8,24},{9,... | collective-permute-start | bytes 3145736 | tf_op jit(solution)/shard_map/ppermute | solution.py:28
  153.8 4.2 collective-permute-start.10
  156.6 5.9 %copy-start.4 = (bf16[2,2,4,64,1280]{4,3,2,1,0:T(8,128)(2,1)}, bf16[2,2,4,64,1280]{4,3,2,1,0:T(8,128)(2,1)S(1)}, u32[]{:S(2)}) copy-start(bf16[2,2,4,64,1280]{4,3,2,1,0:T(8,128)(2,1)S(1)} %fusion.7) | copy-start | bytes 7864324
  177.2 36.4 %collective-permute-start.19 = (f32[512,2432]{1,0:T(8,128)}, f32[512,2432]{1,0:T(8,128)}, u32[]{:S(2)}, u32[]{:S(2)}) collective-permute-start(f32[512,2432]{1,0:T(8,128)} %get-tuple-element.80), channel_id=1, source_target_pairs={{0,8},{1,9},{2,10},{3,11},{4,12},{5,13},{6,14},{7,15},{8,0},{9,1},... | collective-permute-start | bytes 14942216 | tf_op jit(solution)/shard_map/ppermute | solution.py:28
  177.3 177.3 %copy-start.30 = (pred[2432]{0:T(1024)(128)(4,1)}, pred[2432]{0:T(1024)(128)(4,1)S(1)}, u32[]{:S(2)}) copy-start(pred[2432]{0:T(1024)(128)(4,1)S(1)} %iota_compare_fusion.2) | copy-start | bytes 7300
  177.3 36.2 %slice-start = ((s8[4980736]{0:T(1024)(128)(4,1)}), s8[786432]{0:T(1024)(128)(4,1)S(1)}, s32[]{:S(2)}) async-start(s8[4980736]{0:T(1024)(128)(4,1)} %bitcast.414), calls=%async_computation.6 | async-start | bytes 1572864
  177.3 104.4 %all-to-all-start.1 = ((bf16[4,1216,512]{2,1,0:T(8,128)(2,1)}), bf16[4,1216,512]{2,1,0:T(8,128)(2,1)}, u32[]{:S(2)}, u32[]{:S(2)}) async-start(bf16[4,1216,512]{2,1,0:T(8,128)(2,1)} %bitcast.397), calls=%async_computation.1 | async-start | bytes 9961472 | tf_op jit(solution)/shard_map/all_to_all | solution.py:233
  194.4 2.2 copy-start
  196.6 17.0 %slice-start.1 = ((s8[4980736]{0:T(1024)(128)(4,1)}), s8[4194304]{0:T(1024)(128)(4,1)S(1)}, s32[]{:S(2)}) async-start(s8[4980736]{0:T(1024)(128)(4,1)} %bitcast.414), calls=%async_computation.7 | async-start | bytes 8388608
  206.9 2.7 copy-start.27
  207.2 3.8 copy-start.26
  207.2 5.8 %copy-start.25 = (bf16[320,2348]{1,0:T(8,128)(2,1)S(1)}, bf16[320,2348]{1,0:T(8,128)(2,1)}, u32[]{:S(2)}) copy-start(bf16[320,2348]{1,0:T(8,128)(2,1)} %get-tuple-element.69) | copy-start | bytes 4508164
  208.4 31.6 %collective-permute-start.18 = (s16[1024,640]{1,0:T(8,128)(2,1)S(1)}, s16[1024,640]{1,0:T(8,128)(2,1)S(1)}, u32[]{:S(2)}, u32[]{:S(2)}) collective-permute-start(s16[1024,640]{1,0:T(8,128)(2,1)S(1)} %select_convert_fusion.1), channel_id=1, source_target_pairs={{0,4},{1,5},{2,6},{3,7},{4,0},{5,1},{6,2},{7,3},{8,12},{9,13},{10,... | collective-permute-start | bytes 3932168 | tf_op jit(solution)/shard_map/ppermute | solution.py:28
  209.6 37.8 %collective-permute-start.15 = (bf16[320,2348]{1,0:T(8,128)(2,1)S(1)}, bf16[320,2348]{1,0:T(8,128)(2,1)S(1)}, u32[]{:S(2)}, u32[]{:S(2)}) collective-permute-start(bf16[320,2348]{1,0:T(8,128)(2,1)S(1)} %copy-done.27), channel_id=1, source_target_pairs={{0,32},{1,33},{2,34},{3,35},{4,36},{5,37},{6,38},{7,39},{8,40},{9,... | collective-permute-start | bytes 4508168 | tf_op jit(solution)/shard_map/ppermute | solution.py:28
  211.0 68.4 %collective-permute-start.16 = (bf16[320,2348]{1,0:T(8,128)(2,1)S(1)}, bf16[320,2348]{1,0:T(8,128)(2,1)S(1)}, u32[]{:S(2)}, u32[]{:S(2)}) collective-permute-start(bf16[320,2348]{1,0:T(8,128)(2,1)S(1)} %copy-done.26), channel_id=1, source_target_pairs={{0,96},{1,97},{2,98},{3,99},{4,100},{5,101},{6,102},{7,103},{8,104... | collective-permute-start | bytes 4508168 | tf_op jit(solution)/shard_map/ppermute | solution.py:28
  213.0 67.6 %collective-permute-start.17 = (bf16[320,2348]{1,0:T(8,128)(2,1)S(1)}, bf16[320,2348]{1,0:T(8,128)(2,1)S(1)}, u32[]{:S(2)}, u32[]{:S(2)}) collective-permute-start(bf16[320,2348]{1,0:T(8,128)(2,1)S(1)} %copy-done.25), channel_id=1, source_target_pairs={{0,64},{1,65},{2,66},{3,67},{4,68},{5,69},{6,70},{7,71},{8,72},{9,... | collective-permute-start | bytes 4508168 | tf_op jit(solution)/shard_map/ppermute | solution.py:28
  219.1 62.7 %collective-permute-start.20 = (s16[256,2432]{1,0:T(8,128)(2,1)S(1)}, s16[256,2432]{1,0:T(8,128)(2,1)S(1)}, u32[]{:S(2)}, u32[]{:S(2)}) collective-permute-start(s16[256,2432]{1,0:T(8,128)(2,1)S(1)} %get-tuple-element.146), channel_id=1, source_target_pairs={{0,16},{1,17},{2,18},{3,19},{4,20},{5,21},{6,22},{7,23},{8,24},{9,... | collective-permute-start | bytes 3735560 | tf_op jit(solution)/shard_map/ppermute | solution.py:28
  240.0 39.3 %copy-start.23 = (s16[1024,640]{1,0:T(8,128)(2,1)}, s16[1024,640]{1,0:T(8,128)(2,1)S(1)}, u32[]{:S(2)}) copy-start(s16[1024,640]{1,0:T(8,128)(2,1)S(1)} %collective-permute-done.18) | copy-start | bytes 3932164
  282.9 2.2 copy-start.1
  285.1 11.9 %copy-start.5 = (bf16[2,2,4,64,1280]{4,3,2,1,0:T(8,128)(2,1)S(1)}, bf16[2,2,4,64,1280]{4,3,2,1,0:T(8,128)(2,1)}, u32[]{:S(2)}) copy-start(bf16[2,2,4,64,1280]{4,3,2,1,0:T(8,128)(2,1)} %copy-done.4) | copy-start | bytes 7864324
  285.1 11.9 %copy-start.8 = (bf16[320,2348]{1,0:T(8,128)(2,1)S(1)}, bf16[320,2348]{1,0:T(8,128)(2,1)}, u32[]{:S(2)}) copy-start(bf16[320,2348]{1,0:T(8,128)(2,1)} %get-tuple-element.94.w0) | copy-start | bytes 4508164
  285.1 11.9 %copy-start.15 = (bf16[320,2348]{1,0:T(8,128)(2,1)S(1)}, bf16[320,2348]{1,0:T(8,128)(2,1)}, u32[]{:S(2)}) copy-start(bf16[320,2348]{1,0:T(8,128)(2,1)} %copy-done.14) | copy-start | bytes 4508164
  285.1 11.9 %copy-start.17 = (bf16[320,2348]{1,0:T(8,128)(2,1)S(1)}, bf16[320,2348]{1,0:T(8,128)(2,1)}, u32[]{:S(2)}) copy-start(bf16[320,2348]{1,0:T(8,128)(2,1)} %copy-done.16) | copy-start | bytes 4508164
  298.4 10.1 %copy-start.24 = (s16[1024,640]{1,0:T(8,128)(2,1)S(1)}, s16[1024,640]{1,0:T(8,128)(2,1)}, u32[]{:S(2)}) copy-start(s16[1024,640]{1,0:T(8,128)(2,1)} %copy-done.23) | copy-start | bytes 3932164
  298.4 10.4 %copy-start.7 = (f32[1024,640]{1,0:T(8,128)S(1)}, f32[1024,640]{1,0:T(8,128)}, u32[]{:S(2)}) copy-start(f32[1024,640]{1,0:T(8,128)} %copy-done.6) | copy-start | bytes 7864324
  308.4 35.0 %collective-permute-start.25 = (f32[512,2432]{1,0:T(8,128)}, f32[512,2432]{1,0:T(8,128)}, u32[]{:S(2)}, u32[]{:S(2)}) collective-permute-start(f32[512,2432]{1,0:T(8,128)} %get-tuple-element.99), channel_id=1, source_target_pairs={{0,8},{1,9},{2,10},{3,11},{4,12},{5,13},{6,14},{7,15},{8,0},{9,1},... | collective-permute-start | bytes 14942216 | tf_op jit(solution)/shard_map/ppermute | solution.py:28
  310.4 26.3 %all-to-all-start.2 = ((bf16[16,64,640]{2,1,0:T(8,128)(2,1)}), bf16[16,64,640]{2,1,0:T(8,128)(2,1)}, u32[]{:S(2)}, u32[]{:S(2)}) async-start(bf16[16,64,640]{2,1,0:T(8,128)(2,1)} %bitcast.410), calls=%async_computation.2 | async-start | bytes 2621440 | tf_op jit(solution)/shard_map/all_to_all | solution.py:218
  318.7 3.1 copy-start.29
  318.7 3.3 copy-start.22
  320.6 67.4 %collective-permute-start.21 = (s16[1024,640]{1,0:T(8,128)(2,1)}, s16[1024,640]{1,0:T(8,128)(2,1)}, u32[]{:S(2)}, u32[]{:S(2)}) collective-permute-start(s16[1024,640]{1,0:T(8,128)(2,1)} %select_convert_fusion), channel_id=1, source_target_pairs={{0,4},{1,5},{2,6},{3,7},{4,0},{5,1},{6,2},{7,3},{8,12},{9,13},{10,... | collective-permute-start | bytes 3932168 | tf_op jit(solution)/shard_map/ppermute | solution.py:28
  336.7 40.8 %all-to-all-start.3 = ((bf16[8,2,64,640]{3,2,1,0:T(8,128)(2,1)}), bf16[8,2,64,640]{3,2,1,0:T(8,128)(2,1)}, u32[]{:S(2)}, u32[]{:S(2)}) async-start(bf16[8,2,64,640]{3,2,1,0:T(8,128)(2,1)} %bitcast.33), calls=%async_computation.3 | async-start | bytes 2621440 | tf_op jit(solution)/shard_map/all_to_all | solution.py:219
  350.9 52.1 %collective-permute-start.26 = (s16[256,2432]{1,0:T(8,128)(2,1)}, s16[256,2432]{1,0:T(8,128)(2,1)}, u32[]{:S(2)}, u32[]{:S(2)}) collective-permute-start(s16[256,2432]{1,0:T(8,128)(2,1)} %get-tuple-element.144), channel_id=1, source_target_pairs={{0,16},{1,17},{2,18},{3,19},{4,20},{5,21},{6,22},{7,23},{8,24},{9,... | collective-permute-start | bytes 3735560 | tf_op jit(solution)/shard_map/ppermute | solution.py:28
  356.0 32.0 %collective-permute-start.22 = (s16[64,2432]{1,0:T(8,128)(2,1)}, s16[64,2432]{1,0:T(8,128)(2,1)S(1)}, u32[]{:S(2)}, u32[]{:S(2)}) collective-permute-start(s16[64,2432]{1,0:T(8,128)(2,1)} %get-tuple-element.152), channel_id=1, source_target_pairs={{0,32},{1,33},{2,34},{3,35},{4,36},{5,37},{6,38},{7,39},{8,40},{9,... | collective-permute-start | bytes 933896 | tf_op jit(solution)/shard_map/ppermute | solution.py:28
  356.0 32.0 %collective-permute-start.23 = (s16[64,2432]{1,0:T(8,128)(2,1)}, s16[64,2432]{1,0:T(8,128)(2,1)}, u32[]{:S(2)}, u32[]{:S(2)}) collective-permute-start(s16[64,2432]{1,0:T(8,128)(2,1)} %get-tuple-element.153), channel_id=1, source_target_pairs={{0,96},{1,97},{2,98},{3,99},{4,100},{5,101},{6,102},{7,103},{8,104... | collective-permute-start | bytes 933896 | tf_op jit(solution)/shard_map/ppermute | solution.py:28
  359.3 28.7 %collective-permute-start.24 = (s16[64,2432]{1,0:T(8,128)(2,1)}, s16[64,2432]{1,0:T(8,128)(2,1)}, u32[]{:S(2)}, u32[]{:S(2)}) collective-permute-start(s16[64,2432]{1,0:T(8,128)(2,1)} %get-tuple-element.151), channel_id=1, source_target_pairs={{0,64},{1,65},{2,66},{3,67},{4,68},{5,69},{6,70},{7,71},{8,72},{9,... | collective-permute-start | bytes 933896 | tf_op jit(solution)/shard_map/ppermute | solution.py:28
  381.3 23.0 %copy-start.3 = (f32[1024,640]{1,0:T(8,128)S(1)}, f32[1024,640]{1,0:T(8,128)}, u32[]{:S(2)}) copy-start(f32[1024,640]{1,0:T(8,128)} %copy-done.2) | copy-start | bytes 7864324
  407.3 9.0 %copy-start.21 = (f32[256,2432]{1,0:T(8,128)S(1)}, f32[256,2432]{1,0:T(8,128)}, u32[]{:S(2)}) copy-start(f32[256,2432]{1,0:T(8,128)} %get-tuple-element.104) | copy-start | bytes 7471108
  407.3 34.9 %all-to-all-start.4 = ((bf16[16,64,640]{2,1,0:T(8,128)(2,1)}), bf16[16,64,640]{2,1,0:T(8,128)(2,1)}, u32[]{:S(2)}, u32[]{:S(2)}) async-start(bf16[16,64,640]{2,1,0:T(8,128)(2,1)} %bitcast.409), calls=%async_computation.4 | async-start | bytes 2621440 | tf_op jit(solution)/shard_map/all_to_all | solution.py:218
  416.3 2.1 copy-start.31
  419.0 20.9 %collective-permute-start.27 = (s16[64,2432]{1,0:T(8,128)(2,1)S(1)}, s16[64,2432]{1,0:T(8,128)(2,1)S(1)}, u32[]{:S(2)}, u32[]{:S(2)}) collective-permute-start(s16[64,2432]{1,0:T(8,128)(2,1)S(1)} %get-tuple-element.149), channel_id=1, source_target_pairs={{0,32},{1,33},{2,34},{3,35},{4,36},{5,37},{6,38},{7,39},{8,40},{9,... | collective-permute-start | bytes 933896 | tf_op jit(solution)/shard_map/ppermute | solution.py:28
  422.6 17.5 %collective-permute-start.28 = (s16[64,2432]{1,0:T(8,128)(2,1)S(1)}, s16[64,2432]{1,0:T(8,128)(2,1)S(1)}, u32[]{:S(2)}, u32[]{:S(2)}) collective-permute-start(s16[64,2432]{1,0:T(8,128)(2,1)S(1)} %get-tuple-element.150), channel_id=1, source_target_pairs={{0,96},{1,97},{2,98},{3,99},{4,100},{5,101},{6,102},{7,103},{8,104... | collective-permute-start | bytes 933896 | tf_op jit(solution)/shard_map/ppermute | solution.py:28
  433.6 15.5 %collective-permute-start.29 = (s16[64,2432]{1,0:T(8,128)(2,1)S(1)}, s16[64,2432]{1,0:T(8,128)(2,1)S(1)}, u32[]{:S(2)}, u32[]{:S(2)}) collective-permute-start(s16[64,2432]{1,0:T(8,128)(2,1)S(1)} %get-tuple-element.148), channel_id=1, source_target_pairs={{0,64},{1,65},{2,66},{3,67},{4,68},{5,69},{6,70},{7,71},{8,72},{9,... | collective-permute-start | bytes 933896 | tf_op jit(solution)/shard_map/ppermute | solution.py:28
  440.3 10.1 %copy-start.32 = (s32[2]{0:T(128)S(1)}, s32[2]{0:T(128)}, u32[]{:S(2)}) copy-start(s32[2]{0:T(128)} %get-tuple-element.182) | copy-start | bytes 28
  442.2 24.3 %all-to-all-start.5 = ((bf16[8,2,64,640]{3,2,1,0:T(8,128)(2,1)}), bf16[8,2,64,640]{3,2,1,0:T(8,128)(2,1)S(1)}, u32[]{:S(2)}, u32[]{:S(2)}) async-start(bf16[8,2,64,640]{3,2,1,0:T(8,128)(2,1)} %bitcast.48), calls=%async_computation.5 | async-start | bytes 2621440 | tf_op jit(solution)/shard_map/all_to_all | solution.py:219
  467.8 3.2 copy-start.20
  470.9 2.0 copy-start.33
  477.4 3.7 collective-permute-start.30
  481.1 4.9 collective-permute-start.31
  482.0 4.0 collective-permute-start.32
  484.5 5.1 %collective-permute-start.33 = (f32[6,64]{1,0:T(8,128)S(1)}, f32[6,64]{1,0:T(8,128)S(1)}, u32[]{:S(2)}, u32[]{:S(2)}) collective-permute-start(f32[6,64]{1,0:T(8,128)S(1)} %stack.174), channel_id=1, source_target_pairs={{0,2},{1,3},{2,0},{3,1},{4,6},{5,7},{6,4},{7,5},{8,10},{9,11},{10,... | collective-permute-start | bytes 4616 | tf_op jit(solution)/shard_map/ppermute | solution.py:28
  (14 other events, 19.6 us)

commit v4 on v3

--- a/solution.py
+++ b/solution.py
@@ -8,9 +8,8 @@
 from jax.sharding import PartitionSpec as P
 
 AXES = ("tv", "sv")
-GROUPS = 2
 SHIFTS = (0, 1, 3, 2)
-TILE = 512
+TILE = 256
 F32 = jnp.float32
 BF16 = jnp.bfloat16
 
@@ -87,15 +86,17 @@
         out[...] = jnp.where(column < words, logits, 0.0)
 
 
-def student_partial(hidden, weights, padded):
+def student_partial(hidden, weights, first, words):
     _, rows, width = hidden.shape
-    depth, words = weights[0].shape
+    depth = weights[0].shape[0]
+    padded = (words // 128 + 1) * 128
+    last = pl.cdiv(weights[0].shape[1], TILE) - 1
     block = pl.BlockSpec((rows, TILE), lambda j: (0, j))
     return pl.pallas_call(
         functools.partial(student_kernel, words),
         grid=(pl.cdiv(padded, TILE),),
         in_specs=[pl.BlockSpec((2, rows, width), lambda j: (0, 0, 0))]
-        + [pl.BlockSpec((depth, TILE), lambda j: (0, j))] * 4,
+        + [pl.BlockSpec((depth, TILE), lambda j: (0, jnp.minimum(j + first, last)))] * 4,
         out_specs=[block, block],
         out_shape=[jax.ShapeDtypeStruct((rows, padded), F32)] * 2,
         scratch_shapes=[pltpu.VMEM((4 * depth, TILE), BF16)],
@@ -165,28 +166,10 @@
     return hidden.reshape(2, 8 * rows, -1)
 
 
-def first_stage(teacher_hidden, student_hidden):
-    width = teacher_hidden.shape[1]
-    pack = jnp.concatenate([teacher_hidden, student_hidden.reshape(-1, width)])
-    return ring(pack, along_z)
-
-
-def all_rows(stage, teacher_shape, student_shape, z, xh, c, xl, y):
-    rows, width = teacher_shape
-    s_rows, s_depth = student_shape
-    student = jnp.concatenate([part[rows:].reshape(s_rows, s_depth) for part in stage], axis=1)
-    student = paired(student, other_xl, xl)
-    teacher = ordered(ring(ordered([part[:rows] for part in stage], z), along_y), y)
-    student = ordered(ring(student, along_y), y)
-    teacher = paired(teacher.reshape(16, rows, width), other_xh, xh, axis=1)
-    teacher = paired(teacher.reshape(32, rows, width), other_core, c, axis=1)
-    return teacher.reshape(4, 16 * rows, width), student_rows(student, z, xh, c)
-
-
-def student_pieces(student_head, z, start, words):
+def student_pieces(student_head, z):
     quarter = student_head.shape[1] // 4
     return [
-        lax.dynamic_slice_in_dim(student_head, ((z + d) % 4) * quarter + start, words, axis=1)
+        lax.dynamic_slice_in_dim(student_head, ((z + d) % 4) * quarter, quarter, axis=1)
         for d in SHIFTS
     ]
 
@@ -195,8 +178,8 @@
     return [p if d == 0 else moved(p, along_z(d)) for d, p in zip(SHIFTS, pieces)]
 
 
-def student_halves(hidden, weights, padded):
-    theirs, ours = student_partial(hidden, weights, padded)
+def student_halves(hidden, weights, first, words):
+    theirs, ours = student_partial(hidden, weights, first, words)
     ours = ours + moved(theirs, other_core)
     half = ours.shape[0] // 2
     return ours[:half], moved(coded(ours[half:]), other_xh)
@@ -213,13 +196,12 @@
     return (ours + decoded(theirs)).astype(BF16)
 
 
-def teacher_place(logits, chunk, padded):
+def teacher_place(logits, chunk):
     rows, part = logits.shape[0] // 16, logits.shape[1]
     logits = lax.all_to_all(logits.reshape(16, rows, part), "tv", 0, 0, tiled=True)
     logits = lax.all_to_all(logits.reshape(8, 2, rows, part), "sv", 0, 0, tiled=True)
-    logits = logits.reshape(2, GROUPS, 2, 2, rows, part)[..., :chunk].transpose(3, 1, 4, 2, 0, 5)
-    logits = logits.reshape(2, GROUPS, rows, 4 * chunk)
-    return jnp.pad(logits, ((0, 0), (0, 0), (0, 0), (0, padded - 4 * chunk)))
+    logits = logits.reshape(2, 4, 2, rows, part)[..., :chunk].transpose(2, 3, 1, 0, 4)
+    return logits.reshape(2, rows, 8 * chunk)
 
 
 def tiled_rows(rows, chunk):
@@ -250,70 +232,77 @@
 
 def shards(teacher_hidden, student_hidden, teacher_head, student_head, token_ids):
     t, s = lax.axis_index("tv"), lax.axis_index("sv")
-    here = place(t, s)
-    z, c = here[0], here[2]
+    z, xh, c, xl, y = place(t, s)
     width = student_head.shape[1]
     quarter = width // 4
     chunk = -(-quarter // 64) * 8
-    sizes = (4 * chunk, quarter - 4 * chunk)
-    padded = (4 * chunk // 128 + 1) * 128
     t_padded = (chunk // 128 + 1) * 128
+    padded = -(-8 * chunk // 128) * 128
+    split = -(-quarter // (2 * TILE))
+    sizes = (split * TILE, quarter - split * TILE)
+    rows, depth = teacher_hidden.shape
     barrier = lax.optimization_barrier
-    xl = here[3]
-
-    stage = first_stage(teacher_hidden, student_hidden)
+
+    t_hidden = ring(teacher_hidden, along_y)
+    s_hidden = ring(student_hidden, along_z)
+    s_pieces = student_pieces(student_head, z)
     tall = teacher_head.T
     t_first = tiled_rows(tall[:8 * chunk], chunk)
-    s_first = student_pieces(student_head, z, 0, sizes[0])
-    stage, t_first, s_first = barrier((stage, t_first, s_first))
-    s_first = sent(s_first)
+    t_hidden = ordered(ring(ordered(t_hidden, y), along_z), z)
+    s_hidden = paired(jnp.concatenate(s_hidden, axis=1), other_xl, xl)
+    t_hidden, s_hidden, s_pieces, t_first = barrier((t_hidden, s_hidden, s_pieces, t_first))
+
+    s_weights = sent(s_pieces)
     t_first = over_y(t_first)
-    t_hidden, s_hidden = all_rows(stage, teacher_hidden.shape, student_hidden.shape, *here)
-
+    t_hidden = t_hidden.transpose(1, 0, 2, 3).reshape(16, rows, depth)
+    t_hidden = paired(t_hidden, other_xh, xh, axis=1)
+    t_hidden, tall = barrier((t_hidden, tall))
+    t_hidden = paired(t_hidden.reshape(32, rows, depth), other_core, c, axis=1)
+    t_hidden = t_hidden.reshape(4, 16 * rows, depth)
     t_second = jnp.pad(tall[quarter:], ((0, 8 * chunk - quarter), (0, 0)))
     t_second = tiled_rows(t_second, chunk)
-    s_second = student_pieces(student_head, z, sizes[0], sizes[1])
-    s_second, t_second, s_first, t_first, t_hidden, s_hidden = barrier(
-        (s_second, t_second, s_first, t_first, t_hidden, s_hidden)
-    )
-    s_second = sent(s_second)
+    s_hidden, t_first = barrier((s_hidden, t_first))
+    s_hidden = over_y(jnp.broadcast_to(s_hidden[None], (4,) + s_hidden.shape))
+    t_second, s_hidden = barrier((t_second, s_hidden))
     t_second = over_y(t_second)
+    s_hidden = student_rows(s_hidden, z, xh, c)
     t_theirs, t_ours = teacher_partial(t_hidden, t_first, xl, t_padded)
     t_first = t_ours, moved(coded(t_theirs), other_xl)
-    s_first = student_halves(s_hidden, s_first, padded)
-
-    s_second, t_second, t_first, s_first = barrier((s_second, t_second, t_first, s_first))
+
+    t_second, t_first, s_hidden = barrier((t_second, t_first, s_hidden))
     t_theirs, t_ours = teacher_partial(t_hidden, t_second, xl, t_padded)
-    t_theirs, t_ours, s_second = barrier((t_theirs, t_ours, s_second))
+    t_theirs, t_ours, s_weights, t_first = barrier((t_theirs, t_ours, s_weights, t_first))
     t_second = t_ours, moved(coded(t_theirs), other_xl)
-    t_first = teacher_place(teacher_logits(*t_first), chunk, padded)
+    t_first = teacher_place(teacher_logits(*t_first), chunk)
+    s_first = student_halves(s_hidden, s_weights, 0, sizes[0])
+    s_second = student_halves(s_hidden, s_weights, split, sizes[1])
     s_first = student_logits(*s_first)
-    s_second = student_halves(s_hidden, s_second, padded)
-    t_second, t_first, s_first, s_second = barrier((t_second, t_first, s_first, s_second))
-    t_second = teacher_place(teacher_logits(*t_second), chunk, padded)
+    t_second, t_first = barrier((t_second, t_first))
+    t_second = teacher_place(teacher_logits(*t_second), chunk)
     s_second = student_logits(*s_second)
 
-    teacher = jnp.stack([t_first, t_second], axis=1).reshape(4, GROUPS, -1, padded).astype(F32)
+    teacher = jnp.stack([t_first, t_second], axis=1).reshape(4, rows, 8 * chunk)
+    teacher = jnp.pad(teacher, ((0, 0), (0, 0), (0, padded - 8 * chunk))).astype(F32)
     student = jnp.zeros(teacher.shape, F32)
-    for g, parts in enumerate((s_first, s_second)):
+    for start, parts in ((0, s_first), (sizes[0], s_second)):
         for d, part in zip(SHIFTS, parts):
             part = part if d == 0 else decoded(part)
-            student = lax.dynamic_update_slice(student, part[None, None], ((z - d) % 4, g, 0, 0))
-    column = lax.broadcasted_iota(jnp.int32, student.shape, 3)
-    group = lax.broadcasted_iota(jnp.int32, student.shape, 1)
-    index = lax.broadcasted_iota(jnp.int32, student.shape, 0) * quarter + group * sizes[0] + column
-    real = column < jnp.where(group == 0, sizes[0], sizes[1])
+            part = part[:, :min(part.shape[1], sizes[0] if start == 0 else padded - start)]
+            student = lax.dynamic_update_slice(student, part[None], ((z - d) % 4, 0, start))
+    column = lax.broadcasted_iota(jnp.int32, student.shape, 2)
+    index = lax.broadcasted_iota(jnp.int32, student.shape, 0) * quarter + column
+    real = column < quarter
     student = jnp.where(real, student, -1e30)
     teacher = jnp.where(real, teacher, -1e30)
     gap = student - teacher
     chosen = real & (s * width + index == token_ids[:, None])
-    picked = jnp.sum(jnp.where(chosen, gap, 0.0), axis=(0, 1, 3))
-    peak_s = jnp.max(student, axis=(0, 1, 3))
-    peak_t = jnp.max(teacher, axis=(0, 1, 3))
+    picked = jnp.sum(jnp.where(chosen, gap, 0.0), axis=(0, 2))
+    peak_s = jnp.max(student, axis=(0, 2))
+    peak_t = jnp.max(teacher, axis=(0, 2))
     raw = jnp.exp(student - peak_s[:, None])
-    mass_s = jnp.sum(raw, axis=(0, 1, 3))
-    mass_t = jnp.sum(jnp.exp(teacher - peak_t[:, None]), axis=(0, 1, 3))
-    cross = jnp.sum(raw * gap, axis=(0, 1, 3))
+    mass_s = jnp.sum(raw, axis=(0, 2))
+    mass_t = jnp.sum(jnp.exp(teacher - peak_t[:, None]), axis=(0, 2))
+    cross = jnp.sum(raw * gap, axis=(0, 2))
     stats = jnp.stack([peak_s, mass_s, cross, peak_t, mass_t, picked])
     stats = pooled(stats, moved(stats, other_xl))
     stats = functools.reduce(pooled, ring(stats, along_y))
@@ -324,7 +313,7 @@
     rewards = norm_s - norm_t - stats[5]
     prob = jnp.exp(student - norm_s[:, None])
     grad = (prob * (gap - mean_gap[:, None])).astype(BF16)
-    pieces = [grad[q, g, :, :sizes[g]] for q in range(4) for g in range(GROUPS)]
+    pieces = [grad[q, :, :quarter] for q in range(4)]
     return rewards, kl_div, jnp.concatenate(pieces, axis=1)
 
 

time: 509 us -> 563 us (1.11)
  waiting for transfers between devices: 214 us -> 281 us
  blocking collectives: 0 us -> 41.8 us
  local copies, waits for them, and re-layouts: 85.6 us -> 53.5 us
  starting transfers between devices: 97.8 us -> 73.8 us
  Pallas kernels: 41.2 us -> 47.7 us
  other arithmetic: 58.4 us -> 52.5 us
    all_to_all x2 -> x3, waiting for transfers between devices: 0.01 us -> 83.2 us  [over_y(): lax.all_to_all(pieces, 'sv', 0, 0, axis_index_groups=groups, tiled=True)]
    all_to_all x0 -> x1, blocking collectives: none -> 41.8 us  [teacher_place(): lax.all_to_all(logits.reshape(8, 2, rows, part), 'sv', 0, 0, tiled=True)]
    all_to_all x2 -> x1, waiting for transfers between devices: 30.4 us -> 7.42 us  [teacher_place(): lax.all_to_all(logits.reshape(8, 2, rows, part), 'sv', 0, 0, tiled=True)]
    all_to_all x2, waiting for transfers between devices: 14 us -> 33.6 us  [teacher_place(): lax.all_to_all(logits.reshape(16, rows, part), 'tv', 0, 0, tiled=True)]
    unnamed x100 -> x53, local copies, waits for them, and re-layouts: 26.2 us -> 9.34 us
    ppermute x34 -> x31, waiting for transfers between devices: 170 us -> 157 us  [moved(): return lax.ppermute(x, AXES, pairs)]
    all_to_all x2 -> x1, starting transfers between devices: 13.7 us -> 5 us  [teacher_place(): lax.all_to_all(logits.reshape(8, 2, rows, part), 'sv', 0, 0, tiled=True)]
    all_to_all x2 -> x3, starting transfers between devices: 22.1 us -> 13.7 us  [over_y(): lax.all_to_all(pieces, 'sv', 0, 0, axis_index_groups=groups, tiled=True)]
  transfers between devices with their start and end apart: 40 -> 37, of which waited for: 16 -> 18; matrix products, arithmetic and copies ran while one was open for 20% -> 15% of each run, Pallas kernels for 2% -> 6%
where the time goes in v4:
time: 563 us; the launch traced here: 552 us
  waiting for transfers between devices  281 us (50%)
  starting transfers between devices  73.8 us (13%)
  local copies, waits for them, and re-layouts  53.5 us (10%)
  other arithmetic  52.5 us (9%)
  Pallas kernels  47.7 us (8%)
  blocking collectives  41.8 us (7%)
    ppermute x31, waiting for transfers between devices, moved(): return lax.ppermute(x, AXES, pairs)  157 us
    all_to_all x3, waiting for transfers between devices, over_y(): lax.all_to_all(pieces, 'sv', 0, 0, axis_index_groups=groups, tiled=True)  83.2 us
    all_to_all x1, blocking collectives, teacher_place(): lax.all_to_all(logits.reshape(8, 2, rows, part), 'sv', 0, 0, tiled=True)  41.8 us
    ppermute x31, starting transfers between devices, moved(): return lax.ppermute(x, AXES, pairs)  40.7 us
    all_to_all x2, waiting for transfers between devices, teacher_place(): lax.all_to_all(logits.reshape(16, rows, part), 'tv', 0, 0, tiled=True)  33.6 us
    pallas_call x2, Pallas kernels, student_partial(): pl.pallas_call(functools.partial(student_kernel, words), grid=(pl.cdiv(pa...  26.8 us
    pallas_call x2, Pallas kernels, teacher_partial(): pl.pallas_call(functools.partial(teacher_kernel, words), grid_spec=pltpu....  20.9 us
    all_to_all x2, starting transfers between devices, teacher_place(): lax.all_to_all(logits.reshape(16, rows, part), 'tv', 0, 0, tiled=True)  14.4 us
  transfers between devices with their start and end apart: 37, of which 18 were waited for; matrix products, arithmetic and copies ran while one was open for 15% of the time, Pallas kernels for 6%

profile of v4, /device:TPU:6, one launch (start us, length us, event | category | flops | bytes accessed | tf_op | source)
XLA Modules:
  0.0 552.3 jit_solution(15324515781551479369)
XLA Ops:
  0.6 3.1 collective-permute-start
  5.3 1.9 collective-permute-start.6
  7.2 2.1 collective-permute-start.7
  9.4 4.9 slice.238
  14.2 5.1 pad.15
  19.4 11.3 %constant_dynamic-slice_fusion = (bf16[320,4748]{1,0:T(8,128)(2,1)}, bf16[320,4748]{1,0:T(8,128)(2,1)}, bf16[320,4748]{1,0:T(8,128)(2,1)}, bf16[320,4748]{1,0:T(8,128)(2,1)}) fusion(bf16[320,18992]{1,0:T(8,128)(2,1)} %param.8, s32[]{:T(128)S(6)} %select_n.204, s32[]{:T(128)S(6)} %select_n.200, s32[]{:T(128)S(6)} %select_n.198, s32[]{:T(128)S(6)} %select_n.202), kind=kLoop, calls=%fused_computation.99 | loop fusion | bytes 24309776 | tf_op jit(solution)/shard_map/dynamic_slice | solution.py:172
  30.7 1.9 collective-permute-start.8
  33.6 2.4 collective-permute-start.4
  38.5 4.1 collective-permute-done.3
  42.6 1.7 collective-permute-done.4
  44.4 3.4 collective-permute-done.5
  49.2 5.0 all-to-all-start
  55.7 56.0 %all-to-all-done.weights = bf16[4,1216,512]{2,1,0:T(8,128)(2,1)} async-done(((bf16[4,1216,512]{2,1,0:T(8,128)(2,1)}), bf16[4,1216,512]{2,1,0:T(8,128)(2,1)}, u32[]{:S(2)}, u32[]{:S(2)}) %all-to-all-start) | async-done | bytes 4980768 | tf_op jit(solution)/shard_map/all_to_all | solution.py:215
  112.0 1.6 broadcast_in_dim.115
  113.6 3.7 all-to-all-start.1
  117.3 2.6 maximum_select_fusion.1
  121.5 3.6 slice.182
  125.3 2.8 pad.17
  128.2 20.4 %all-to-all-done.1 = bf16[4,2,128,1280]{3,2,1,0:T(8,128)(2,1)S(1)} async-done(((bf16[4,2,128,1280]{3,2,1,0:T(8,128)(2,1)}), bf16[4,2,128,1280]{3,2,1,0:T(8,128)(2,1)S(1)}, u32[]{:S(2)}, u32[]{:S(2)}) %all-to-all-start.1) | async-done | bytes 2621472 | tf_op jit(solution)/shard_map/all_to_all | solution.py:215
  148.5 5.0 all-to-all-start.2
  153.9 3.2 collective-permute-start.14
  157.7 4.2 maximum_select_fusion
  162.4 10.6 %shard_map.76 = (f32[1024,640]{1,0:T(8,128)S(1)}, f32[1024,640]{1,0:T(8,128)S(1)}) custom-call(s32[1]{0:T(128)} %bitcast.22.here, bf16[4,1024,512]{2,1,0:T(8,128)(2,1)S(1)} %bitcast.367, bf16[4,1216,512]{2,1,0:T(8,128)(2,1)} %all-to-all-done.weights), custom_call_target="tpu_custom_call" | custom-call | flops 5100273664 | bytes 18612224 | tf_op jit(solution)/shard_map/pallas_call | solution.py:136
  176.8 2.5 fusion.4
  179.2 23.3 %collective-permute-done.12 = s16[1024,640]{1,0:T(8,128)(2,1)} collective-permute-done((s16[1024,640]{1,0:T(8,128)(2,1)S(1)}, s16[1024,640]{1,0:T(8,128)(2,1)}, u32[]{:S(2)}, u32[]{:S(2)}) %collective-permute-start.12) | collective-permute-done | bytes 1310752 | tf_op jit(solution)/shard_map/ppermute | solution.py:27
  202.5 6.8 %all-to-all-done.2.weights = bf16[4,1216,512]{2,1,0:T(8,128)(2,1)} async-done(((bf16[4,1216,512]{2,1,0:T(8,128)(2,1)}), bf16[4,1216,512]{2,1,0:T(8,128)(2,1)}, u32[]{:S(2)}, u32[]{:S(2)}) %all-to-all-start.2) | async-done | bytes 4980768 | tf_op jit(solution)/shard_map/all_to_all | solution.py:215
  209.3 2.2 copy-done.1
  211.5 10.3 %shard_map.77 = (f32[1024,640]{1,0:T(8,128)S(1)}, f32[1024,640]{1,0:T(8,128)S(1)}) custom-call(s32[1]{0:T(128)} %bitcast.22.here, bf16[4,1024,512]{2,1,0:T(8,128)(2,1)S(1)} %bitcast.368, bf16[4,1216,512]{2,1,0:T(8,128)(2,1)} %all-to-all-done.2.weights), custom_call_target="tpu_custom_call" | custom-call | flops 5100273664 | bytes 18612224 | tf_op jit(solution)/shard_map/pallas_call | solution.py:136
  221.8 67.7 %collective-permute-done.13.w1 = bf16[320,4748]{1,0:T(8,128)(2,1)} collective-permute-done((bf16[320,4748]{1,0:T(8,128)(2,1)}, bf16[320,4748]{1,0:T(8,128)(2,1)}, u32[]{:S(2)}, u32[]{:S(2)}) %collective-permute-start.13) | collective-permute-done | bytes 3038752 | tf_op jit(solution)/shard_map/ppermute | solution.py:27
  289.5 1.7 copy-done.7
  291.2 12.2 %shard_map.79 = (f32[512,2304]{1,0:T(8,128)}, f32[512,2304]{1,0:T(8,128)}) custom-call(bf16[2,512,1280]{2,1,0:T(8,128)(2,1)S(1)} %bitcast.369, bf16[320,4748]{1,0:T(8,128)(2,1)S(1)} %copy-done.2, bf16[320,4748]{1,0:T(8,128)(2,1)} %collective-permute-done.13.w1, bf16[320,4748]{1,0:T(8,128)(2,1)} %collective-permute-done.14.w2, ...), custom_call_target="tpu_custom_call" | custom-call | flops 5735710720 | bytes 14563328 | tf_op jit(solution)/shard_map/pallas_call | solution.py:95
  303.5 14.6 %shard_map.78 = (f32[512,2688]{1,0:T(8,128)}, f32[512,2688]{1,0:T(8,128)}) custom-call(bf16[2,512,1280]{2,1,0:T(8,128)(2,1)S(1)} %bitcast.370, bf16[320,4748]{1,0:T(8,128)(2,1)S(1)} %copy-done.2, bf16[320,4748]{1,0:T(8,128)(2,1)} %collective-permute-done.13.w1, bf16[320,4748]{1,0:T(8,128)(2,1)} %collective-permute-done.14.w2, ...), custom_call_target="tpu_custom_call" | custom-call | flops 6710886400 | bytes 17039360 | tf_op jit(solution)/shard_map/pallas_call | solution.py:95
  319.8 2.9 add_convert_fusion.1
  322.7 7.2 %all-to-all-start.3 = ((bf16[16,64,640]{2,1,0:T(8,128)(2,1)}), bf16[16,64,640]{2,1,0:T(8,128)(2,1)}, u32[]{:S(2)}, u32[]{:S(2)}) async-start(bf16[16,64,640]{2,1,0:T(8,128)(2,1)} %bitcast.389), calls=%async_computation.3 | async-start | bytes 2621440 | tf_op jit(solution)/shard_map/all_to_all | solution.py:201
  330.2 1.9 select_convert_fusion.1
  332.9 15.3 %all-to-all-done.3 = bf16[16,64,640]{2,1,0:T(8,128)(2,1)} async-done(((bf16[16,64,640]{2,1,0:T(8,128)(2,1)}), bf16[16,64,640]{2,1,0:T(8,128)(2,1)}, u32[]{:S(2)}, u32[]{:S(2)}) %all-to-all-start.3) | async-done | bytes 1310752 | tf_op jit(solution)/shard_map/all_to_all | solution.py:201
  348.2 41.8 %all_to_all.35 = bf16[8,2,64,640]{3,2,1,0:T(8,128)(2,1)S(1)} all-to-all(bf16[8,2,64,640]{3,2,1,0:T(8,128)(2,1)} %bitcast.42), channel_id=1, replica_groups=mesh['tv'=16,'sv'=8] {'sv'}, dimensions={0} | all-to-all | bytes 2621440 | tf_op jit(solution)/shard_map/all_to_all | solution.py:202
  390.0 2.4 copy.45
  392.4 4.4 reshape.441
  398.2 2.9 add_convert_fusion
  401.1 7.2 %all-to-all-start.5 = ((bf16[16,64,640]{2,1,0:T(8,128)(2,1)}), bf16[16,64,640]{2,1,0:T(8,128)(2,1)}, u32[]{:S(2)}, u32[]{:S(2)}) async-start(bf16[16,64,640]{2,1,0:T(8,128)(2,1)} %bitcast.388), calls=%async_computation.5 | async-start | bytes 2621440 | tf_op jit(solution)/shard_map/all_to_all | solution.py:201
  408.4 18.3 %all-to-all-done.5 = bf16[16,64,640]{2,1,0:T(8,128)(2,1)} async-done(((bf16[16,64,640]{2,1,0:T(8,128)(2,1)}), bf16[16,64,640]{2,1,0:T(8,128)(2,1)}, u32[]{:S(2)}, u32[]{:S(2)}) %all-to-all-start.5) | async-done | bytes 1310752 | tf_op jit(solution)/shard_map/all_to_all | solution.py:201
  426.7 5.0 all-to-all-start.6
  431.7 4.3 add.393
  436.3 2.2 select_convert_fusion.3
  438.5 3.4 collective-permute-start.22
  441.9 7.4 %all-to-all-done.6 = bf16[8,2,64,640]{3,2,1,0:T(8,128)(2,1)S(1)} async-done(((bf16[8,2,64,640]{3,2,1,0:T(8,128)(2,1)}), bf16[8,2,64,640]{3,2,1,0:T(8,128)(2,1)S(1)}, u32[]{:S(2)}, u32[]{:S(2)}) %all-to-all-start.6) | async-done | bytes 1310752 | tf_op jit(solution)/shard_map/all_to_all | solution.py:202
  450.6 1.8 stack_reshape.13
  452.5 4.9 add.380
  458.5 2.9 collective-permute-start.17
  461.4 14.9 %collective-permute-done.22 = s16[256,2304]{1,0:T(8,128)(2,1)} collective-permute-done((s16[256,2304]{1,0:T(8,128)(2,1)}, s16[256,2304]{1,0:T(8,128)(2,1)}, u32[]{:S(2)}, u32[]{:S(2)}) %collective-permute-start.22) | collective-permute-done | bytes 1179680 | tf_op jit(solution)/shard_map/ppermute | solution.py:27
  477.4 1.8 slice_add_fusion.1
  480.1 3.5 collective-permute-start.24
  483.8 10.3 %collective-permute-done.23 = s16[64,2304]{1,0:T(8,128)(2,1)S(1)} collective-permute-done((s16[64,2304]{1,0:T(8,128)(2,1)S(1)}, s16[64,2304]{1,0:T(8,128)(2,1)S(1)}, u32[]{:S(2)}, u32[]{:S(2)}) %collective-permute-start.23) | collective-permute-done | bytes 294944 | tf_op jit(solution)/shard_map/ppermute | solution.py:27
  494.7 9.6 %collective-permute-done.17 = s16[256,2688]{1,0:T(8,128)(2,1)S(1)} collective-permute-done((s16[256,2688]{1,0:T(8,128)(2,1)S(1)}, s16[256,2688]{1,0:T(8,128)(2,1)S(1)}, u32[]{:S(2)}, u32[]{:S(2)}) %collective-permute-start.17) | collective-permute-done | bytes 1376288 | tf_op jit(solution)/shard_map/ppermute | solution.py:27
  506.1 3.2 collective-permute-start.19
  509.8 13.6 %collective-permute-done.18 = s16[64,2688]{1,0:T(8,128)(2,1)S(1)} collective-permute-done((s16[64,2688]{1,0:T(8,128)(2,1)S(1)}, s16[64,2688]{1,0:T(8,128)(2,1)S(1)}, u32[]{:S(2)}, u32[]{:S(2)}) %collective-permute-start.18) | collective-permute-done | bytes 344096 | tf_op jit(solution)/shard_map/ppermute | solution.py:27
  527.0 3.6 multiply_reduce_fusion
  530.8 3.6 collective-permute-done.27
  535.9 1.8 collective-permute-start.29
  537.7 1.8 collective-permute-start.30
  539.5 3.3 collective-permute-done.30
  543.4 4.0 multiply_convert_fusion
  547.6 4.0 concatenate.11
  (155 shorter events, 33.3 us)
Async XLA Ops:
  0.6 30.0 %collective-permute-start = (bf16[64,512]{1,0:T(8,128)(2,1)}, bf16[64,512]{1,0:T(8,128)(2,1)S(1)}, u32[]{:S(2)}, u32[]{:S(2)}) collective-permute-start(bf16[64,512]{1,0:T(8,128)(2,1)} %param.5), channel_id=1, source_target_pairs={{0,3},{1,0},{2,1},{3,2},{4,7},{5,4},{6,5},{7,6},{8,11},{9,8},{10,9... | collective-permute-start | bytes 196616 | tf_op jit(solution)/shard_map/ppermute | solution.py:27
  3.7 28.9 %collective-permute-start.1 = (bf16[64,512]{1,0:T(8,128)(2,1)}, bf16[64,512]{1,0:T(8,128)(2,1)S(1)}, u32[]{:S(2)}, u32[]{:S(2)}) collective-permute-start(bf16[64,512]{1,0:T(8,128)(2,1)} %param.5), channel_id=1, source_target_pairs={{0,2},{1,3},{2,0},{3,1},{4,6},{5,7},{6,4},{7,5},{8,10},{9,11},{10,... | collective-permute-start | bytes 196616 | tf_op jit(solution)/shard_map/ppermute | solution.py:27
  4.3 28.3 %collective-permute-start.2 = (bf16[64,512]{1,0:T(8,128)(2,1)}, bf16[64,512]{1,0:T(8,128)(2,1)S(1)}, u32[]{:S(2)}, u32[]{:S(2)}) collective-permute-start(bf16[64,512]{1,0:T(8,128)(2,1)} %param.5), channel_id=1, source_target_pairs={{0,1},{1,2},{2,3},{3,0},{4,5},{5,6},{6,7},{7,4},{8,9},{9,10},{10,1... | collective-permute-start | bytes 196616 | tf_op jit(solution)/shard_map/ppermute | solution.py:27
  5.3 30.6 %collective-permute-start.6 = (bf16[128,320]{0,1:T(8,128)(2,1)}, bf16[128,320]{0,1:T(8,128)(2,1)S(1)}, u32[]{:S(2)}, u32[]{:S(2)}) collective-permute-start(bf16[128,320]{0,1:T(8,128)(2,1)} %param.6), channel_id=1, source_target_pairs={{0,32},{1,33},{2,34},{3,35},{4,36},{5,37},{6,38},{7,39},{8,40},{9,... | collective-permute-start | bytes 245768 | tf_op jit(solution)/shard_map/ppermute | solution.py:27
  7.2 28.7 %collective-permute-start.7 = (bf16[128,320]{0,1:T(8,128)(2,1)}, bf16[128,320]{0,1:T(8,128)(2,1)S(1)}, u32[]{:S(2)}, u32[]{:S(2)}) collective-permute-start(bf16[128,320]{0,1:T(8,128)(2,1)} %param.6), channel_id=1, source_target_pairs={{0,96},{1,97},{2,98},{3,99},{4,100},{5,101},{6,102},{7,103},{8,104... | collective-permute-start | bytes 245768 | tf_op jit(solution)/shard_map/ppermute | solution.py:27
  19.4 11.3 %copy-start.13 = (bf16[128,320]{0,1:T(8,128)(2,1)S(1)}, bf16[128,320]{0,1:T(8,128)(2,1)}, u32[]{:S(2)}) copy-start(bf16[128,320]{0,1:T(8,128)(2,1)} %param.6) | copy-start | bytes 245764
  19.4 13.3 %copy-start.12 = (bf16[64,512]{1,0:T(8,128)(2,1)S(1)}, bf16[64,512]{1,0:T(8,128)(2,1)}, u32[]{:S(2)}) copy-start(bf16[64,512]{1,0:T(8,128)(2,1)} %param.5) | copy-start | bytes 196612
  30.7 6.9 %collective-permute-start.8 = (bf16[128,320]{0,1:T(8,128)(2,1)S(1)}, bf16[128,320]{0,1:T(8,128)(2,1)S(1)}, u32[]{:S(2)}, u32[]{:S(2)}) collective-permute-start(bf16[128,320]{0,1:T(8,128)(2,1)S(1)} %copy-done.13), channel_id=1, source_target_pairs={{0,64},{1,65},{2,66},{3,67},{4,68},{5,69},{6,70},{7,71},{8,72},{9,... | collective-permute-start | bytes 245768 | tf_op jit(solution)/shard_map/ppermute | solution.py:27
  32.8 9.8 %collective-permute-start.3 = (bf16[4,64,512]{2,1,0:T(8,128)(2,1)S(1)}, bf16[4,64,512]{2,1,0:T(8,128)(2,1)S(1)}, u32[]{:S(2)}, u32[]{:S(2)}) collective-permute-start(bf16[4,64,512]{2,1,0:T(8,128)(2,1)S(1)} %constant_dynamic-slice_fusion.5), channel_id=1, source_target_pairs={{0,96},{1,97},{2,98},{3,99},{4,100},{5,101},{6,102},{7,103},{8,104... | collective-permute-start | bytes 786440 | tf_op jit(solution)/shard_map/ppermute | solution.py:27
  33.6 10.8 %collective-permute-start.4 = (bf16[4,64,512]{2,1,0:T(8,128)(2,1)S(1)}, bf16[4,64,512]{2,1,0:T(8,128)(2,1)S(1)}, u32[]{:S(2)}, u32[]{:S(2)}) collective-permute-start(bf16[4,64,512]{2,1,0:T(8,128)(2,1)S(1)} %constant_dynamic-slice_fusion.5), channel_id=1, source_target_pairs={{0,64},{1,65},{2,66},{3,67},{4,68},{5,69},{6,70},{7,71},{8,72},{9,... | collective-permute-start | bytes 786440 | tf_op jit(solution)/shard_map/ppermute | solution.py:27
  36.0 11.9 %collective-permute-start.5 = (bf16[4,64,512]{2,1,0:T(8,128)(2,1)S(1)}, bf16[4,64,512]{2,1,0:T(8,128)(2,1)S(1)}, u32[]{:S(2)}, u32[]{:S(2)}) collective-permute-start(bf16[4,64,512]{2,1,0:T(8,128)(2,1)S(1)} %constant_dynamic-slice_fusion.5), channel_id=1, source_target_pairs={{0,32},{1,33},{2,34},{3,35},{4,36},{5,37},{6,38},{7,39},{8,40},{9,... | collective-permute-start | bytes 786440 | tf_op jit(solution)/shard_map/ppermute | solution.py:27
  37.6 11.5 %collective-permute-start.9 = (bf16[128,1280]{0,1:T(8,128)(2,1)S(1)}, bf16[128,1280]{0,1:T(8,128)(2,1)S(1)}, u32[]{:S(2)}, u32[]{:S(2)}) collective-permute-start(bf16[128,1280]{0,1:T(8,128)(2,1)S(1)} %constant_dynamic-update-slice_fusion), channel_id=1, source_target_pairs={{0,4},{1,5},{2,6},{3,7},{4,0},{5,1},{6,2},{7,3},{8,12},{9,13},{10,... | collective-permute-start | bytes 983048 | tf_op jit(solution)/shard_map/ppermute | solution.py:27
  49.2 62.5 %all-to-all-start = ((bf16[4,1216,512]{2,1,0:T(8,128)(2,1)}), bf16[4,1216,512]{2,1,0:T(8,128)(2,1)}, u32[]{:S(2)}, u32[]{:S(2)}) async-start(bf16[4,1216,512]{2,1,0:T(8,128)(2,1)} %bitcast.376), calls=%async_computation | async-start | bytes 9961472 | tf_op jit(solution)/shard_map/all_to_all | solution.py:215
  54.2 63.1 %collective-permute-start.10 = (bf16[16,64,512]{2,1,0:T(8,128)(2,1)}, bf16[16,64,512]{2,1,0:T(8,128)(2,1)}, u32[]{:S(2)}, u32[]{:S(2)}) collective-permute-start(bf16[16,64,512]{2,1,0:T(8,128)(2,1)} %bitcast.17), channel_id=1, source_target_pairs={{0,16},{1,17},{2,18},{3,19},{4,20},{5,21},{6,22},{7,23},{8,24},{9,... | collective-permute-start | bytes 3145736 | tf_op jit(solution)/shard_map/ppermute | solution.py:27
  113.6 34.9 %all-to-all-start.1 = ((bf16[4,2,128,1280]{3,2,1,0:T(8,128)(2,1)}), bf16[4,2,128,1280]{3,2,1,0:T(8,128)(2,1)S(1)}, u32[]{:S(2)}, u32[]{:S(2)}) async-start(bf16[4,2,128,1280]{3,2,1,0:T(8,128)(2,1)} %broadcast_in_dim.115), calls=%async_computation.1 | async-start | bytes 5242880 | tf_op jit(solution)/shard_map/all_to_all | solution.py:215
  121.4 36.3 %collective-permute-start.11 = (bf16[32,64,512]{2,1,0:T(8,128)(2,1)}, bf16[32,64,512]{2,1,0:T(8,128)(2,1)}, u32[]{:S(2)}, u32[]{:S(2)}) collective-permute-start(bf16[32,64,512]{2,1,0:T(8,128)(2,1)} %bitcast.24), channel_id=1, source_target_pairs={{0,8},{1,9},{2,10},{3,11},{4,12},{5,13},{6,14},{7,15},{8,0},{9,1},... | collective-permute-start | bytes 6291464 | tf_op jit(solution)/shard_map/ppermute | solution.py:27
  148.5 60.7 %all-to-all-start.2 = ((bf16[4,1216,512]{2,1,0:T(8,128)(2,1)}), bf16[4,1216,512]{2,1,0:T(8,128)(2,1)}, u32[]{:S(2)}, u32[]{:S(2)}) async-start(bf16[4,1216,512]{2,1,0:T(8,128)(2,1)} %bitcast.377), calls=%async_computation.2 | async-start | bytes 9961472 | tf_op jit(solution)/shard_map/all_to_all | solution.py:215
  153.6 135.9 %collective-permute-start.13 = (bf16[320,4748]{1,0:T(8,128)(2,1)}, bf16[320,4748]{1,0:T(8,128)(2,1)}, u32[]{:S(2)}, u32[]{:S(2)}) collective-permute-start(bf16[320,4748]{1,0:T(8,128)(2,1)} %get-tuple-element.55), channel_id=1, source_target_pairs={{0,32},{1,33},{2,34},{3,35},{4,36},{5,37},{6,38},{7,39},{8,40},{9,... | collective-permute-start | bytes 9116168 | tf_op jit(solution)/shard_map/ppermute | solution.py:27
  153.9 135.5 %collective-permute-start.14 = (bf16[320,4748]{1,0:T(8,128)(2,1)}, bf16[320,4748]{1,0:T(8,128)(2,1)}, u32[]{:S(2)}, u32[]{:S(2)}) collective-permute-start(bf16[320,4748]{1,0:T(8,128)(2,1)} %get-tuple-element.56), channel_id=1, source_target_pairs={{0,96},{1,97},{2,98},{3,99},{4,100},{5,101},{6,102},{7,103},{8,104... | collective-permute-start | bytes 9116168 | tf_op jit(solution)/shard_map/ppermute | solution.py:27
  157.2 132.3 %collective-permute-start.15 = (bf16[320,4748]{1,0:T(8,128)(2,1)}, bf16[320,4748]{1,0:T(8,128)(2,1)}, u32[]{:S(2)}, u32[]{:S(2)}) collective-permute-start(bf16[320,4748]{1,0:T(8,128)(2,1)} %get-tuple-element.57), channel_id=1, source_target_pairs={{0,64},{1,65},{2,66},{3,67},{4,68},{5,69},{6,70},{7,71},{8,72},{9,... | collective-permute-start | bytes 9116168 | tf_op jit(solution)/shard_map/ppermute | solution.py:27
  162.4 10.7 %copy-start = (bf16[32,2,64,512]{3,2,1,0:T(8,128)(2,1)}, bf16[32,2,64,512]{3,2,1,0:T(8,128)(2,1)S(1)}, u32[]{:S(2)}) copy-start(bf16[32,2,64,512]{3,2,1,0:T(8,128)(2,1)S(1)} %copy.36) | copy-start | bytes 12582916
  173.1 1.5 copy-start.5
  174.6 27.9 %collective-permute-start.12 = (s16[1024,640]{1,0:T(8,128)(2,1)S(1)}, s16[1024,640]{1,0:T(8,128)(2,1)}, u32[]{:S(2)}, u32[]{:S(2)}) collective-permute-start(s16[1024,640]{1,0:T(8,128)(2,1)S(1)} %select_convert_fusion.2), channel_id=1, source_target_pairs={{0,4},{1,5},{2,6},{3,7},{4,0},{5,1},{6,2},{7,3},{8,12},{9,13},{10,... | collective-permute-start | bytes 3932168 | tf_op jit(solution)/shard_map/ppermute | solution.py:27
  209.3 2.2 copy-start.1
  211.5 78.0 %copy-start.2 = (bf16[320,4748]{1,0:T(8,128)(2,1)S(1)}, bf16[320,4748]{1,0:T(8,128)(2,1)}, u32[]{:S(2)}) copy-start(bf16[320,4748]{1,0:T(8,128)(2,1)} %get-tuple-element.60.w0) | copy-start | bytes 9116164
  221.8 81.7 %copy-start.3 = (f32[1024,640]{1,0:T(8,128)}, f32[1024,640]{1,0:T(8,128)S(1)}, u32[]{:S(2)}) copy-start(f32[1024,640]{1,0:T(8,128)S(1)} %get-tuple-element.73) | copy-start | bytes 7864324
  289.5 1.7 copy-start.7
  303.4 16.3 %copy-start.6 = (f32[1024,640]{1,0:T(8,128)S(1)}, f32[1024,640]{1,0:T(8,128)}, u32[]{:S(2)}) copy-start(f32[1024,640]{1,0:T(8,128)} %copy-done.5) | copy-start | bytes 7864324
  303.4 128.2 %collective-permute-start.21 = (f32[512,2304]{1,0:T(8,128)}, f32[512,2304]{1,0:T(8,128)}, u32[]{:S(2)}, u32[]{:S(2)}) collective-permute-start(f32[512,2304]{1,0:T(8,128)} %get-tuple-element.67), channel_id=1, source_target_pairs={{0,8},{1,9},{2,10},{3,11},{4,12},{5,13},{6,14},{7,15},{8,0},{9,1},... | collective-permute-start | bytes 14155784 | tf_op jit(solution)/shard_map/ppermute | solution.py:27
  318.1 134.3 %collective-permute-start.16 = (f32[512,2688]{1,0:T(8,128)}, f32[512,2688]{1,0:T(8,128)}, u32[]{:S(2)}, u32[]{:S(2)}) collective-permute-start(f32[512,2688]{1,0:T(8,128)} %get-tuple-element.65), channel_id=1, source_target_pairs={{0,8},{1,9},{2,10},{3,11},{4,12},{5,13},{6,14},{7,15},{8,0},{9,1},... | collective-permute-start | bytes 16515080 | tf_op jit(solution)/shard_map/ppermute | solution.py:27
  322.7 25.5 %all-to-all-start.3 = ((bf16[16,64,640]{2,1,0:T(8,128)(2,1)}), bf16[16,64,640]{2,1,0:T(8,128)(2,1)}, u32[]{:S(2)}, u32[]{:S(2)}) async-start(bf16[16,64,640]{2,1,0:T(8,128)(2,1)} %bitcast.389), calls=%async_computation.3 | async-start | bytes 2621440 | tf_op jit(solution)/shard_map/all_to_all | solution.py:201
  332.1 64.8 %collective-permute-start.26 = (s16[1024,640]{1,0:T(8,128)(2,1)}, s16[1024,640]{1,0:T(8,128)(2,1)}, u32[]{:S(2)}, u32[]{:S(2)}) collective-permute-start(s16[1024,640]{1,0:T(8,128)(2,1)} %select_convert_fusion.1), channel_id=1, source_target_pairs={{0,4},{1,5},{2,6},{3,7},{4,0},{5,1},{6,2},{7,3},{8,12},{9,13},{10,... | collective-permute-start | bytes 3932168 | tf_op jit(solution)/shard_map/ppermute | solution.py:27
  390.0 8.2 %copy-start.4 = (f32[1024,640]{1,0:T(8,128)S(1)}, f32[1024,640]{1,0:T(8,128)}, u32[]{:S(2)}) copy-start(f32[1024,640]{1,0:T(8,128)} %copy-done.3) | copy-start | bytes 7864324
  401.1 25.5 %all-to-all-start.5 = ((bf16[16,64,640]{2,1,0:T(8,128)(2,1)}), bf16[16,64,640]{2,1,0:T(8,128)(2,1)}, u32[]{:S(2)}, u32[]{:S(2)}) async-start(bf16[16,64,640]{2,1,0:T(8,128)(2,1)} %bitcast.388), calls=%async_computation.5 | async-start | bytes 2621440 | tf_op jit(solution)/shard_map/all_to_all | solution.py:201
  426.7 22.6 %all-to-all-start.6 = ((bf16[8,2,64,640]{3,2,1,0:T(8,128)(2,1)}), bf16[8,2,64,640]{3,2,1,0:T(8,128)(2,1)S(1)}, u32[]{:S(2)}, u32[]{:S(2)}) async-start(bf16[8,2,64,640]{3,2,1,0:T(8,128)(2,1)} %bitcast.47), calls=%async_computation.6 | async-start | bytes 2621440 | tf_op jit(solution)/shard_map/all_to_all | solution.py:202
  436.0 2.5 copy-start.9
  438.5 37.8 %collective-permute-start.22 = (s16[256,2304]{1,0:T(8,128)(2,1)}, s16[256,2304]{1,0:T(8,128)(2,1)}, u32[]{:S(2)}, u32[]{:S(2)}) collective-permute-start(s16[256,2304]{1,0:T(8,128)(2,1)} %select_convert_fusion.3), channel_id=1, source_target_pairs={{0,16},{1,17},{2,18},{3,19},{4,20},{5,21},{6,22},{7,23},{8,24},{9,... | collective-permute-start | bytes 3538952 | tf_op jit(solution)/shard_map/ppermute | solution.py:27
  452.5 24.9 %slice-start = ((s8[4718592]{0:T(1024)(128)(4,1)}), s8[4194304]{0:T(1024)(128)(4,1)S(1)}, s32[]{:S(2)}) async-start(s8[4718592]{0:T(1024)(128)(4,1)} %bitcast.374), calls=%async_computation.7 | async-start | bytes 8388608
  452.5 24.9 %slice-start.1 = ((s8[4718592]{0:T(1024)(128)(4,1)}), s8[524288]{0:T(1024)(128)(4,1)S(1)}, s32[]{:S(2)}) async-start(s8[4718592]{0:T(1024)(128)(4,1)} %bitcast.374), calls=%async_computation.8 | async-start | bytes 1048576
  458.5 45.8 %collective-permute-start.17 = (s16[256,2688]{1,0:T(8,128)(2,1)S(1)}, s16[256,2688]{1,0:T(8,128)(2,1)S(1)}, u32[]{:S(2)}, u32[]{:S(2)}) collective-permute-start(s16[256,2688]{1,0:T(8,128)(2,1)S(1)} %select_convert_fusion), channel_id=1, source_target_pairs={{0,16},{1,17},{2,18},{3,19},{4,20},{5,21},{6,22},{7,23},{8,24},{9,... | collective-permute-start | bytes 4128776 | tf_op jit(solution)/shard_map/ppermute | solution.py:27
  479.1 4.4 copy-start.10
  479.1 4.4 copy-start.11
  480.0 14.1 %collective-permute-start.23 = (s16[64,2304]{1,0:T(8,128)(2,1)S(1)}, s16[64,2304]{1,0:T(8,128)(2,1)S(1)}, u32[]{:S(2)}, u32[]{:S(2)}) collective-permute-start(s16[64,2304]{1,0:T(8,128)(2,1)S(1)} %get-tuple-element.117), channel_id=1, source_target_pairs={{0,32},{1,33},{2,34},{3,35},{4,36},{5,37},{6,38},{7,39},{8,40},{9,... | collective-permute-start | bytes 884744 | tf_op jit(solution)/shard_map/ppermute | solution.py:27
  480.1 14.2 %collective-permute-start.24 = (s16[64,2304]{1,0:T(8,128)(2,1)S(1)}, s16[64,2304]{1,0:T(8,128)(2,1)S(1)}, u32[]{:S(2)}, u32[]{:S(2)}) collective-permute-start(s16[64,2304]{1,0:T(8,128)(2,1)S(1)} %get-tuple-element.118), channel_id=1, source_target_pairs={{0,96},{1,97},{2,98},{3,99},{4,100},{5,101},{6,102},{7,103},{8,104... | collective-permute-start | bytes 884744 | tf_op jit(solution)/shard_map/ppermute | solution.py:27
  483.6 10.9 %collective-permute-start.25 = (s16[64,2304]{1,0:T(8,128)(2,1)S(1)}, s16[64,2304]{1,0:T(8,128)(2,1)S(1)}, u32[]{:S(2)}, u32[]{:S(2)}) collective-permute-start(s16[64,2304]{1,0:T(8,128)(2,1)S(1)} %get-tuple-element.116), channel_id=1, source_target_pairs={{0,64},{1,65},{2,66},{3,67},{4,68},{5,69},{6,70},{7,71},{8,72},{9,... | collective-permute-start | bytes 884744 | tf_op jit(solution)/shard_map/ppermute | solution.py:27
  506.0 17.3 %collective-permute-start.18 = (s16[64,2688]{1,0:T(8,128)(2,1)S(1)}, s16[64,2688]{1,0:T(8,128)(2,1)S(1)}, u32[]{:S(2)}, u32[]{:S(2)}) collective-permute-start(s16[64,2688]{1,0:T(8,128)(2,1)S(1)} %get-tuple-element.110), channel_id=1, source_target_pairs={{0,32},{1,33},{2,34},{3,35},{4,36},{5,37},{6,38},{7,39},{8,40},{9,... | collective-permute-start | bytes 1032200 | tf_op jit(solution)/shard_map/ppermute | solution.py:27
  506.1 17.4 %collective-permute-start.19 = (s16[64,2688]{1,0:T(8,128)(2,1)S(1)}, s16[64,2688]{1,0:T(8,128)(2,1)S(1)}, u32[]{:S(2)}, u32[]{:S(2)}) collective-permute-start(s16[64,2688]{1,0:T(8,128)(2,1)S(1)} %get-tuple-element.111), channel_id=1, source_target_pairs={{0,96},{1,97},{2,98},{3,99},{4,100},{5,101},{6,102},{7,103},{8,104... | collective-permute-start | bytes 1032200 | tf_op jit(solution)/shard_map/ppermute | solution.py:27
  509.3 14.4 %collective-permute-start.20 = (s16[64,2688]{1,0:T(8,128)(2,1)S(1)}, s16[64,2688]{1,0:T(8,128)(2,1)S(1)}, u32[]{:S(2)}, u32[]{:S(2)}) collective-permute-start(s16[64,2688]{1,0:T(8,128)(2,1)S(1)} %get-tuple-element.109), channel_id=1, source_target_pairs={{0,64},{1,65},{2,66},{3,67},{4,68},{5,69},{6,70},{7,71},{8,72},{9,... | collective-permute-start | bytes 1032200 | tf_op jit(solution)/shard_map/ppermute | solution.py:27
  524.8 2.2 copy-start.8
  524.8 2.2 copy-start.14
  530.7 3.7 collective-permute-start.27
  534.4 5.1 collective-permute-start.28
  535.9 3.6 collective-permute-start.29
  537.7 5.1 collective-permute-start.30
